TPU v7x, 32 devices: a whole 2x2x4 slice. The times are simulated.
32 devices in a mesh: dp: 16 (over z, x, core), mp: 2 (over y).
Axes of the slice: x: 2, y: 2, z: 4, core: 2. Of those that a mesh axis runs over, the one named last changes fastest.
Arguments:
- patches: bfloat16 [32, 1024, 768], P('dp'), may hold values from -6 to 6
- extra_tokens: bfloat16 [32, 2, 768], P('dp'), may hold values from -6 to 6
- visible: int32 [32, 256], P('dp'), may hold values from 0 to 1023, as said below
- qkv_weight: bfloat16 [3, 768, 768], P(None, None, 'mp'), may hold values from -0.21875 to 0.21875
- out_weight: bfloat16 [768, 768], P('mp'), may hold values from -1.75 to 1.75
- out_bias: float32 [768], replicated, may hold values from -3 to 3
- up_weight: bfloat16 [768, 3072], P(None, 'mp'), may hold values from -0.21875 to 0.21875
- up_bias: float32 [3072], P('mp'), may hold values from -3 to 3
- down_weight: bfloat16 [3072, 768], P('mp'), may hold values from -0.109375 to 0.109375
- down_bias: float32 [768], replicated, may hold values from -3 to 3
- first_gain: float32 [768], replicated, may hold values from 0.5 to 1.5
- first_shift: float32 [768], replicated, may hold values from -3 to 3
- second_gain: float32 [768], replicated, may hold values from 0.5 to 1.5
- second_shift: float32 [768], replicated, may hold values from -3 to 3
- cotangent: bfloat16 [32, 258, 768], P('dp'), may hold values from -6 to 6
Outputs:
- output: bfloat16 [32, 258, 768], P('dp')
- input_grad: float32 [32, 258, 768], P('dp')
- qkv_grad: float32 [3, 768, 768], P(None, 'dp', 'mp')
- out_grad: float32 [768, 768], P('mp', 'dp')
- out_bias_grad: float32 [768], replicated
- up_grad: float32 [768, 3072], P('dp', 'mp')
- up_bias_grad: float32 [3072], P('mp')
- down_grad: float32 [3072, 768], P('mp', 'dp')
- down_bias_grad: float32 [768], replicated
- first_gain_grad: float32 [768], replicated
- first_shift_grad: float32 [768], replicated
- second_gain_grad: float32 [768], replicated
- second_shift_grad: float32 [768], replicated
Inputs may be any that keep to these rules, and one draw needn't show every extreme that they name: `visible`: each row names 256 different patches of its image.
All inputs are finite; a program needn't handle non-finite values.
Results may differ from a plain program's by a relative error of at most 0.012.
Values sent between devices are 32-bit elements; how exact they have to be, the bound alone decides.
No kernel may reach another device: no remote copies, remote signals or barrier semaphores. Data moves between devices by JAX's collectives and lax.ppermute only.
A program may use at most 128 MiB of HBM per device.

v0:
```python
from functools import partial

import jax
import jax.numpy as jnp
from jax import lax
from jax.experimental import pallas as pl
from jax.experimental.pallas import tpu as pltpu
from jax.sharding import PartitionSpec as P

HEAD_DIM = 64
PAIR = 2 * HEAD_DIM
F32 = jnp.float32
BF16 = jnp.bfloat16
MIB = 1 << 20
SWAP = ((0, 1), (1, 0))


def mm(a, b):
    return lax.dot_general(a, b, (((1,), (0,)), ((), ())), preferred_element_type=F32)


def mm_nt(a, b):
    return lax.dot_general(a, b, (((1,), (1,)), ((), ())), preferred_element_type=F32)


def mm_tn(a, b):
    return lax.dot_general(a, b, (((0,), (0,)), ((), ())), preferred_element_type=F32)


def normed(values):
    center = values - jnp.mean(values, -1, keepdims=True)
    rate = lax.rsqrt(jnp.mean(center * center, -1, keepdims=True) + 1e-06)
    return center * rate, rate


def norm_back(grad, hat, rate, gain):
    scaled = grad * gain
    return rate * (
        scaled
        - jnp.mean(scaled, -1, keepdims=True)
        - hat * jnp.mean(scaled * hat, -1, keepdims=True)
    )


def shape(dims, dtype=F32):
    return jax.ShapeDtypeStruct(tuple(dims), dtype)


def far(dims, dtype=F32):
    return pltpu.HBM(tuple(dims), dtype)


def whole(x):
    return pl.BlockSpec(x.shape, lambda i: (0,) * len(x.shape))


def one_of(x, image):
    return pl.BlockSpec((None,) + x.shape[1:], lambda i: (image,) + (0,) * (x.ndim - 1))


def scalars():
    return pl.BlockSpec(memory_space=pltpu.SMEM)


ANYWHERE = pl.BlockSpec(memory_space=pl.ANY)


class Chain:
    def __init__(self):
        self.token = jnp.zeros((8, 128), F32)

    def call(self, body, args, specs, outs, vmem, name, grid=1, out_specs=None, scratch=(), deep=()):
        taken, given = len(args), len(outs)
        args = [pltpu.with_memory_space_constraint(a, pltpu.HBM) if i in deep else a for i, a in enumerate(args)]

        def without_tokens(*refs):
            return body(*refs[:taken], *refs[taken + 1 : taken + 1 + given], *refs[taken + 2 + given :])

        *got, self.token = pl.pallas_call(
            without_tokens,
            grid=(grid,),
            out_shape=(*outs, shape((8, 128))),
            in_specs=[*specs, ANYWHERE],
            out_specs=(*(out_specs or [whole(o) for o in outs]), ANYWHERE),
            scratch_shapes=list(scratch),
            compiler_params=pltpu.CompilerParams(vmem_limit_bytes=vmem * MIB),
            cost_estimate=pl.CostEstimate(flops=1 << 31, bytes_accessed=1, transcendentals=0),
            name=name,
        )(*args, self.token)
        return got

    def at_once(self, ids, moves, *values):
        outs = jax.eval_shape(moves, *values)
        moved = lambda token, *vs: (token, *moves(*vs))
        never = lambda token, *vs: (token, *(jnp.zeros(o.shape, o.dtype) for o in outs))
        self.token, *got = lax.cond(ids[0] >= 0, moved, never, self.token, *values)
        return got


def line(vector):
    return vector[...].reshape(1, -1)


def side_masks():
    lane = lax.broadcasted_iota(jnp.int32, (1, PAIR), 1)
    low = jnp.where(lane < HEAD_DIM, 1.0, 0.0)
    return low.astype(BF16), (1.0 - low).astype(BF16)


def attend_body(images, pick, patch, extra, weight, gain, shift, *refs):
    seq_out, first_out, qkv_out, log_out, *mixed_outs = refs
    rows, width = seq_out.shape
    inner = mixed_outs[0].shape[1]
    image = pl.program_id(0)
    extras, picks = extra.shape[1], pick.shape[1]
    spread = jnp.broadcast_to(pick[pl.ds(image, 1), :].astype(F32), (128, picks))
    column = spread.T[:, 0:1].astype(jnp.int32)
    hot = lax.broadcasted_iota(jnp.int32, (picks, patch.shape[0]), 1) == column
    seq_out[extras:, :] = mm(jnp.where(hot, 1.0, 0.0).astype(BF16), patch[...])
    seq_out[0:extras, :] = extra[image].astype(F32)
    hat, _ = normed(seq_out[...])
    first = (hat * line(gain) + line(shift)).astype(BF16)
    first_out[...] = first
    for j in range(3):
        qkv_out[:, j * inner : (j + 1) * inner] = mm(first, weight[j]).astype(BF16)
    masks = side_masks()
    lane = lax.broadcasted_iota(jnp.int32, (rows, PAIR), 1)
    logs = jnp.zeros((rows, PAIR), F32)
    for pair in range(inner // PAIR):
        q = qkv_out[:, pair * PAIR : (pair + 1) * PAIR]
        k = qkv_out[:, inner + pair * PAIR : inner + (pair + 1) * PAIR]
        v = qkv_out[:, 2 * inner + pair * PAIR : 2 * inner + (pair + 1) * PAIR]
        sides = []
        for side in range(2):
            scores = mm_nt(q * masks[side], k) * (HEAD_DIM**-0.5)
            top = jnp.max(scores, -1, keepdims=True)
            expo = jnp.exp(scores - top)
            total = jnp.sum(expo, -1, keepdims=True)
            sides.append(mm((expo / total).astype(BF16), v))
            logs = jnp.where(lane == 2 * pair + side, top + jnp.log(total), logs)
        mixed = jnp.where(lane < HEAD_DIM, sides[0], sides[1]).astype(BF16).astype(F32)
        for b, out in enumerate(mixed_outs):
            @pl.when(image == b)
            def _(out=out, mixed=mixed, pair=pair):
                out[:, pair * PAIR : (pair + 1) * PAIR] = mixed
    log_out[...] = logs


def join_body(ids, mine, near, far, full_out):
    half = mine.shape[0]
    part = near.shape[0]
    mp = ids[4]
    core = ids[0]
    own = pl.multiple_of(mp * half, part)
    other = pl.multiple_of((1 - mp) * half, part)
    full_out[pl.ds(own, half), :] = mine[...]
    full_out[pl.ds(pl.multiple_of(other + core * part, part), part), :] = near[...].astype(BF16)
    full_out[pl.ds(pl.multiple_of(other + (1 - core) * part, part), part), :] = far[...].astype(BF16)


def forward_body(
    ids, seq, dy, out_bias, gain, shift, up_bias, mine, other, full, up, down,
    middle_out, second_out, hidden_out, upper_out, norm_out, small_out,
):
    rows, width = seq.shape
    inner = mine.shape[1]
    first_half = ids[4] == 0
    left = jnp.where(first_half, mine[...], other[...]).astype(BF16)
    right = jnp.where(first_half, other[...], mine[...]).astype(BF16)
    attn = mm(left, full[0:inner, :]) + mm(right, full[inner:, :]) + line(out_bias)
    middle = seq[...] + attn
    middle_out[...] = middle
    hat, _ = normed(middle)
    second = (hat * line(gain) + line(shift)).astype(BF16)
    second_out[...] = second
    grad = dy[...].astype(BF16)
    small_out[...] = jnp.zeros_like(small_out)
    chunk = 512
    biases = line(up_bias)
    norm = jnp.zeros((rows, width), F32)
    for start in range(0, up.shape[1], chunk):
        cols = slice(start, start + chunk)
        upper = mm(second, up[:, cols]) + biases[:, cols]
        phi = 0.5 + 0.5 * lax.erf(upper * (0.5**0.5))
        hidden_out[:, cols] = (upper * phi).astype(BF16)
        slope = phi + upper * (jnp.exp(-0.5 * upper * upper) * 0.3989422804014327)
        back = (mm_nt(grad, down[cols, :]) * slope).astype(BF16)
        upper_out[:, cols] = back
        total = jnp.sum(back.astype(F32), 0, keepdims=True)
        for at in range(start, start + chunk, 256):
            row, place = divmod(at, width)
            small_out[row : row + 1, place : place + 256] = total[:, at - start : at - start + 256]
        norm = norm + mm_nt(back, up[:, cols])
    norm_out[...] = norm
    small_out[4:5, :] = jnp.sum(grad.astype(F32), 0, keepdims=True)


def backward_body(mine, other, middle, qkv, logs, seq, dy, gain, out_weight, weight, *refs):
    (*before, grad_out, attn_out, back, part_out, small_out, cross_out) = refs
    before = before[0] if before else None
    rows, width = middle.shape
    inner = out_weight.shape[0]
    hat, rate = normed(middle[...])
    total = mine[...] + other[...]
    grad = dy[...].astype(F32) + norm_back(total, hat, rate, line(gain))
    grad_out[...] = grad
    attn = grad.astype(BF16)
    attn_out[...] = attn
    small_out[...] = jnp.zeros_like(small_out)
    small_out[2:3, :] = jnp.sum(total * hat, 0, keepdims=True)
    small_out[3:4, :] = jnp.sum(total, 0, keepdims=True)
    small_out[5:6, :] = jnp.sum(attn.astype(F32), 0, keepdims=True)
    mixed = mm_nt(attn, out_weight[...]).astype(BF16)
    masks = side_masks()
    lane = lax.broadcasted_iota(jnp.int32, (rows, PAIR), 1)
    scale = HEAD_DIM**-0.5
    for pair in range(inner // PAIR):
        cols = slice(pair * PAIR, (pair + 1) * PAIR)
        q = qkv[:, cols]
        k = qkv[:, inner + pair * PAIR : inner + (pair + 1) * PAIR]
        v = qkv[:, 2 * inner + pair * PAIR : 2 * inner + (pair + 1) * PAIR]
        dm = mixed[:, cols]
        q_t = q.astype(F32).T.astype(BF16)
        dm_t = dm.astype(F32).T.astype(BF16)
        dq, dk, dv = [], [], []
        for side in range(2):
            half = slice(side * HEAD_DIM, (side + 1) * HEAD_DIM)
            head = 2 * pair + side
            scores = mm_nt(q * masks[side], k) * scale
            probs = jnp.exp(scores - logs[:, head : head + 1])
            dv.append(mm(dm_t[half, :], probs.astype(BF16)))
            prob_grad = mm_nt(dm * masks[side], v)
            score = probs * (prob_grad - jnp.sum(prob_grad * probs, -1, keepdims=True))
            score = score.astype(BF16)
            dq.append(mm(score, k))
            dk.append(mm(q_t[half, :], score))
        parts = (
            jnp.where(lane < HEAD_DIM, dq[0], dq[1]) * scale,
            (jnp.concatenate(dk, 0) * scale).T,
            jnp.concatenate(dv, 0).T,
        )
        for j, value in enumerate(parts):
            start = j * inner + pair * PAIR
            back[:, start : start + PAIR] = value.astype(BF16)
    part = mm_nt(back[:, 0:inner], weight[0])
    for j in range(1, 3):
        part = part + mm_nt(back[:, j * inner : (j + 1) * inner], weight[j])
    part_out[...] = part
    first_hat, _ = normed(seq[...])
    cross_out[...] = jnp.zeros_like(cross_out) if before is None else before[...]
    cross_out[6:7, 0:width] += jnp.sum(part * first_hat, 0, keepdims=True)
    cross_out[7:8, 0:width] += jnp.sum(part, 0, keepdims=True)


def branch_body(*refs):
    (*hiddens, down, part_out) = refs
    rows, size = hiddens[0].shape[0], part_out.shape[0] // len(hiddens)
    for image, hidden in enumerate(hiddens):
        part_out[(image + 1) * size - 8 : (image + 1) * size, :] = jnp.zeros((8, part_out.shape[1]), F32)
        part_out[image * size : image * size + rows, :] = mm(hidden[...], down[...])


def output_body(images, down_mine, down_other, bias, *refs):
    middles, out = refs[:images], refs[images]
    rows, size = middles[0].shape[0], down_mine.shape[0] // images
    for image in range(images):
        own = slice(image * size, image * size + rows)
        branch = down_mine[own, :] + down_other[own, :] + line(bias)
        out[image] = (middles[image][...] + branch).astype(BF16)


def input_body(gain, seq, mine, other, grad, out):
    hat, rate = normed(seq[...])
    out[...] = grad[...] + norm_back(mine[...] + other[...], hat, rate, line(gain))


def grads_body(layout, order, chunk, smalls, ids, *refs):
    lefts, rights, at = [], [], 0
    for images, _ in layout:
        lefts.append(refs[at : at + images])
        rights.append(refs[at + images : at + 2 * images])
        at += 2 * images
    small_refs = refs[at : at + smalls]
    keep, send, turned, stacked, tail = refs[at + smalls :]
    width = lefts[0][0].shape[1]
    size, half = width // 16, width // 2
    main = lefts[0][0].shape[0] // 8 * 8
    spare = lefts[0][0].shape[0] - main
    step = pl.program_id(0)
    even = ids[0] == 0

    def turn(value, start):
        columns = value.astype(F32).T
        stop = start + value.shape[0]
        for place in range(8):
            source = 0
            for digit, bit in enumerate(order):
                source |= ((place >> (2 - digit)) & 1) << bit
            zero = columns[source * size : (source + 1) * size, :]
            one = columns[(source + 1) * size : (source + 2) * size, :]
            rows = slice(place * size, (place + 1) * size)
            turned[rows, start:stop] = jnp.where(even, zero, one).astype(BF16)
            rows = slice(half + place * size, half + (place + 1) * size)
            turned[rows, start:stop] = jnp.where(even, one, zero).astype(BF16)

    begin = 0
    for (images, steps), left, right in zip(layout, lefts, rights):
        @pl.when(step == begin)
        def _(left=left, images=images):
            tail[...] = jnp.zeros_like(tail)
            for i, ref in enumerate(left):
                turn(ref[0:main, :], i * main)
                tail[i * spare : (i + 1) * spare, 0:width] = ref[main:, :].astype(F32)
            turn(tail[:, 0:width], images * main)

        @pl.when((step >= begin) & (step < begin + steps))
        def _(right=right, images=images):
            tail[...] = jnp.zeros_like(tail)
            for i, ref in enumerate(right):
                stacked[i * main : (i + 1) * main, :] = ref[0:main, :].astype(BF16)
                tail[i * spare : (i + 1) * spare, 0:chunk] = ref[main:, :].astype(F32)
            stacked[images * main :, :] = tail[:, 0:chunk].astype(BF16)

        begin += steps
    total = mm(turned[...], stacked[...])
    keep[0:half, :] = total[0:half, :]
    send[0:half, :] = total[half:, :]
    if smalls:
        keep[half:, :] = jnp.zeros_like(keep[half:, :])
        send[half:, :] = jnp.zeros_like(send[half:, :])
        for place in range(width // chunk):
            @pl.when(step == place)
            def _(place=place):
                cols = slice(place * chunk, (place + 1) * chunk)
                small = small_refs[0][:, cols]
                for ref in small_refs[1:]:
                    small = small + ref[:, cols]
                keep[half:, :] = small
                send[half:, :] = small


def fold_body(size, bit, ids, kept, got, *refs):
    *cross, keep, send = refs
    own = pl.ds(pl.multiple_of(ids[bit] * size, 8), size)
    away = pl.ds(pl.multiple_of((1 - ids[bit]) * size, 8), size)
    send[0:size, :] = kept[away, :] + got[away, :]
    keep[0:size, :] = kept[own, :] + got[own, :]
    if keep.shape[0] > size:
        small = kept[2 * size :, :] + got[2 * size :, :]
        if cross:
            small = small + (cross[0][...] + cross[1][...])
        send[size:, :] = small
        keep[size:, :] = small


def last_body(size, kept, got, out, *small):
    out[...] = kept[0:size, :] + got[0:size, :]
    for ref in small:
        ref[...] = kept[size:, :] + got[size:, :]


class WeightSum:
    def __init__(self, chain, ids, dp, name, order, chunk):
        self.chain, self.ids, self.dp, self.name, self.order, self.chunk = chain, ids, dp, name, order, chunk
        self.plain = not folded(dp)

    def start(self, sets, small=()):
        width = sets[0][0][0].shape[1]
        self.columns = columns = sum(rights[0].shape[1] for _, rights in sets)
        self.size = width // self.dp
        self.extra = 8 if small else 0
        if self.plain:
            products = [
                sum(mm_tn(left, right.astype(BF16)) for left, right in zip(*pair)) for pair in sets
            ]
            self.full = jnp.concatenate(products, 1)
            self.part = sum(small)
            return
        chunk, args, specs, layout, begin = self.chunk, [], [], [], 0
        for lefts, rights in sets:
            steps = rights[0].shape[1] // chunk
            args += [*lefts, *rights]
            specs += [whole(v) for v in lefts]
            for v in rights:
                block = lambda j, begin=begin, steps=steps: (0, jnp.clip(j - begin, 0, steps - 1))
                specs.append(pl.BlockSpec((v.shape[0], chunk), block))
            layout.append((len(lefts), steps))
            begin += steps
        images, rows = len(sets[0][0]), sets[0][0][0].shape[0]
        spare = 8 * pl.cdiv(images * (rows % 8), 8)
        depth = images * (rows // 8 * 8) + spare
        self.rows = width // 2
        dims = (self.rows + self.extra, columns)
        block = pl.BlockSpec((self.rows + self.extra, chunk), lambda j: (0, j))
        self.keep, send = self.chain.call(
            partial(grads_body, layout, self.order, chunk, len(small)), [self.ids, *args, *small],
            [scalars(), *specs] + [whole(v) for v in small], [far(dims), far(dims)], 32,
            f"{self.name}_grads", grid=begin, out_specs=[block, block],
            scratch=[
                pltpu.VMEM((width, depth), BF16),
                pltpu.VMEM((depth, chunk), BF16),
                pltpu.VMEM((spare, max(width, chunk)), F32),
            ],
            deep=range(1, 1 + len(args)),
        )
        (self.got,) = self.chain.at_once(
            self.ids, lambda v: (lax.ppermute(v, "dp", flips(self.dp, 0)),), send
        )
        self.at = 0

    def fold(self, *cross):
        if self.plain:
            return
        bit = self.order[self.at]
        self.at += 1
        self.rows //= 2
        args = [self.ids, self.keep, self.got, *cross]
        out = shape((self.rows + self.extra, self.columns))
        if self.at == 1:
            block = lambda v: pl.BlockSpec((v.shape[0], 512), lambda j: (0, j))
            specs = [block(v) for v in args[1:]]
            more = dict(grid=self.columns // 512, out_specs=[block(out)] * 2, deep=range(1, len(args)))
        else:
            specs, more = [whole(v) for v in args[1:]], {}
        self.keep, send = self.chain.call(
            partial(fold_body, self.rows, bit), args, [scalars(), *specs],
            [far(out.shape), out] if self.at == 1 else [out, out], 16, f"{self.name}_fold{bit}", **more,
        )
        self.got = lax.ppermute(send, "dp", flips(self.dp, bit))

    def finish(self):
        if self.plain:
            return lax.psum_scatter(self.full, "dp", scatter_dimension=0, tiled=True)
        outs = [shape((self.size, self.columns))]
        if self.extra:
            outs.append(shape((self.extra, self.columns)))
        got = self.chain.call(
            partial(last_body, self.size), [self.keep, self.got],
            [whole(self.keep), whole(self.got)], outs, 16, f"{self.name}_last",
        )
        if self.extra:
            self.small = got[1]
        return got[0]


def folded(dp):
    return dp == 16


def flips(dp, bit):
    return [(i, i ^ (1 << bit)) for i in range(dp)]


def per_device(
    dp,
    patches,
    extra_tokens,
    visible,
    qkv_weight,
    out_weight,
    out_bias,
    up_weight,
    up_bias,
    down_weight,
    down_bias,
    first_gain,
    first_shift,
    second_gain,
    second_shift,
    cotangent,
):
    images, _, width = patches.shape
    rows = visible.shape[1] + extra_tokens.shape[1]
    inner = qkv_weight.shape[2]
    hidden_width = up_weight.shape[1]
    place = lax.axis_index("dp")
    core = place % 2
    ids = jnp.stack([core] + [(place >> bit) & 1 for bit in (1, 2, 3)] + [lax.axis_index("mp")])
    ids = lax.optimization_barrier(ids.astype(jnp.int32))
    across = lambda v: lax.ppermute(v, "mp", SWAP)

    core_swap = lambda v: (lax.ppermute(v, "dp", flips(dp, 0)),)
    chain = Chain()

    quarter = inner // 2
    piece = lax.dynamic_slice_in_dim(out_weight, core * quarter, quarter, 0).astype(F32)
    near = across(piece)

    every = range(images)
    args = [visible, patches, extra_tokens, qkv_weight, first_gain, first_shift]
    each = lambda dims: pl.BlockSpec((None, *dims[1:]), lambda j: (j,) + (0,) * (len(dims) - 1))
    stacks = [
        far((images, rows, width)), far((images, rows, width), BF16), far((images, rows, 3 * inner), BF16),
        far((images, rows, PAIR)),
    ]
    flat = [shape((rows, inner))] * images
    seqs, firsts, qkvs, logs, *mixeds = chain.call(
        partial(attend_body, images), args,
        [whole(visible), each(patches.shape)] + [whole(a) for a in args[2:]],
        stacks + flat, 40, "attend", grid=images,
        out_specs=[each(o.shape) for o in stacks] + [whole(o) for o in flat], deep=range(6),
    )
    mixed_others = [across(m) for m in mixeds]
    (distant,) = chain.at_once(ids, core_swap, near)
    (full,) = chain.call(
        join_body, [ids, out_weight, near, distant],
        [scalars(), whole(out_weight), whole(near), whole(distant)],
        [shape((2 * inner, width), BF16)], 16, "join",
    )

    middles, seconds, hiddens, uppers, norms, smalls, norm_others = [], [], [], [], [], [], []
    for b in every:
        args = [ids, seqs, cotangent, out_bias, second_gain, second_shift, up_bias,
                mixeds[b], mixed_others[b], full, up_weight, down_weight]
        got = chain.call(
            forward_body, args,
            [scalars(), one_of(seqs, b), one_of(cotangent, b)] + [whole(a) for a in args[3:]],
            [far((rows, width)), far((rows, width), BF16), far((rows, hidden_width), BF16),
             far((rows, hidden_width), BF16), shape((rows, width)), far((8, width))],
            44, f"forward{b}", deep=(1, 3, 4, 5, 6),
        )
        for kept, one in zip((middles, seconds, hiddens, uppers, norms, smalls), got):
            kept.append(one)
        norm_others.append(across(norms[b]))

    down_sum, up_sum, last_sum = (
        WeightSum(chain, ids, dp, *how)
        for how in (("down", (1, 2, 3), 512), ("up", (2, 3, 1), 512), ("last", (1, 2, 3), 384))
    )
    down_sum.start([([cotangent[b] for b in every], hiddens)])
    down_sum.fold()

    grads, attns, backs, firsts_part, crosses, part_others = [], [], [], [], [], []
    for b in every:
        args = [norms[b], norm_others[b], middles[b], qkvs, logs, seqs, cotangent, second_gain,
                out_weight, qkv_weight, *crosses[-1:]]
        specs = [whole(a) for a in args]
        for i in (3, 4, 5, 6):
            specs[i] = one_of(args[i], b)
        got = chain.call(
            backward_body, args, specs,
            [far((rows, width)), far((rows, width), BF16), far((rows, 3 * inner), BF16),
             shape((rows, width)), far((8, width)), shape((8, hidden_width))],
            44, f"backward{b}", deep=(2, 3, 4, 5, 7),
        )
        for kept, one in zip((grads, attns, backs, firsts_part, smalls, crosses), got):
            kept.append(one)
        if b < images - 1:
            part_others.append(across(firsts_part[b]))
        if b == 0:
            up_sum.start([(seconds, uppers)])
            up_sum.fold()
    last_sum.start(
        [(attns, mixeds), ([firsts[b] for b in every], backs)], [*smalls, crosses[-1][:, :width]]
    )
    down_sum.fold()
    pairs = [((d, m), (d ^ 1, m ^ 1)) for d in range(dp) for m in range(2)]
    corners = [(2 * p[0] + p[1], 2 * q[0] + q[1]) for p, q in pairs]
    cross = chain.at_once(
        ids, lambda v: (across(v), lax.ppermute(v, ("dp", "mp"), corners)), crosses[-1]
    )
    firsts_part[-1], chain.token = lax.optimization_barrier((firsts_part[-1], chain.token))
    part_others.append(across(firsts_part[-1]))

    def input_of(b):
        args = [first_gain, seqs, firsts_part[b], part_others[b], grads[b]]
        specs = [whole(a) for a in args]
        specs[1] = one_of(seqs, b)
        return chain.call(
            input_body, args, specs, [shape((rows, width))], 32, f"input{b}", deep=(0, 1, 4)
        )[0]

    input_grads = [input_of(b) for b in range(images - 1)]
    last_sum.fold(*cross)
    up_sum.fold()
    padded = images * 8 * pl.cdiv(rows, 8)
    (down_part,) = chain.call(
        branch_body, [*hiddens, down_weight], [whole(a) for a in (*hiddens, down_weight)],
        [shape((padded, width))], 32, "branch",
    )
    down_other = across(down_part)
    down_sum.fold()
    input_grads.append(input_of(images - 1))
    down_total = down_sum.finish()
    last_sum.fold()
    up_sum.fold()
    last_sum.fold()
    up_total = up_sum.finish()
    args = [down_part, down_other, down_bias, *middles]
    (output,) = chain.call(
        partial(output_body, images), args, [whole(a) for a in args],
        [shape((images, rows, width), BF16)], 32, "output", deep=(2,),
    )
    last_total = last_sum.finish()
    if last_sum.plain:
        last_sum.small = lax.psum(last_sum.part + across(crosses[-1][:, :width]), "dp")
    small = last_sum.small[:, :width]
    return (
        output,
        jnp.stack(input_grads),
        last_total[:, inner:].reshape(-1, 3, inner).transpose(1, 0, 2),
        last_total[:, :inner].T,
        small[5],
        up_total,
        small[0:2].reshape(-1),
        down_total.T,
        small[4],
        small[6],
        small[7],
        small[2],
        small[3],
    )


def solution(mesh):
    return jax.shard_map(
        partial(per_device, mesh.shape["dp"]),
        mesh=mesh,
        in_specs=(
            P("dp", None, None),
            P("dp", None, None),
            P("dp", None),
            P(None, None, "mp"),
            P("mp", None),
            P(),
            P(None, "mp"),
            P("mp"),
            P("mp", None),
            P(),
            P(),
            P(),
            P(),
            P(),
            P("dp", None, None),
        ),
        out_specs=(
            P("dp", None, None),
            P("dp", None, None),
            P(None, "dp", "mp"),
            P("mp", "dp"),
            P(),
            P("dp", "mp"),
            P("mp"),
            P("mp", "dp"),
            P(),
            P(),
            P(),
            P(),
            P(),
        ),
        check_vma=False,
    )
```

profile of v0, /device:TPU:0, one launch (start us, length us, event | category | flops | bytes accessed | tf_op | source)
XLA Modules:
  0.0 213.7 jit_solution(16263519671026203799)
XLA Ops:
  0.7 1.0 dynamic-slice_convert_fusion
  1.7 3.0 %collective-permute-start.7 = (f32[192,768]{1,0:T(8,128)S(1)}, f32[192,768]{1,0:T(8,128)}, u32[]{:S(2)}, u32[]{:S(2)}) collective-permute-start(f32[192,768]{1,0:T(8,128)S(1)} %dynamic-slice_convert_fusion), channel_id=1, source_target_pairs={{0,1},{1,0},{2,3},{3,2},{4,5},{5,4},{6,7},{7,6},{8,9},{9,8},{10,11... | collective-permute-start | bytes 1769480 | tf_op jit(solution)/shard_map/ppermute | solution.py:480
  4.7 13.0 %attend.1 = (f32[2,258,768]{2,1,0:T(8,128)}, bf16[2,258,768]{2,1,0:T(8,128)(2,1)}, bf16[2,258,1152]{2,1,0:T(8,128)(2,1)}, f32[2,258,128]{2,1,0:T(8,128)}, f32[25...) custom-call(s32[2,256]{1,0:T(2,128)} %refs_0_.3, bf16[2,1024,768]{2,1,0:T(8,128)(2,1)} %refs_1_.2, ...), custom_call_target="tpu_custom_call" | custom-call | flops 2147483648 | bytes 1 | tf_op jit(solution)/shard_map/attend/pallas_call | solution.py:79
  17.8 2.0 collective-permute-start.8
  20.1 2.4 %conditional.5 = (f32[192,768]{1,0:T(8,128)}) conditional(s32[]{:T(128)} %bitcast.5, () %tuple.41, f32[192,768]{1,0:T(8,128)} %collective-permute-done.7.refs_2_), branch_computations={%region_0.1_spmd, %region_1.2_spmd} | conditional | bytes 2359344 | solution.py:96
  20.2 2.3 %collective-permute-done = f32[192,768]{1,0:T(8,128)} collective-permute-done((f32[192,768]{1,0:T(8,128)}, f32[192,768]{1,0:T(8,128)}, u32[]{:S(2)}, u32[]{:S(2)}) %collective-permute-start) | collective-permute-done | bytes 589856 | tf_op jit(solution)/shard_map/cond/branch_1_fun/ppermute | solution.py:482
  22.5 1.1 copy-done.4
  23.6 1.5 join.1
  25.1 5.3 %collective-permute-done.6.refs_8_ = f32[258,384]{1,0:T(8,128)} collective-permute-done((f32[258,384]{1,0:T(8,128)}, f32[258,384]{1,0:T(8,128)}, u32[]{:S(2)}, u32[]{:S(2)}) %collective-permute-start.6) | collective-permute-done | bytes 396320 | tf_op jit(solution)/shard_map/ppermute | solution.py:480
  30.4 6.2 %forward0.1 = (f32[258,768]{1,0:T(8,128)}, bf16[258,768]{1,0:T(8,128)(2,1)}, bf16[258,1536]{1,0:T(8,128)(2,1)}, bf16[258,1536]{1,0:T(8,128)(2,1)}, f32[258,768]{...) custom-call(s32[5]{0:T(128)S(1)} %stack.32.refs_0_, f32[2,258,768]{2,1,0:T(8,128)} %get-tuple-element.121.refs_1_.refs_5_, ...), custom_call_target="tpu_custom_call" | custom-call | flops 2147483648 | bytes 1 | tf_op jit(solution)/shard_map/forward0/pallas_call | solution.py:79
  38.5 6.2 %forward1.1 = (f32[258,768]{1,0:T(8,128)}, bf16[258,768]{1,0:T(8,128)(2,1)}, bf16[258,1536]{1,0:T(8,128)(2,1)}, bf16[258,1536]{1,0:T(8,128)(2,1)}, f32[258,768]{...) custom-call(s32[5]{0:T(128)S(1)} %stack.32.refs_0_, f32[2,258,768]{2,1,0:T(8,128)} %get-tuple-element.121.refs_1_.refs_5_, ...), custom_call_target="tpu_custom_call" | custom-call | flops 2147483648 | bytes 1 | tf_op jit(solution)/shard_map/forward1/pallas_call | solution.py:79
  44.6 1.2 collective-permute-start.11
  45.8 5.9 %down_grads.1 = (f32[384,1536]{1,0:T(8,128)}, f32[384,1536]{1,0:T(8,128)}, f32[8,128]{1,0:T(8,128)S(1)}) custom-call(s32[5]{0:T(128)S(1)} %stack.32.refs_0_, bf16[258,768]{1,0:T(8,128)(2,1)} %get-tuple-element.247.refs_1_, bf16[258,768]{1,0:T(8,128)(2,1)} %get-tuple-element.246.refs_2_, bf16[258,1536]{1,0:T(8,128)(2,1)} %get-tuple-element.126.refs_3_.refs_0_, ...), custom_call_target="tpu_custom_call" | custom-call | flops 2147483648 | bytes 1 | tf_op jit(solution)/shard_map/down_grads/pallas_call | solution.py:79
  51.7 4.9 %conditional.6 = (f32[384,1536]{1,0:T(8,128)}) conditional(s32[]{:T(128)} %bitcast.5, () %tuple.42, f32[384,1536]{1,0:T(8,128)} %get-tuple-element.140), branch_computations={%region_2.3_spmd, %region_3.4_spmd} | conditional | bytes 9437232 | solution.py:96
  51.7 4.9 %collective-permute-done.1 = f32[384,1536]{1,0:T(8,128)} collective-permute-done((f32[384,1536]{1,0:T(8,128)}, f32[384,1536]{1,0:T(8,128)}, u32[]{:S(2)}, u32[]{:S(2)}) %collective-permute-start.1) | collective-permute-done | bytes 2359328 | tf_op jit(solution)/shard_map/cond/branch_1_fun/ppermute | solution.py:407
  56.6 4.7 %down_fold1.1 = (f32[192,1536]{1,0:T(8,128)}, f32[192,1536]{1,0:T(8,128)}, f32[8,128]{1,0:T(8,128)S(1)}) custom-call(s32[5]{0:T(128)S(1)} %stack.32.refs_0_, f32[384,1536]{1,0:T(8,128)} %get-tuple-element.139.refs_1_, f32[384,1536]{1,0:T(8,128)} %get-tuple-element.253.refs_2_, f32[8,128]{1,0:T(8,128)S(1)} %get-tuple-element.141.refs_3_), custom_call_target="tpu_custom_call" | custom-call | flops 2147483648 | bytes 1 | tf_op jit(solution)/shard_map/down_fold1/pallas_call | solution.py:79
  61.3 1.5 collective-permute-start.13
  62.7 9.0 %backward0.1 = (f32[258,768]{1,0:T(8,128)}, bf16[258,768]{1,0:T(8,128)(2,1)}, bf16[258,1152]{1,0:T(8,128)(2,1)}, f32[258,768]{1,0:T(8,128)}, f32[8,768]{1,0:T(8,...) custom-call(f32[258,768]{1,0:T(8,128)} %get-tuple-element.134.refs_0_, f32[258,768]{1,0:T(8,128)} %collective-permute-done.9.refs_1_, ...), custom_call_target="tpu_custom_call" | custom-call | flops 2147483648 | bytes 1 | tf_op jit(solution)/shard_map/backward0/pallas_call | solution.py:79
  72.7 6.0 %up_grads.1 = (f32[384,1536]{1,0:T(8,128)}, f32[384,1536]{1,0:T(8,128)}, f32[8,128]{1,0:T(8,128)S(1)}) custom-call(s32[5]{0:T(128)S(1)} %stack.32.refs_0_, bf16[258,768]{1,0:T(8,128)(2,1)} %get-tuple-element.130.refs_1_, bf16[258,768]{1,0:T(8,128)(2,1)} %get-tuple-element.131.refs_2_, bf16[258,1536]{1,0:T(8,128)(2,1)} %get-tuple-element.132.refs_3_, ...), custom_call_target="tpu_custom_call" | custom-call | flops 2147483648 | bytes 1 | tf_op jit(solution)/shard_map/up_grads/pallas_call | solution.py:79
  78.7 4.9 %conditional.7 = (f32[384,1536]{1,0:T(8,128)}) conditional(s32[]{:T(128)} %bitcast.5, () %tuple.43, f32[384,1536]{1,0:T(8,128)} %get-tuple-element.145), branch_computations={%region_4.5_spmd, %region_5.6_spmd} | conditional | bytes 9437232 | solution.py:96
  78.7 4.9 %collective-permute-done.2 = f32[384,1536]{1,0:T(8,128)} collective-permute-done((f32[384,1536]{1,0:T(8,128)}, f32[384,1536]{1,0:T(8,128)}, u32[]{:S(2)}, u32[]{:S(2)}) %collective-permute-start.2) | collective-permute-done | bytes 2359328 | tf_op jit(solution)/shard_map/cond/branch_1_fun/ppermute | solution.py:407
  83.5 4.8 %up_fold2.1 = (f32[192,1536]{1,0:T(8,128)}, f32[192,1536]{1,0:T(8,128)}, f32[8,128]{1,0:T(8,128)S(1)}) custom-call(s32[5]{0:T(128)S(1)} %stack.32.refs_0_, f32[384,1536]{1,0:T(8,128)} %get-tuple-element.144.refs_1_, f32[384,1536]{1,0:T(8,128)} %get-tuple-element.254.refs_2_, f32[8,128]{1,0:T(8,128)S(1)} %get-tuple-element.146.refs_3_), custom_call_target="tpu_custom_call" | custom-call | flops 2147483648 | bytes 1 | tf_op jit(solution)/shard_map/up_fold2/pallas_call | solution.py:79
  88.3 1.6 collective-permute-start.10
  90.9 8.6 %backward1.1 = (f32[258,768]{1,0:T(8,128)}, bf16[258,768]{1,0:T(8,128)(2,1)}, bf16[258,1152]{1,0:T(8,128)(2,1)}, f32[258,768]{1,0:T(8,128)S(1)}, f32[8,768]{1,0:...) custom-call(f32[258,768]{1,0:T(8,128)} %get-tuple-element.150.refs_0_, ...), custom_call_target="tpu_custom_call" | custom-call | flops 2147483648 | bytes 1 | tf_op jit(solution)/shard_map/backward1/pallas_call | solution.py:79
  100.5 5.2 %conditional.9 = (f32[8,1536]{1,0:T(8,128)}, f32[8,1536]{1,0:T(8,128)}) conditional(s32[]{:T(128)} %bitcast.5, () %tuple.45, f32[8,1536]{1,0:T(8,128)S(1)} %get-tuple-element.162), branch_computations={%region_8.9_spmd, %region_9.10_spmd} | conditional | bytes 393312 | solution.py:96
  100.5 1.2 collective-permute-start.4
  101.7 3.0 %collective-permute-done.4 = f32[8,1536]{1,0:T(8,128)} collective-permute-done((f32[8,1536]{1,0:T(8,128)S(1)}, f32[8,1536]{1,0:T(8,128)}, u32[]{:S(2)}, u32[]{:S(2)}) %collective-permute-start.4) | collective-permute-done | bytes 49184 | tf_op jit(solution)/shard_map/cond/branch_1_fun/ppermute | solution.py:480
  104.7 1.1 collective-permute-done.5
  106.5 7.5 %last_grads.1 = (f32[392,1536]{1,0:T(8,128)}, f32[392,1536]{1,0:T(8,128)}, f32[8,128]{1,0:T(8,128)S(1)}) custom-call(s32[5]{0:T(128)S(1)} %stack.32.refs_0_, bf16[258,768]{1,0:T(8,128)(2,1)} %get-tuple-element.149.refs_1_, bf16[258,768]{1,0:T(8,128)(2,1)} %get-tuple-element.154.refs_2_, f32[258,384]{1,0:T(8,128)} %get-tuple-element.122.refs_7_.refs_3_, ...), custom_call_target="tpu_custom_call" | custom-call | flops 2147483648 | bytes 1 | tf_op jit(solution)/shard_map/last_grads/pallas_call | solution.py:79
  114.0 5.0 %conditional.8 = (f32[392,1536]{1,0:T(8,128)}) conditional(s32[]{:T(128)} %bitcast.5, () %tuple.44, f32[392,1536]{1,0:T(8,128)} %get-tuple-element.165), branch_computations={%region_6.7_spmd, %region_7.8_spmd} | conditional | bytes 9633840 | solution.py:96
  114.1 4.8 %collective-permute-done.3 = f32[392,1536]{1,0:T(8,128)} collective-permute-done((f32[392,1536]{1,0:T(8,128)}, f32[392,1536]{1,0:T(8,128)}, u32[]{:S(2)}, u32[]{:S(2)}) %collective-permute-start.3) | collective-permute-done | bytes 2408480 | tf_op jit(solution)/shard_map/cond/branch_1_fun/ppermute | solution.py:407
  119.0 1.3 copy-done.18
  120.2 1.4 down_fold2.1
  122.2 2.4 %input0.1 = (f32[258,768]{1,0:T(8,128)S(1)}, f32[8,128]{1,0:T(8,128)S(1)}) custom-call(f32[768]{0:T(1024)} %refs_0_.5, f32[2,258,768]{2,1,0:T(8,128)} %get-tuple-element.121.refs_1_.refs_5_, f32[258,768]{1,0:T(8,128)} %get-tuple-element.168.refs_2_, f32[258,768]{1,0:T(8,128)} %collective-permute-done.12.refs_3_, f32[258,768]{1,0:T(8,128)} %get-tuple-element.169.refs_4_, ...), custom_call_target="tpu_custom_call" | custom-call | flops 2147483648 | bytes 1 | tf_op jit(solution)/shard_map/input0/pallas_call | solution.py:79
  124.6 4.3 %last_fold1.1 = (f32[200,1536]{1,0:T(8,128)}, f32[200,1536]{1,0:T(8,128)S(1)}, f32[8,128]{1,0:T(8,128)S(1)}) custom-call(s32[5]{0:T(128)S(1)} %stack.32.refs_0_, f32[392,1536]{1,0:T(8,128)} %get-tuple-element.164.refs_1_, f32[392,1536]{1,0:T(8,128)} %get-tuple-element.255.refs_2_, f32[8,1536]{1,0:T(8,128)} %get-tuple-element.166.refs_3_, ...), custom_call_target="tpu_custom_call" | custom-call | flops 2147483648 | bytes 1 | tf_op jit(solution)/shard_map/last_fold1/pallas_call | solution.py:79
  130.4 1.5 up_fold3.1
  132.1 1.5 branch.1
  133.6 3.5 %collective-permute-done.17.refs_2_ = f32[96,1536]{1,0:T(8,128)S(1)} collective-permute-done((f32[96,1536]{1,0:T(8,128)S(1)}, f32[96,1536]{1,0:T(8,128)S(1)}, u32[]{:S(2)}, u32[]{:S(2)}) %collective-permute-start.17) | collective-permute-done | bytes 589856 | tf_op jit(solution)/shard_map/ppermute | solution.py:429
  137.7 2.7 %collective-permute-start.18 = (f32[48,1536]{1,0:T(8,128)S(1)}, f32[48,1536]{1,0:T(8,128)S(1)}, u32[]{:S(2)}, u32[]{:S(2)}) collective-permute-start(f32[48,1536]{1,0:T(8,128)S(1)} %get-tuple-element.188), channel_id=1, source_target_pairs={{0,16},{2,18},{4,20},{6,22},{8,24},{10,26},{12,28},{14,30},{16,0},... | collective-permute-start | bytes 884744 | tf_op jit(solution)/shard_map/ppermute | solution.py:429
  140.7 1.2 collective-permute-start.14
  141.9 8.5 %collective-permute-done.19.refs_3_ = f32[258,768]{1,0:T(8,128)S(1)} collective-permute-done((f32[258,768]{1,0:T(8,128)S(1)}, f32[258,768]{1,0:T(8,128)S(1)}, u32[]{:S(2)}, u32[]{:S(2)}) %collective-permute-start.19) | collective-permute-done | bytes 792608 | tf_op jit(solution)/shard_map/ppermute | solution.py:480
  150.4 1.9 input1.1
  152.3 13.5 %collective-permute-done.18.refs_1_ = f32[48,1536]{1,0:T(8,128)S(1)} collective-permute-done((f32[48,1536]{1,0:T(8,128)S(1)}, f32[48,1536]{1,0:T(8,128)S(1)}, u32[]{:S(2)}, u32[]{:S(2)}) %collective-permute-start.18) | collective-permute-done | bytes 294944 | tf_op jit(solution)/shard_map/ppermute | solution.py:429
  168.9 9.6 %collective-permute-done.15.refs_2_ = f32[96,1536]{1,0:T(8,128)S(1)} collective-permute-done((f32[96,1536]{1,0:T(8,128)S(1)}, f32[96,1536]{1,0:T(8,128)S(1)}, u32[]{:S(2)}, u32[]{:S(2)}) %collective-permute-start.15) | collective-permute-done | bytes 589856 | tf_op jit(solution)/shard_map/ppermute | solution.py:429
  179.8 2.0 copy.44
  181.8 10.3 %collective-permute-done.21.refs_2_ = f32[104,1536]{1,0:T(8,128)S(1)} collective-permute-done((f32[104,1536]{1,0:T(8,128)S(1)}, f32[104,1536]{1,0:T(8,128)S(1)}, u32[]{:S(2)}, u32[]{:S(2)}) %collective-permute-start.21) | collective-permute-done | bytes 639008 | tf_op jit(solution)/shard_map/ppermute | solution.py:429
  195.9 1.5 copy.43
  197.4 13.6 %collective-permute-done.22.refs_1_ = f32[56,1536]{1,0:T(8,128)S(1)} collective-permute-done((f32[56,1536]{1,0:T(8,128)S(1)}, f32[56,1536]{1,0:T(8,128)S(1)}, u32[]{:S(2)}, u32[]{:S(2)}) %collective-permute-start.22) | collective-permute-done | bytes 344096 | tf_op jit(solution)/shard_map/ppermute | solution.py:429
  (89 shorter events, 19.9 us)
Async XLA Ops:
  1.7 18.4 %collective-permute-start.7 = (f32[192,768]{1,0:T(8,128)S(1)}, f32[192,768]{1,0:T(8,128)}, u32[]{:S(2)}, u32[]{:S(2)}) collective-permute-start(f32[192,768]{1,0:T(8,128)S(1)} %dynamic-slice_convert_fusion), channel_id=1, source_target_pairs={{0,1},{1,0},{2,3},{3,2},{4,5},{5,4},{6,7},{7,6},{8,9},{9,8},{10,11... | collective-permute-start | bytes 1769480 | tf_op jit(solution)/shard_map/ppermute | solution.py:480
  4.7 15.2 %copy-start.21 = (bf16[2,258,768]{2,0,1:T(2,128)(2,1)S(1)}, bf16[2,258,768]{2,0,1:T(2,128)(2,1)}, u32[]{:S(2)}) copy-start(bf16[2,258,768]{2,0,1:T(2,128)(2,1)} %param.39) | copy-start | bytes 2377732
  17.7 12.7 %collective-permute-start.6 = (f32[258,384]{1,0:T(8,128)}, f32[258,384]{1,0:T(8,128)}, u32[]{:S(2)}, u32[]{:S(2)}) collective-permute-start(f32[258,384]{1,0:T(8,128)} %get-tuple-element.122.refs_7_.refs_3_), channel_id=1, source_target_pairs={{0,1},{1,0},{2,3},{3,2},{4,5},{5,4},{6,7},{7,6},{8,9},{9,8},{10,11... | collective-permute-start | bytes 1188872 | tf_op jit(solution)/shard_map/ppermute | solution.py:480
  17.8 20.6 %collective-permute-start.8 = (f32[258,384]{1,0:T(8,128)}, f32[258,384]{1,0:T(8,128)}, u32[]{:S(2)}, u32[]{:S(2)}) collective-permute-start(f32[258,384]{1,0:T(8,128)} %get-tuple-element.127.refs_7_.refs_4_), channel_id=1, source_target_pairs={{0,1},{1,0},{2,3},{3,2},{4,5},{5,4},{6,7},{7,6},{8,9},{9,8},{10,11... | collective-permute-start | bytes 1188872 | tf_op jit(solution)/shard_map/ppermute | solution.py:480
  20.1 2.4 %collective-permute-start = (f32[192,768]{1,0:T(8,128)}, f32[192,768]{1,0:T(8,128)}, u32[]{:S(2)}, u32[]{:S(2)}) collective-permute-start(f32[192,768]{1,0:T(8,128)} %param.1), channel_id=1, source_target_pairs={{0,2},{2,0},{4,6},{6,4},{8,10},{10,8},{12,14},{14,12},{16,18},{18,... | collective-permute-start | bytes 1769480 | tf_op jit(solution)/shard_map/cond/branch_1_fun/ppermute | solution.py:482
  22.5 1.1 copy-start.4
  23.6 6.9 %copy-start = (bf16[768,1536]{1,0:T(8,128)(2,1)S(1)}, bf16[768,1536]{1,0:T(8,128)(2,1)}, u32[]{:S(2)}) copy-start(bf16[768,1536]{1,0:T(8,128)(2,1)} %refs_10_.3) | copy-start | bytes 7077892
  23.6 6.9 %copy-start.1 = (bf16[1536,768]{1,0:T(8,128)(2,1)S(1)}, bf16[1536,768]{1,0:T(8,128)(2,1)}, u32[]{:S(2)}) copy-start(bf16[1536,768]{1,0:T(8,128)(2,1)} %refs_2_.6) | copy-start | bytes 7077892
  36.6 26.1 %collective-permute-start.9 = (f32[258,768]{1,0:T(8,128)}, f32[258,768]{1,0:T(8,128)}, u32[]{:S(2)}, u32[]{:S(2)}) collective-permute-start(f32[258,768]{1,0:T(8,128)} %get-tuple-element.134.refs_0_), channel_id=1, source_target_pairs={{0,1},{1,0},{2,3},{3,2},{4,5},{5,4},{6,7},{7,6},{8,9},{9,8},{10,11... | collective-permute-start | bytes 2377736 | tf_op jit(solution)/shard_map/ppermute | solution.py:480
  44.6 46.2 %collective-permute-start.11 = (f32[258,768]{1,0:T(8,128)}, f32[258,768]{1,0:T(8,128)}, u32[]{:S(2)}, u32[]{:S(2)}) collective-permute-start(f32[258,768]{1,0:T(8,128)} %get-tuple-element.150.refs_0_), channel_id=1, source_target_pairs={{0,1},{1,0},{2,3},{3,2},{4,5},{5,4},{6,7},{7,6},{8,9},{9,8},{10,11... | collective-permute-start | bytes 2377736 | tf_op jit(solution)/shard_map/ppermute | solution.py:480
  51.7 4.9 %collective-permute-start.1 = (f32[384,1536]{1,0:T(8,128)}, f32[384,1536]{1,0:T(8,128)}, u32[]{:S(2)}, u32[]{:S(2)}) collective-permute-start(f32[384,1536]{1,0:T(8,128)} %param.3), channel_id=1, source_target_pairs={{0,2},{2,0},{4,6},{6,4},{8,10},{10,8},{12,14},{14,12},{16,18},{18,... | collective-permute-start | bytes 7077896 | tf_op jit(solution)/shard_map/cond/branch_1_fun/ppermute | solution.py:407
  56.6 6.2 %copy-start.2 = (bf16[3,768,384]{2,1,0:T(8,128)(2,1)S(1)}, bf16[3,768,384]{2,1,0:T(8,128)(2,1)}, u32[]{:S(2)}) copy-start(bf16[3,768,384]{2,1,0:T(8,128)(2,1)} %refs_9_.3) | copy-start | bytes 5308420
  56.6 6.2 %copy-start.5 = (bf16[384,768]{1,0:T(8,128)(2,1)S(1)}, bf16[384,768]{1,0:T(8,128)(2,1)}, u32[]{:S(2)}) copy-start(bf16[384,768]{1,0:T(8,128)(2,1)} %refs_8_.3) | copy-start | bytes 1769476
  61.3 57.7 %collective-permute-start.13 = (f32[192,1536]{1,0:T(8,128)}, f32[192,1536]{1,0:T(8,128)}, u32[]{:S(2)}, u32[]{:S(2)}) collective-permute-start(f32[192,1536]{1,0:T(8,128)} %get-tuple-element.172), channel_id=1, source_target_pairs={{0,4},{2,6},{4,0},{6,2},{8,12},{10,14},{12,8},{14,10},{16,20},{18,... | collective-permute-start | bytes 3538952 | tf_op jit(solution)/shard_map/ppermute | solution.py:429
  71.8 50.4 %collective-permute-start.12 = (f32[258,768]{1,0:T(8,128)}, f32[258,768]{1,0:T(8,128)}, u32[]{:S(2)}, u32[]{:S(2)}) collective-permute-start(f32[258,768]{1,0:T(8,128)} %get-tuple-element.168.refs_2_), channel_id=1, source_target_pairs={{0,1},{1,0},{2,3},{3,2},{4,5},{5,4},{6,7},{7,6},{8,9},{9,8},{10,11... | collective-permute-start | bytes 2377736 | tf_op jit(solution)/shard_map/ppermute | solution.py:480
  78.7 4.9 %collective-permute-start.2 = (f32[384,1536]{1,0:T(8,128)}, f32[384,1536]{1,0:T(8,128)}, u32[]{:S(2)}, u32[]{:S(2)}) collective-permute-start(f32[384,1536]{1,0:T(8,128)} %param.5), channel_id=1, source_target_pairs={{0,2},{2,0},{4,6},{6,4},{8,10},{10,8},{12,14},{14,12},{16,18},{18,... | collective-permute-start | bytes 7077896 | tf_op jit(solution)/shard_map/cond/branch_1_fun/ppermute | solution.py:407
  83.5 6.4 %copy-start.20 = (bf16[2,258,768]{2,1,0:T(8,128)(2,1)S(1)}, bf16[2,258,768]{2,1,0:T(8,128)(2,1)}, u32[]{:S(2)}) copy-start(bf16[2,258,768]{2,1,0:T(8,128)(2,1)} %get-tuple-element.155) | copy-start | bytes 2377732
  83.5 7.3 %copy-start.3 = (bf16[3,768,384]{2,1,0:T(8,128)(2,1)S(1)}, bf16[3,768,384]{2,1,0:T(8,128)(2,1)}, u32[]{:S(2)}) copy-start(bf16[3,768,384]{2,1,0:T(8,128)(2,1)} %refs_9_.3) | copy-start | bytes 5308420
  88.3 2.6 %copy-start.6 = (bf16[384,768]{1,0:T(8,128)(2,1)S(1)}, bf16[384,768]{1,0:T(8,128)(2,1)}, u32[]{:S(2)}) copy-start(bf16[384,768]{1,0:T(8,128)(2,1)} %refs_8_.3) | copy-start | bytes 1769476
  88.3 42.0 %collective-permute-start.10 = (f32[192,1536]{1,0:T(8,128)}, f32[192,1536]{1,0:T(8,128)}, u32[]{:S(2)}, u32[]{:S(2)}) collective-permute-start(f32[192,1536]{1,0:T(8,128)} %get-tuple-element.148), channel_id=1, source_target_pairs={{0,8},{2,10},{4,12},{6,14},{8,0},{10,2},{12,4},{14,6},{16,24},{18,... | collective-permute-start | bytes 3538952 | tf_op jit(solution)/shard_map/ppermute | solution.py:429
  90.9 14.8 %copy-start.13 = (f32[8,768]{1,0:T(8,128)S(1)}, f32[8,768]{1,0:T(8,128)}, u32[]{:S(2)}) copy-start(f32[8,768]{1,0:T(8,128)} %get-tuple-element.158.refs_9_) | copy-start | bytes 73732
  90.9 14.8 %copy-start.14 = (f32[8,768]{1,0:T(8,128)S(1)}, f32[8,768]{1,0:T(8,128)}, u32[]{:S(2)}) copy-start(f32[8,768]{1,0:T(8,128)} %get-tuple-element.159.refs_10_) | copy-start | bytes 73732
  90.9 14.8 %copy-start.15 = (f32[8,768]{1,0:T(8,128)S(1)}, f32[8,768]{1,0:T(8,128)}, u32[]{:S(2)}) copy-start(f32[8,768]{1,0:T(8,128)} %get-tuple-element.160.refs_11_) | copy-start | bytes 73732
  99.6 0.9 copy-start.11
  100.5 4.2 %collective-permute-start.4 = (f32[8,1536]{1,0:T(8,128)S(1)}, f32[8,1536]{1,0:T(8,128)}, u32[]{:S(2)}, u32[]{:S(2)}) collective-permute-start(f32[8,1536]{1,0:T(8,128)S(1)} %param.9), channel_id=1, source_target_pairs={{0,1},{1,0},{2,3},{3,2},{4,5},{5,4},{6,7},{7,6},{8,9},{9,8},{10,11... | collective-permute-start | bytes 147464 | tf_op jit(solution)/shard_map/cond/branch_1_fun/ppermute | solution.py:480
  101.6 4.1 %collective-permute-start.5 = (f32[8,1536]{1,0:T(8,128)S(1)}, f32[8,1536]{1,0:T(8,128)}, u32[]{:S(2)}, u32[]{:S(2)}) collective-permute-start(f32[8,1536]{1,0:T(8,128)S(1)} %param.9), channel_id=1, source_target_pairs={{0,3},{1,2},{2,1},{3,0},{4,7},{5,6},{6,5},{7,4},{8,11},{9,10},{10,... | collective-permute-start | bytes 147464 | tf_op jit(solution)/shard_map/cond/branch_1_fun/ppermute | solution.py:560
  105.7 0.7 copy-start.16
  114.0 5.0 %collective-permute-start.3 = (f32[392,1536]{1,0:T(8,128)}, f32[392,1536]{1,0:T(8,128)}, u32[]{:S(2)}, u32[]{:S(2)}) collective-permute-start(f32[392,1536]{1,0:T(8,128)} %param.7), channel_id=1, source_target_pairs={{0,2},{2,0},{4,6},{6,4},{8,10},{10,8},{12,14},{14,12},{16,18},{18,... | collective-permute-start | bytes 7225352 | tf_op jit(solution)/shard_map/cond/branch_1_fun/ppermute | solution.py:407
  119.0 1.3 copy-start.18
  121.7 15.4 %collective-permute-start.17 = (f32[96,1536]{1,0:T(8,128)S(1)}, f32[96,1536]{1,0:T(8,128)S(1)}, u32[]{:S(2)}, u32[]{:S(2)}) collective-permute-start(f32[96,1536]{1,0:T(8,128)S(1)} %get-tuple-element.185), channel_id=1, source_target_pairs={{0,8},{2,10},{4,12},{6,14},{8,0},{10,2},{12,4},{14,6},{16,24},{18,... | collective-permute-start | bytes 1769480 | tf_op jit(solution)/shard_map/ppermute | solution.py:429
  124.6 4.9 %copy-start.12 = (f32[258,768]{1,0:T(8,128)S(1)}, f32[258,768]{1,0:T(8,128)}, u32[]{:S(2)}) copy-start(f32[258,768]{1,0:T(8,128)} %copy-done.11) | copy-start | bytes 2377732
  124.6 5.8 %copy-start.19 = (f32[192,1536]{1,0:T(8,128)S(1)}, f32[192,1536]{1,0:T(8,128)}, u32[]{:S(2)}) copy-start(f32[192,1536]{1,0:T(8,128)} %get-tuple-element.147.refs_1_) | copy-start | bytes 3538948
  128.8 37.7 %collective-permute-start.16 = (f32[200,1536]{1,0:T(8,128)S(1)}, f32[200,1536]{1,0:T(8,128)S(1)}, u32[]{:S(2)}, u32[]{:S(2)}) collective-permute-start(f32[200,1536]{1,0:T(8,128)S(1)} %get-tuple-element.183), channel_id=1, source_target_pairs={{0,4},{2,6},{4,0},{6,2},{8,12},{10,14},{12,8},{14,10},{16,20},{18,... | collective-permute-start | bytes 3686408 | tf_op jit(solution)/shard_map/ppermute | solution.py:429
  129.4 21.0 %collective-permute-start.19 = (f32[258,768]{1,0:T(8,128)S(1)}, f32[258,768]{1,0:T(8,128)S(1)}, u32[]{:S(2)}, u32[]{:S(2)}) collective-permute-start(f32[258,768]{1,0:T(8,128)S(1)} %copy-done.12), channel_id=1, source_target_pairs={{0,1},{1,0},{2,3},{3,2},{4,5},{5,4},{6,7},{7,6},{8,9},{9,8},{10,11... | collective-permute-start | bytes 2377736 | tf_op jit(solution)/shard_map/ppermute | solution.py:480
  130.3 1.5 copy-start.9
  130.4 1.7 copy-start.10
  137.7 28.1 %collective-permute-start.18 = (f32[48,1536]{1,0:T(8,128)S(1)}, f32[48,1536]{1,0:T(8,128)S(1)}, u32[]{:S(2)}, u32[]{:S(2)}) collective-permute-start(f32[48,1536]{1,0:T(8,128)S(1)} %get-tuple-element.188), channel_id=1, source_target_pairs={{0,16},{2,18},{4,20},{6,22},{8,24},{10,26},{12,28},{14,30},{16,0},... | collective-permute-start | bytes 884744 | tf_op jit(solution)/shard_map/ppermute | solution.py:429
  140.4 38.1 %collective-permute-start.15 = (f32[96,1536]{1,0:T(8,128)S(1)}, f32[96,1536]{1,0:T(8,128)S(1)}, u32[]{:S(2)}, u32[]{:S(2)}) collective-permute-start(f32[96,1536]{1,0:T(8,128)S(1)} %get-tuple-element.181), channel_id=1, source_target_pairs={{0,16},{2,18},{4,20},{6,22},{8,24},{10,26},{12,28},{14,30},{16,0},... | collective-permute-start | bytes 1769480 | tf_op jit(solution)/shard_map/ppermute | solution.py:429
  140.7 53.5 %collective-permute-start.14 = (f32[528,768]{1,0:T(8,128)S(1)}, f32[528,768]{1,0:T(8,128)S(1)}, u32[]{:S(2)}, u32[]{:S(2)}) collective-permute-start(f32[528,768]{1,0:T(8,128)S(1)} %get-tuple-element.179.refs_0_), channel_id=1, source_target_pairs={{0,1},{1,0},{2,3},{3,2},{4,5},{5,4},{6,7},{7,6},{8,9},{9,8},{10,11... | collective-permute-start | bytes 4866056 | tf_op jit(solution)/shard_map/ppermute | solution.py:480
  165.8 1.4 copy-start.17
  167.9 24.1 %collective-permute-start.21 = (f32[104,1536]{1,0:T(8,128)S(1)}, f32[104,1536]{1,0:T(8,128)S(1)}, u32[]{:S(2)}, u32[]{:S(2)}) collective-permute-start(f32[104,1536]{1,0:T(8,128)S(1)} %get-tuple-element.198), channel_id=1, source_target_pairs={{0,8},{2,10},{4,12},{6,14},{8,0},{10,2},{12,4},{14,6},{16,24},{18,... | collective-permute-start | bytes 1916936 | tf_op jit(solution)/shard_map/ppermute | solution.py:429
  179.1 14.3 %collective-permute-start.20 = (f32[48,1536]{1,0:T(8,128)S(1)}, f32[48,1536]{1,0:T(8,128)S(1)}, u32[]{:S(2)}, u32[]{:S(2)}) collective-permute-start(f32[48,1536]{1,0:T(8,128)S(1)} %get-tuple-element.196), channel_id=1, source_target_pairs={{0,4},{2,6},{4,0},{6,2},{8,12},{10,14},{12,8},{14,10},{16,20},{18,... | collective-permute-start | bytes 884744 | tf_op jit(solution)/shard_map/ppermute | solution.py:429
  192.7 18.3 %collective-permute-start.22 = (f32[56,1536]{1,0:T(8,128)S(1)}, f32[56,1536]{1,0:T(8,128)S(1)}, u32[]{:S(2)}, u32[]{:S(2)}) collective-permute-start(f32[56,1536]{1,0:T(8,128)S(1)} %get-tuple-element.206), channel_id=1, source_target_pairs={{0,16},{2,18},{4,20},{6,22},{8,24},{10,26},{12,28},{14,30},{16,0},... | collective-permute-start | bytes 1032200 | tf_op jit(solution)/shard_map/ppermute | solution.py:429
  193.4 1.2 copy-start.7
  193.4 1.5 copy-start.8
where the time goes:
time: 215 us; the launch traced here: 214 us
  Pallas kernels  91.5 us (43%)
  waiting for transfers between devices  86.2 us (40%)
  starting transfers between devices  20 us (9%)
  local copies, waits for them, and re-layouts  13.8 us (6%)
    pallas_call x25, Pallas kernels, call(): pl.pallas_call(without_tokens, grid=(grid,), out_shape=(*outs, shape((8,...  91.5 us
    ppermute x9, waiting for transfers between devices, fold(): self.got = lax.ppermute(send, 'dp', flips(self.dp, bit))  50.5 us
    ppermute x9, waiting for transfers between devices, per_device(): across = lambda v: lax.ppermute(v, 'mp', SWAP)  17.7 us
    ppermute x3, waiting for transfers between devices, start(): lax.ppermute(v, 'dp', flips(self.dp, 0))  14.6 us
    ppermute x9, starting transfers between devices, per_device(): across = lambda v: lax.ppermute(v, 'mp', SWAP)  10.4 us
    unnamed x48, local copies, waits for them, and re-layouts  9.84 us
    ppermute x9, starting transfers between devices, fold(): self.got = lax.ppermute(send, 'dp', flips(self.dp, bit))  9.41 us
  transfers between devices with their start and end apart: 23, of which 14 were waited for; matrix products, arithmetic and copies ran while one was open for 3% of the time, Pallas kernels for 43%

commit v1 on v0

--- a/solution.py
+++ b/solution.py
@@ -51,11 +51,11 @@
 
 
 def whole(x):
-    return pl.BlockSpec(x.shape, lambda i: (0,) * len(x.shape))
+    return pl.BlockSpec(x.shape, lambda i, *_: (0,) * len(x.shape))
 
 
 def one_of(x, image):
-    return pl.BlockSpec((None,) + x.shape[1:], lambda i: (image,) + (0,) * (x.ndim - 1))
+    return pl.BlockSpec((None,) + x.shape[1:], lambda i, *_: (image,) + (0,) * (x.ndim - 1))
 
 
 def scalars():
@@ -63,31 +63,45 @@
 
 
 ANYWHERE = pl.BlockSpec(memory_space=pl.ANY)
+
+
+def kernel(body, args, specs, outs, vmem, name, grid=1, out_specs=None, scratch=(), deep=(), scalar=0):
+    args = [pltpu.with_memory_space_constraint(a, pltpu.HBM) if i in deep else a for i, a in enumerate(args)]
+    return pl.pallas_call(
+        body,
+        out_shape=tuple(outs),
+        grid_spec=pltpu.PrefetchScalarGridSpec(
+            num_scalar_prefetch=scalar,
+            grid=(grid,),
+            in_specs=specs,
+            out_specs=tuple(out_specs or [whole(o) for o in outs]),
+            scratch_shapes=list(scratch),
+        ),
+        compiler_params=pltpu.CompilerParams(vmem_limit_bytes=vmem * MIB),
+        cost_estimate=pl.CostEstimate(flops=1 << 31, bytes_accessed=1, transcendentals=0),
+        name=name,
+    )(*args)
 
 
 class Chain:
     def __init__(self):
         self.token = jnp.zeros((8, 128), F32)
 
-    def call(self, body, args, specs, outs, vmem, name, grid=1, out_specs=None, scratch=(), deep=()):
+    def call(self, body, args, specs, outs, vmem, name, out_specs=None, **more):
         taken, given = len(args), len(outs)
-        args = [pltpu.with_memory_space_constraint(a, pltpu.HBM) if i in deep else a for i, a in enumerate(args)]
 
         def without_tokens(*refs):
             return body(*refs[:taken], *refs[taken + 1 : taken + 1 + given], *refs[taken + 2 + given :])
 
-        *got, self.token = pl.pallas_call(
-            without_tokens,
-            grid=(grid,),
-            out_shape=(*outs, shape((8, 128))),
-            in_specs=[*specs, ANYWHERE],
-            out_specs=(*(out_specs or [whole(o) for o in outs]), ANYWHERE),
-            scratch_shapes=list(scratch),
-            compiler_params=pltpu.CompilerParams(vmem_limit_bytes=vmem * MIB),
-            cost_estimate=pl.CostEstimate(flops=1 << 31, bytes_accessed=1, transcendentals=0),
-            name=name,
-        )(*args, self.token)
+        *got, self.token = kernel(
+            without_tokens, [*args, self.token], [*specs, ANYWHERE], [*outs, shape((8, 128))], vmem, name,
+            out_specs=[*(out_specs or [whole(o) for o in outs]), ANYWHERE], **more,
+        )
         return got
+
+    def hold(self, value):
+        value, self.token = lax.optimization_barrier((value, self.token))
+        return value
 
     def at_once(self, ids, moves, *values):
         outs = jax.eval_shape(moves, *values)
@@ -339,108 +353,145 @@
                 send[half:, :] = small
 
 
-def fold_body(size, bit, ids, kept, got, *refs):
-    *cross, keep, send = refs
-    own = pl.ds(pl.multiple_of(ids[bit] * size, 8), size)
-    away = pl.ds(pl.multiple_of((1 - ids[bit]) * size, 8), size)
-    send[0:size, :] = kept[away, :] + got[away, :]
-    keep[0:size, :] = kept[own, :] + got[own, :]
-    if keep.shape[0] > size:
-        small = kept[2 * size :, :] + got[2 * size :, :]
-        if cross:
-            small = small + (cross[0][...] + cross[1][...])
-        send[size:, :] = small
-        keep[size:, :] = small
-
-
-def last_body(size, kept, got, out, *small):
-    out[...] = kept[0:size, :] + got[0:size, :]
-    for ref in small:
-        ref[...] = kept[size:, :] + got[size:, :]
-
-
-class WeightSum:
-    def __init__(self, chain, ids, dp, name, order, chunk):
-        self.chain, self.ids, self.dp, self.name, self.order, self.chunk = chain, ids, dp, name, order, chunk
-        self.plain = not folded(dp)
-
-    def start(self, sets, small=()):
-        width = sets[0][0][0].shape[1]
-        self.columns = columns = sum(rights[0].shape[1] for _, rights in sets)
-        self.size = width // self.dp
-        self.extra = 8 if small else 0
-        if self.plain:
-            products = [
-                sum(mm_tn(left, right.astype(BF16)) for left, right in zip(*pair)) for pair in sets
-            ]
-            self.full = jnp.concatenate(products, 1)
-            self.part = sum(small)
+def sum_body(count, smalls, ids, *refs):
+    blocks, small_refs, outs = refs[:count], refs[count : count + smalls], refs[count + smalls :]
+    size = blocks[0].shape[0]
+    total = blocks[0][...] + blocks[1][...]
+    for ref in blocks[2:]:
+        total = total + ref[...]
+    outs[0][0:size, :] = total
+    if smalls:
+        kept, got, near, far_one, *rest = (ref[...] for ref in small_refs)
+        small = (kept + got) + (near + far_one)
+        for one in rest:
+            small = small + one
+        if len(outs) == 1:
+            outs[0][size:, :] = small
+        else:
+            outs[1][...] = small
+
+
+class Part:
+    def __init__(self, chain, ids, dp, name, order, arrays, columns, at, cross):
+        self.chain, self.ids, self.dp, self.name, self.order = chain, ids, dp, name, order
+        self.columns, self.at, self.cross = columns, at, cross
+        self.arrays = [(array, 0) for array in arrays]
+        self.half = arrays[0].shape[0] // 8 * 8 if cross is None else arrays[0].shape[0] - 8
+        self.steps = 0
+
+    def add(self, digits, flip, outs, name):
+        size = self.half >> digits
+        args, specs = [self.ids], []
+
+        def rows_of(level):
+            def index(j, ids):
+                at = 0
+                for digit in range(level, digits):
+                    bit = ids[self.order[digit]]
+                    at = 2 * at + ((1 - bit) if flip and digit == digits - 1 else bit)
+                return (at, self.at if level == 0 else 0)
+            return index
+
+        for array, level in self.arrays:
+            args.append(array)
+            specs.append(pl.BlockSpec((size, self.columns), rows_of(level)))
+        smalls = 0
+        if self.cross is not None:
+            small = [(array, (self.half >> level) // 8) for array, level in self.arrays]
+            small[2:2] = [(array, 0) for array in self.cross]
+            for array, row in small:
+                args.append(array)
+                specs.append(pl.BlockSpec((8, self.columns), lambda j, ids, row=row: (row, 0)))
+            smalls = len(small)
+        return self.chain.call(
+            partial(sum_body, len(self.arrays), smalls), args, specs, outs, 16, f"{self.name}_{name}",
+            scalar=1, deep=(1, 2) if digits == 1 else (1,),
+        )
+
+    def step(self):
+        if self.arrays is None:
             return
-        chunk, args, specs, layout, begin = self.chunk, [], [], [], 0
-        for lefts, rights in sets:
-            steps = rights[0].shape[1] // chunk
-            args += [*lefts, *rights]
-            specs += [whole(v) for v in lefts]
-            for v in rights:
-                block = lambda j, begin=begin, steps=steps: (0, jnp.clip(j - begin, 0, steps - 1))
-                specs.append(pl.BlockSpec((v.shape[0], chunk), block))
-            layout.append((len(lefts), steps))
-            begin += steps
-        images, rows = len(sets[0][0]), sets[0][0][0].shape[0]
-        spare = 8 * pl.cdiv(images * (rows % 8), 8)
-        depth = images * (rows // 8 * 8) + spare
-        self.rows = width // 2
-        dims = (self.rows + self.extra, columns)
-        block = pl.BlockSpec((self.rows + self.extra, chunk), lambda j: (0, j))
-        self.keep, send = self.chain.call(
-            partial(grads_body, layout, self.order, chunk, len(small)), [self.ids, *args, *small],
-            [scalars(), *specs] + [whole(v) for v in small], [far(dims), far(dims)], 32,
-            f"{self.name}_grads", grid=begin, out_specs=[block, block],
-            scratch=[
-                pltpu.VMEM((width, depth), BF16),
-                pltpu.VMEM((depth, chunk), BF16),
-                pltpu.VMEM((spare, max(width, chunk)), F32),
-            ],
-            deep=range(1, 1 + len(args)),
-        )
-        (self.got,) = self.chain.at_once(
-            self.ids, lambda v: (lax.ppermute(v, "dp", flips(self.dp, 0)),), send
-        )
-        self.at = 0
-
-    def fold(self, *cross):
-        if self.plain:
-            return
-        bit = self.order[self.at]
-        self.at += 1
-        self.rows //= 2
-        args = [self.ids, self.keep, self.got, *cross]
-        out = shape((self.rows + self.extra, self.columns))
-        if self.at == 1:
-            block = lambda v: pl.BlockSpec((v.shape[0], 512), lambda j: (0, j))
-            specs = [block(v) for v in args[1:]]
-            more = dict(grid=self.columns // 512, out_specs=[block(out)] * 2, deep=range(1, len(args)))
-        else:
-            specs, more = [whole(v) for v in args[1:]], {}
-        self.keep, send = self.chain.call(
-            partial(fold_body, self.rows, bit), args, [scalars(), *specs],
-            [far(out.shape), out] if self.at == 1 else [out, out], 16, f"{self.name}_fold{bit}", **more,
-        )
-        self.got = lax.ppermute(send, "dp", flips(self.dp, bit))
+        bit = self.order[self.steps]
+        self.steps += 1
+        extra = 0 if self.cross is None else 8
+        out = shape(((self.half >> self.steps) + extra, self.columns))
+        (send,) = self.add(self.steps, True, [out], f"step{bit}")
+        self.arrays.append((lax.ppermute(send, "dp", flips(self.dp, bit)), self.steps))
 
     def finish(self):
-        if self.plain:
-            return lax.psum_scatter(self.full, "dp", scatter_dimension=0, tiled=True)
-        outs = [shape((self.size, self.columns))]
-        if self.extra:
-            outs.append(shape((self.extra, self.columns)))
-        got = self.chain.call(
-            partial(last_body, self.size), [self.keep, self.got],
-            [whole(self.keep), whole(self.got)], outs, 16, f"{self.name}_last",
-        )
-        if self.extra:
-            self.small = got[1]
-        return got[0]
+        outs = [shape((self.half >> self.steps, self.columns))]
+        if self.cross is not None:
+            outs.append(shape((8, self.columns)))
+        return self.add(self.steps, False, outs, "last")
+
+
+class Plain:
+    def __init__(self, full, small):
+        self.full, self.small = full, small
+
+    def step(self):
+        pass
+
+    def finish(self):
+        total = lax.psum_scatter(self.full, "dp", scatter_dimension=0, tiled=True)
+        return [total] if self.small is None else [total, lax.psum(self.small, "dp")]
+
+
+def weight_sum(chain, ids, dp, name, chunk, sets, smalls=(), cross=None, beside=None, parts=1, order=(1, 2, 3)):
+    width = sets[0][0][0].shape[1]
+    columns = sum(rights[0].shape[1] for _, rights in sets)
+    size = columns // parts
+    if not folded(dp):
+        products = [sum(mm_tn(left, right.astype(BF16)) for left, right in zip(*pair)) for pair in sets]
+        full = jnp.concatenate(products, 1)
+        small = sum(smalls) + cross if smalls else None
+        pieces = [
+            Plain(full[:, i * size : (i + 1) * size], small if i == 0 else None) for i in range(parts)
+        ]
+        return pieces, beside() if beside else None
+    args, specs, layout, begin = [], [], [], 0
+    for lefts, rights in sets:
+        steps = rights[0].shape[1] // chunk
+        args += [*lefts, *rights]
+        specs += [whole(v) for v in lefts]
+        for v in rights:
+            block = lambda j, begin=begin, steps=steps: (0, jnp.clip(j - begin, 0, steps - 1))
+            specs.append(pl.BlockSpec((v.shape[0], chunk), block))
+        layout.append((len(lefts), steps))
+        begin += steps
+    images, rows = len(sets[0][0]), sets[0][0][0].shape[0]
+    spare = 8 * pl.cdiv(images * (rows % 8), 8)
+    depth = images * (rows // 8 * 8) + spare
+    dims = (width // 2 + (8 if smalls else 0), columns)
+    block = pl.BlockSpec((dims[0], chunk), lambda j: (0, j))
+    keep, send = chain.call(
+        partial(grads_body, layout, order, chunk, len(smalls)), [ids, *args, *smalls],
+        [scalars(), *specs] + [whole(v) for v in smalls], [far(dims), far(dims)], 32,
+        f"{name}_grads", grid=begin, out_specs=[block, block],
+        scratch=[
+            pltpu.VMEM((width, depth), BF16),
+            pltpu.VMEM((depth, chunk), BF16),
+            pltpu.VMEM((spare, max(width, chunk)), F32),
+        ],
+        deep=range(1, 1 + len(args)),
+    )
+    swap = lambda v: lax.ppermute(v, "dp", flips(dp, 0))
+    if cross is not None:
+        got, distant = chain.at_once(ids, lambda v, c: (swap(v), swap(c)), send, cross)
+        crosses, done = (cross, distant), None
+    elif beside:
+        got, done = chain.at_once(ids, lambda v: (swap(v), beside()), send)
+        crosses = None
+    else:
+        (got,) = chain.at_once(ids, lambda v: (swap(v),), send)
+        crosses, done = None, None
+    pieces = [
+        Part(chain, ids, dp, f"{name}{i}", order, [keep, got], size, i, crosses if i == 0 else None)
+        for i in range(parts)
+    ]
+    for piece in pieces:
+        piece.half = width // 2
+    return pieces, done
 
 
 def folded(dp):
@@ -523,12 +574,17 @@
             kept.append(one)
         norm_others.append(across(norms[b]))
 
-    down_sum, up_sum, last_sum = (
-        WeightSum(chain, ids, dp, *how)
-        for how in (("down", (1, 2, 3), 512), ("up", (2, 3, 1), 512), ("last", (1, 2, 3), 384))
-    )
-    down_sum.start([([cotangent[b] for b in every], hiddens)])
-    down_sum.fold()
+    padded = images * 8 * pl.cdiv(rows, 8)
+
+    def branch():
+        return kernel(
+            branch_body, [*hiddens, down_weight], [whole(a) for a in (*hiddens, down_weight)],
+            [shape((padded, width))], 32, "branch",
+        )[0]
+
+    dys = [cotangent[b] for b in every]
+    (down_sum,), down_part = weight_sum(chain, ids, dp, "down", 512, [(dys, hiddens)], beside=branch)
+    down_sum.step()
 
     grads, attns, backs, firsts_part, crosses, part_others = [], [], [], [], [], []
     for b in every:
@@ -545,22 +601,21 @@
         )
         for kept, one in zip((grads, attns, backs, firsts_part, smalls, crosses), got):
             kept.append(one)
-        if b < images - 1:
-            part_others.append(across(firsts_part[b]))
+        if b == images - 1:
+            cross = across(crosses[-1])
+        part_others.append(across(firsts_part[b]))
         if b == 0:
-            up_sum.start([(seconds, uppers)])
-            up_sum.fold()
-    last_sum.start(
-        [(attns, mixeds), ([firsts[b] for b in every], backs)], [*smalls, crosses[-1][:, :width]]
+            (up_sum,), _ = weight_sum(chain, ids, dp, "up", 512, [(seconds, uppers)])
+            up_sum.step()
+    part_others[0] = chain.hold(part_others[0])
+    down_sum.step()
+    down_part = chain.hold(down_part)
+    down_other = across(down_part)
+    sets = [(attns, mixeds), ([firsts[b] for b in every], backs)]
+    (out_sum, qkv_sum), _ = weight_sum(
+        chain, ids, dp, "last", 384, sets, [*smalls, crosses[-1][:, :width]],
+        cross if folded(dp) else cross[:, :width], parts=2,
     )
-    down_sum.fold()
-    pairs = [((d, m), (d ^ 1, m ^ 1)) for d in range(dp) for m in range(2)]
-    corners = [(2 * p[0] + p[1], 2 * q[0] + q[1]) for p, q in pairs]
-    cross = chain.at_once(
-        ids, lambda v: (across(v), lax.ppermute(v, ("dp", "mp"), corners)), crosses[-1]
-    )
-    firsts_part[-1], chain.token = lax.optimization_barrier((firsts_part[-1], chain.token))
-    part_others.append(across(firsts_part[-1]))
 
     def input_of(b):
         args = [first_gain, seqs, firsts_part[b], part_others[b], grads[b]]
@@ -570,36 +625,32 @@
             input_body, args, specs, [shape((rows, width))], 32, f"input{b}", deep=(0, 1, 4)
         )[0]
 
+    out_sum.step()
+    qkv_sum.step()
     input_grads = [input_of(b) for b in range(images - 1)]
-    last_sum.fold(*cross)
-    up_sum.fold()
-    padded = images * 8 * pl.cdiv(rows, 8)
-    (down_part,) = chain.call(
-        branch_body, [*hiddens, down_weight], [whole(a) for a in (*hiddens, down_weight)],
-        [shape((padded, width))], 32, "branch",
-    )
-    down_other = across(down_part)
-    down_sum.fold()
+    down_sum.step()
+    up_sum.step()
     input_grads.append(input_of(images - 1))
-    down_total = down_sum.finish()
-    last_sum.fold()
-    up_sum.fold()
-    last_sum.fold()
-    up_total = up_sum.finish()
+    (down_total,) = down_sum.finish()
+    out_sum.step()
+    up_sum.step()
+    qkv_sum.step()
+    out_sum.step()
+    (up_total,) = up_sum.finish()
+    qkv_sum.step()
+    out_total, small = out_sum.finish()
     args = [down_part, down_other, down_bias, *middles]
     (output,) = chain.call(
         partial(output_body, images), args, [whole(a) for a in args],
         [shape((images, rows, width), BF16)], 32, "output", deep=(2,),
     )
-    last_total = last_sum.finish()
-    if last_sum.plain:
-        last_sum.small = lax.psum(last_sum.part + across(crosses[-1][:, :width]), "dp")
-    small = last_sum.small[:, :width]
+    (qkv_total,) = qkv_sum.finish()
+    small = small[:, :width]
     return (
         output,
         jnp.stack(input_grads),
-        last_total[:, inner:].reshape(-1, 3, inner).transpose(1, 0, 2),
-        last_total[:, :inner].T,
+        jnp.stack([out_total[:, inner:], qkv_total[:, :inner], qkv_total[:, inner:]]),
+        out_total[:, :inner].T,
         small[5],
         up_total,
         small[0:2].reshape(-1),

time: 215 us -> 187 us (0.87)
  waiting for transfers between devices: 86.2 us -> 47.7 us
  Pallas kernels: 91.5 us -> 106 us
  local copies, waits for them, and re-layouts: 13.8 us -> 8.63 us
    ppermute x13 -> x16, waiting for transfers between devices: 66.1 us -> 38.8 us  [the longest x12 27.2 us: step(): lax.ppermute(send, 'dp', flips(self.dp, bit))]
    pallas_call x25 -> x29, Pallas kernels: 91.5 us -> 106 us  [kernel(): pl.pallas_call(body, out_shape=tuple(outs), grid_spec=pltpu.PrefetchScala...]
    ppermute x9, waiting for transfers between devices: 17.7 us -> 6.53 us  [per_device(): across = lambda v: lax.ppermute(v, 'mp', SWAP)]
    unnamed x48 -> x33, local copies, waits for them, and re-layouts: 9.84 us -> 4.73 us
    ppermute x13 -> x16, starting transfers between devices: 9.56 us -> 10.2 us  [the longest x12 9.51 us: step(): lax.ppermute(send, 'dp', flips(self.dp, bit))]
  transfers between devices with their start and end apart: 23 -> 26, of which waited for: 14 -> 12; matrix products, arithmetic and copies ran while one was open for 3% -> 4% of each run, Pallas kernels for 43% -> 56%
where the time goes in v1:
time: 187 us
  Pallas kernels  106 us (57%)
  waiting for transfers between devices  47.7 us (26%)
  starting transfers between devices  19.9 us (11%)
  local copies, waits for them, and re-layouts  8.63 us (5%)
  other arithmetic  2.63 us (1%)
    pallas_call x29, Pallas kernels, kernel(): pl.pallas_call(body, out_shape=tuple(outs), grid_spec=pltpu.PrefetchScala...  106 us
    ppermute x12, waiting for transfers between devices, step(): lax.ppermute(send, 'dp', flips(self.dp, bit))  27.2 us
    ppermute x4, waiting for transfers between devices, weight_sum(): swap = lambda v: lax.ppermute(v, 'dp', flips(dp, 0))  11.6 us
    ppermute x9, starting transfers between devices, per_device(): across = lambda v: lax.ppermute(v, 'mp', SWAP)  9.69 us
    ppermute x12, starting transfers between devices, step(): lax.ppermute(send, 'dp', flips(self.dp, bit))  9.51 us
    ppermute x9, waiting for transfers between devices, per_device(): across = lambda v: lax.ppermute(v, 'mp', SWAP)  6.53 us
    unnamed x33, local copies, waits for them, and re-layouts  4.73 us
  transfers between devices with their start and end apart: 26, of which 12 were waited for; matrix products, arithmetic and copies ran while one was open for 4% of the time, Pallas kernels for 56%

profile of v1, /device:TPU:0, one launch (start us, length us, event | category | flops | bytes accessed | tf_op | source)
XLA Modules:
  0.0 186.6 jit_solution(7717885406802056475)
XLA Ops:
  0.7 1.8 dynamic-slice_convert_fusion
  2.5 3.0 %collective-permute-start.6 = (f32[192,768]{1,0:T(8,128)}, f32[192,768]{1,0:T(8,128)}, u32[]{:S(2)}, u32[]{:S(2)}) collective-permute-start(f32[192,768]{1,0:T(8,128)} %dynamic-slice_convert_fusion), channel_id=1, source_target_pairs={{0,1},{1,0},{2,3},{3,2},{4,5},{5,4},{6,7},{7,6},{8,9},{9,8},{10,11... | collective-permute-start | bytes 1769480 | tf_op jit(solution)/shard_map/ppermute | solution.py:531
  5.5 12.7 %attend.1 = (f32[2,258,768]{2,1,0:T(8,128)}, bf16[2,258,768]{2,1,0:T(8,128)(2,1)}, bf16[2,258,1152]{2,1,0:T(8,128)(2,1)}, f32[2,258,128]{2,1,0:T(8,128)}, f32[25...) custom-call(s32[2,256]{1,0:T(2,128)} %refs_0_.3, bf16[2,1024,768]{2,1,0:T(8,128)(2,1)} %refs_1_.2, ...), custom_call_target="tpu_custom_call" | custom-call | flops 2147483648 | bytes 1 | tf_op jit(solution)/shard_map/attend/pallas_call | solution.py:70
  18.2 2.0 %collective-permute-start.7 = (f32[258,384]{1,0:T(8,128)S(1)}, f32[258,384]{1,0:T(8,128)S(1)}, u32[]{:S(2)}, u32[]{:S(2)}) collective-permute-start(f32[258,384]{1,0:T(8,128)S(1)} %get-tuple-element.137.refs_7_.refs_4_), channel_id=1, source_target_pairs={{0,1},{1,0},{2,3},{3,2},{4,5},{5,4},{6,7},{7,6},{8,9},{9,8},{10,11... | collective-permute-start | bytes 1188872 | tf_op jit(solution)/shard_map/ppermute | solution.py:531
  21.6 2.4 %conditional.4 = (f32[192,768]{1,0:T(8,128)}) conditional(s32[]{:T(128)} %bitcast.5, () %tuple.39, f32[192,768]{1,0:T(8,128)} %collective-permute-done.6.refs_2_), branch_computations={%region_0.1_spmd, %region_1.2_spmd} | conditional | bytes 2359344 | solution.py:110
  21.7 2.3 %collective-permute-done = f32[192,768]{1,0:T(8,128)} collective-permute-done((f32[192,768]{1,0:T(8,128)}, f32[192,768]{1,0:T(8,128)}, u32[]{:S(2)}, u32[]{:S(2)}) %collective-permute-start) | collective-permute-done | bytes 589856 | tf_op jit(solution)/shard_map/cond/branch_1_fun/ppermute | solution.py:533
  25.6 5.0 %collective-permute-done.5.refs_8_ = f32[258,384]{1,0:T(8,128)S(1)} collective-permute-done((f32[258,384]{1,0:T(8,128)S(1)}, f32[258,384]{1,0:T(8,128)S(1)}, u32[]{:S(2)}, u32[]{:S(2)}) %collective-permute-start.5) | collective-permute-done | bytes 396320 | tf_op jit(solution)/shard_map/ppermute | solution.py:531
  30.5 5.9 %forward0.1 = (f32[258,768]{1,0:T(8,128)}, bf16[258,768]{1,0:T(8,128)(2,1)}, bf16[258,1536]{1,0:T(8,128)(2,1)}, bf16[258,1536]{1,0:T(8,128)(2,1)}, f32[258,768]{...) custom-call(s32[5]{0:T(128)S(1)} %stack.44.refs_0_, f32[2,258,768]{2,1,0:T(8,128)} %get-tuple-element.131.refs_1_.refs_5_, ...), custom_call_target="tpu_custom_call" | custom-call | flops 2147483648 | bytes 1 | tf_op jit(solution)/shard_map/forward0/pallas_call | solution.py:70
  39.0 6.0 %forward1.1 = (f32[258,768]{1,0:T(8,128)}, bf16[258,768]{1,0:T(8,128)(2,1)}, bf16[258,1536]{1,0:T(8,128)(2,1)}, bf16[258,1536]{1,0:T(8,128)(2,1)}, f32[258,768]{...) custom-call(s32[5]{0:T(128)S(1)} %stack.44.refs_0_, f32[2,258,768]{2,1,0:T(8,128)} %get-tuple-element.131.refs_1_.refs_5_, ...), custom_call_target="tpu_custom_call" | custom-call | flops 2147483648 | bytes 1 | tf_op jit(solution)/shard_map/forward1/pallas_call | solution.py:70
  45.0 6.1 %down_grads.1 = (f32[384,1536]{1,0:T(8,128)}, f32[384,1536]{1,0:T(8,128)}, f32[8,128]{1,0:T(8,128)S(1)}) custom-call(s32[5]{0:T(128)S(1)} %stack.44.refs_0_, bf16[258,768]{1,0:T(8,128)(2,1)} %get-tuple-element.245.refs_1_, bf16[258,768]{1,0:T(8,128)(2,1)} %get-tuple-element.244.refs_2_, bf16[258,1536]{1,0:T(8,128)(2,1)} %get-tuple-element.136.refs_3_, ...), custom_call_target="tpu_custom_call" | custom-call | flops 2147483648 | bytes 1 | tf_op jit(solution)/shard_map/down_grads/pallas_call | solution.py:70
  51.0 5.1 %conditional.5 = (f32[384,1536]{1,0:T(8,128)}, f32[528,768]{1,0:T(8,128)}) conditional(s32[]{:T(128)} %bitcast.5, () %tuple.38, (f32[384,1536]{1,0:T(8,128)}, bf16[258,1536]{1,0:T(8,128)(2,1)S(1)}, bf16[258,1536]{1,0:T(8,128)(2,1)S(1)}, bf16[1536,768]{1,0:T(8,128)(2,1)S(1)}) %tuple.67), branch_computations={%region_2.3_spmd, %region_3.4_spmd} | conditional | flops 2147483648 | bytes 9437241 | solution.py:110
  51.3 2.6 %branch.1 = f32[528,768]{1,0:T(8,128)} custom-call(bf16[258,1536]{1,0:T(8,128)(2,1)S(1)} %get-tuple-element.21.refs_0_, bf16[258,1536]{1,0:T(8,128)(2,1)S(1)} %get-tuple-element.22.refs_1_, bf16[1536,768]{1,0:T(8,128)(2,1)S(1)} %get-tuple-element.23.refs_2_), custom_call_target="tpu_custom_call" | custom-call | flops 2147483648 | bytes 1 | tf_op jit(solution)/shard_map/cond/branch_1_fun/branch/pallas_call | solution.py:70
  53.9 2.2 %collective-permute-done.1 = f32[384,1536]{1,0:T(8,128)} collective-permute-done((f32[384,1536]{1,0:T(8,128)}, f32[384,1536]{1,0:T(8,128)}, u32[]{:S(2)}, u32[]{:S(2)}) %collective-permute-start.1) | collective-permute-done | bytes 2359328 | tf_op jit(solution)/shard_map/cond/branch_1_fun/ppermute | solution.py:478
  56.2 3.3 %down0_step1.1 = (f32[192,1536]{1,0:T(8,128)}, f32[8,128]{1,0:T(8,128)S(1)}) custom-call(s32[5]{0:T(128)S(1)} %stack.44.refs_0_, f32[384,1536]{1,0:T(8,128)} %get-tuple-element.143.refs_1_, f32[384,1536]{1,0:T(8,128)} %get-tuple-element.144.refs_2_, f32[8,128]{1,0:T(8,128)S(1)} %get-tuple-element.145.refs_3_), custom_call_target="tpu_custom_call" | custom-call | flops 2147483648 | bytes 1 | tf_op jit(solution)/shard_map/down0_step1/pallas_call | solution.py:70
  61.5 9.1 %backward0.1 = (f32[258,768]{1,0:T(8,128)}, bf16[258,768]{1,0:T(8,128)(2,1)}, bf16[258,1152]{1,0:T(8,128)(2,1)}, f32[258,768]{1,0:T(8,128)}, f32[8,768]{1,0:T(8,...) custom-call(f32[258,768]{1,0:T(8,128)} %get-tuple-element.147.refs_0_, f32[258,768]{1,0:T(8,128)} %collective-permute-done.9.refs_1_, ...), custom_call_target="tpu_custom_call" | custom-call | flops 2147483648 | bytes 1 | tf_op jit(solution)/shard_map/backward0/pallas_call | solution.py:70
  73.1 5.9 %up_grads.1 = (f32[384,1536]{1,0:T(8,128)}, f32[384,1536]{1,0:T(8,128)}, f32[8,128]{1,0:T(8,128)S(1)}) custom-call(s32[5]{0:T(128)S(1)} %stack.44.refs_0_, bf16[258,768]{1,0:T(8,128)(2,1)} %get-tuple-element.156.refs_1_, bf16[258,768]{1,0:T(8,128)(2,1)} %get-tuple-element.157.refs_2_, bf16[258,1536]{1,0:T(8,128)(2,1)} %get-tuple-element.158.refs_3_, ...), custom_call_target="tpu_custom_call" | custom-call | flops 2147483648 | bytes 1 | tf_op jit(solution)/shard_map/up_grads/pallas_call | solution.py:70
  79.0 4.9 %conditional.6 = (f32[384,1536]{1,0:T(8,128)}) conditional(s32[]{:T(128)} %bitcast.5, () %tuple.41, f32[384,1536]{1,0:T(8,128)} %get-tuple-element.162), branch_computations={%region_4.5_spmd, %region_5.6_spmd} | conditional | bytes 9437232 | solution.py:110
  79.0 4.9 %collective-permute-done.2 = f32[384,1536]{1,0:T(8,128)} collective-permute-done((f32[384,1536]{1,0:T(8,128)}, f32[384,1536]{1,0:T(8,128)}, u32[]{:S(2)}, u32[]{:S(2)}) %collective-permute-start.2) | collective-permute-done | bytes 2359328 | tf_op jit(solution)/shard_map/cond/branch_1_fun/ppermute | solution.py:478
  83.9 3.3 %up0_step1.1 = (f32[192,1536]{1,0:T(8,128)}, f32[8,128]{1,0:T(8,128)S(1)}) custom-call(s32[5]{0:T(128)S(1)} %stack.44.refs_0_, f32[384,1536]{1,0:T(8,128)} %get-tuple-element.161.refs_1_, f32[384,1536]{1,0:T(8,128)} %get-tuple-element.259.refs_2_, f32[8,128]{1,0:T(8,128)S(1)} %get-tuple-element.163.refs_3_), custom_call_target="tpu_custom_call" | custom-call | flops 2147483648 | bytes 1 | tf_op jit(solution)/shard_map/up0_step1/pallas_call | solution.py:70
  87.2 9.0 %backward1.1 = (f32[258,768]{1,0:T(8,128)}, bf16[258,768]{1,0:T(8,128)(2,1)}, bf16[258,1152]{1,0:T(8,128)(2,1)}, f32[258,768]{1,0:T(8,128)}, f32[8,768]{1,0:T(8,...) custom-call(f32[258,768]{1,0:T(8,128)} %get-tuple-element.153.refs_0_, f32[258,768]{1,0:T(8,128)} %collective-permute-done.11.refs_1_, ...), custom_call_target="tpu_custom_call" | custom-call | flops 2147483648 | bytes 1 | tf_op jit(solution)/shard_map/backward1/pallas_call | solution.py:70
  98.8 2.9 %down0_step2.1 = (f32[96,1536]{1,0:T(8,128)}, f32[8,128]{1,0:T(8,128)S(1)}) custom-call(s32[5]{0:T(128)S(1)} %stack.44.refs_0_, f32[384,1536]{1,0:T(8,128)} %get-tuple-element.143.refs_1_, f32[384,1536]{1,0:T(8,128)} %get-tuple-element.144.refs_2_, f32[192,1536]{1,0:T(8,128)} %collective-permute-done.8.refs_3_, f32[8,128]{1,0:T(8,128)S(1)} %get-tuple-element.166.refs_4_), custom_call_target="tpu_custom_call" | custom-call | flops 2147483648 | bytes 1 | tf_op jit(solution)/shard_map/down0_step2/pallas_call | solution.py:70
  101.6 1.6 collective-permute-start.15
  103.2 7.5 %last_grads.1 = (f32[392,1536]{1,0:T(8,128)}, f32[392,1536]{1,0:T(8,128)}, f32[8,128]{1,0:T(8,128)S(1)}) custom-call(s32[5]{0:T(128)S(1)} %stack.44.refs_0_, bf16[258,768]{1,0:T(8,128)(2,1)} %get-tuple-element.169.refs_1_, bf16[258,768]{1,0:T(8,128)(2,1)} %get-tuple-element.170.refs_2_, f32[258,384]{1,0:T(8,128)} %copy-done.5, f32[258,384]{1,0:T(8,128)} %copy-done.6, ...), custom_call_target="tpu_custom_call" | custom-call | flops 2147483648 | bytes 1 | tf_op jit(solution)/shard_map/last_grads/pallas_call | solution.py:70
  110.8 5.1 %conditional.7 = (f32[392,1536]{1,0:T(8,128)}, f32[8,1536]{1,0:T(8,128)}) conditional(s32[]{:T(128)} %bitcast.5, () %tuple.44, (f32[392,1536]{1,0:T(8,128)}, f32[8,1536]{1,0:T(8,128)S(1)}) %tuple.45), branch_computations={%region_6.7_spmd, %region_7.8_spmd} | conditional | bytes 9830496 | solution.py:110
  111.4 3.9 %collective-permute-done.4 = f32[8,1536]{1,0:T(8,128)} collective-permute-done((f32[8,1536]{1,0:T(8,128)S(1)}, f32[8,1536]{1,0:T(8,128)}, u32[]{:S(2)}, u32[]{:S(2)}) %collective-permute-start.4) | collective-permute-done | bytes 49184 | tf_op jit(solution)/shard_map/cond/branch_1_fun/ppermute | solution.py:478
  115.9 1.9 last0_step1.1
  117.7 1.6 collective-permute-start.14
  119.3 1.9 last1_step1.1
  121.7 2.4 %input0.1 = (f32[258,768]{1,0:T(8,128)S(1)}, f32[8,128]{1,0:T(8,128)S(1)}) custom-call(f32[768]{0:T(1024)} %refs_0_.5, f32[2,258,768]{2,1,0:T(8,128)} %get-tuple-element.131.refs_1_.refs_5_, f32[258,768]{1,0:T(8,128)} %get-tuple-element.152.refs_2_, f32[258,768]{1,0:T(8,128)} %collective-permute-done.10.refs_3_, f32[258,768]{1,0:T(8,128)} %get-tuple-element.188.refs_4_, ...), custom_call_target="tpu_custom_call" | custom-call | flops 2147483648 | bytes 1 | tf_op jit(solution)/shard_map/input0/pallas_call | solution.py:70
  124.7 1.8 down0_step3.1
  126.6 2.7 %collective-permute-start.16 = (f32[48,1536]{1,0:T(8,128)S(1)}, f32[48,1536]{1,0:T(8,128)S(1)}, u32[]{:S(2)}, u32[]{:S(2)}) collective-permute-start(f32[48,1536]{1,0:T(8,128)S(1)} %get-tuple-element.192), channel_id=1, source_target_pairs={{0,16},{2,18},{4,20},{6,22},{8,24},{10,26},{12,28},{14,30},{16,0},... | collective-permute-start | bytes 884744 | tf_op jit(solution)/shard_map/ppermute | solution.py:419
  129.2 1.9 %up0_step2.1 = (f32[96,1536]{1,0:T(8,128)S(1)}, f32[8,128]{1,0:T(8,128)S(1)}) custom-call(s32[5]{0:T(128)S(1)} %stack.44.refs_0_, f32[384,1536]{1,0:T(8,128)} %get-tuple-element.161.refs_1_, f32[384,1536]{1,0:T(8,128)} %get-tuple-element.259.refs_2_, f32[192,1536]{1,0:T(8,128)S(1)} %collective-permute-done.18.refs_3_, f32[8,128]{1,0:T(8,128)S(1)} %get-tuple-element.196.refs_4_), custom_call_target="tpu_custom_call" | custom-call | flops 2147483648 | bytes 1 | tf_op jit(solution)/shard_map/up0_step2/pallas_call | solution.py:70
  131.9 2.2 %input1.1 = (f32[258,768]{1,0:T(8,128)S(1)}, f32[8,128]{1,0:T(8,128)S(1)}) custom-call(f32[768]{0:T(1024)} %refs_0_.5, f32[2,258,768]{2,1,0:T(8,128)} %get-tuple-element.131.refs_1_.refs_5_, f32[258,768]{1,0:T(8,128)} %get-tuple-element.193.refs_2_, f32[258,768]{1,0:T(8,128)S(1)} %collective-permute-done.17.refs_3_, f32[258,768]{1,0:T(8,128)} %get-tuple-element.194.refs_4_, ...), custom_call_target="tpu_custom_call" | custom-call | flops 2147483648 | bytes 1 | tf_op jit(solution)/shard_map/input1/pallas_call | solution.py:70
  134.2 2.0 %copy.35 = f32[2,258,768]{2,0,1:T(2,128)} copy(f32[2,258,768]{2,1,0:T(8,128)S(1)} %pad_maximum_fusion) | data formatting | bytes 3170304
  136.2 5.9 %collective-permute-done.16.refs_5_ = f32[48,1536]{1,0:T(8,128)S(1)} collective-permute-done((f32[48,1536]{1,0:T(8,128)S(1)}, f32[48,1536]{1,0:T(8,128)S(1)}, u32[]{:S(2)}, u32[]{:S(2)}) %collective-permute-start.16) | collective-permute-done | bytes 294944 | tf_op jit(solution)/shard_map/ppermute | solution.py:419
  142.0 2.6 %down0_last.1 = (f32[48,1536]{1,0:T(8,128)}, f32[8,128]{1,0:T(8,128)S(1)}) custom-call(s32[5]{0:T(128)S(1)} %stack.44.refs_0_, f32[384,1536]{1,0:T(8,128)} %get-tuple-element.143.refs_1_, f32[384,1536]{1,0:T(8,128)} %get-tuple-element.144.refs_2_, f32[192,1536]{1,0:T(8,128)} %collective-permute-done.8.refs_3_, f32[96,1536]{1,0:T(8,128)} %collective-permute-done.15.refs_4_, ...), custom_call_target="tpu_custom_call" | custom-call | flops 2147483648 | bytes 1 | tf_op jit(solution)/shard_map/down0_last/pallas_call | solution.py:70
  144.6 1.7 last0_step2.1
  146.4 6.8 %collective-permute-done.21.refs_4_ = f32[96,1536]{1,0:T(8,128)S(1)} collective-permute-done((f32[96,1536]{1,0:T(8,128)S(1)}, f32[96,1536]{1,0:T(8,128)S(1)}, u32[]{:S(2)}, u32[]{:S(2)}) %collective-permute-start.21) | collective-permute-done | bytes 589856 | tf_op jit(solution)/shard_map/ppermute | solution.py:419
  153.2 1.7 up0_step3.1
  155.0 1.7 last1_step2.1
  156.7 5.3 %collective-permute-done.19.refs_4_.refs_10_.refs_11_ = f32[104,768]{1,0:T(8,128)S(1)} collective-permute-done((f32[104,768]{1,0:T(8,128)S(1)}, f32[104,768]{1,0:T(8,128)S(1)}, u32[]{:S(2)}, u32[]{:S(2)}) %collective-permute-start.19) | collective-permute-done | bytes 319520 | tf_op jit(solution)/shard_map/ppermute | solution.py:419
  162.0 1.6 last0_step3.1
  163.7 8.5 %collective-permute-done.24.refs_5_ = f32[48,1536]{1,0:T(8,128)S(1)} collective-permute-done((f32[48,1536]{1,0:T(8,128)S(1)}, f32[48,1536]{1,0:T(8,128)S(1)}, u32[]{:S(2)}, u32[]{:S(2)}) %collective-permute-start.24) | collective-permute-done | bytes 294944 | tf_op jit(solution)/shard_map/ppermute | solution.py:419
  172.2 2.4 %up0_last.1 = (f32[48,1536]{1,0:T(8,128)}, f32[8,128]{1,0:T(8,128)S(1)}) custom-call(s32[5]{0:T(128)S(1)} %stack.44.refs_0_, f32[384,1536]{1,0:T(8,128)} %get-tuple-element.161.refs_1_, f32[384,1536]{1,0:T(8,128)} %get-tuple-element.259.refs_2_, f32[192,1536]{1,0:T(8,128)S(1)} %collective-permute-done.18.refs_3_, ...), custom_call_target="tpu_custom_call" | custom-call | flops 2147483648 | bytes 1 | tf_op jit(solution)/shard_map/up0_last/pallas_call | solution.py:70
  174.6 1.6 last1_step3.1
  177.0 1.6 last0_last.1
  180.5 2.2 %output.1 = (bf16[2,258,768]{2,1,0:T(8,128)(2,1)S(1)}, f32[8,128]{1,0:T(8,128)S(1)}) custom-call(f32[528,768]{1,0:T(8,128)} %get-tuple-element.168.refs_0_, f32[528,768]{1,0:T(8,128)} %collective-permute-done.12.refs_1_, f32[768]{0:T(1024)} %refs_2_.5, f32[258,768]{1,0:T(8,128)S(1)} %copy-done.4, f32[258,768]{1,0:T(8,128)S(1)} %copy-done.3, ...), custom_call_target="tpu_custom_call" | custom-call | flops 2147483648 | bytes 1 | tf_op jit(solution)/shard_map/output/pallas_call | solution.py:70
  182.7 1.6 last1_last.1
  (83 shorter events, 21.0 us)
Async XLA Ops:
  2.5 19.1 %collective-permute-start.6 = (f32[192,768]{1,0:T(8,128)}, f32[192,768]{1,0:T(8,128)}, u32[]{:S(2)}, u32[]{:S(2)}) collective-permute-start(f32[192,768]{1,0:T(8,128)} %dynamic-slice_convert_fusion), channel_id=1, source_target_pairs={{0,1},{1,0},{2,3},{3,2},{4,5},{5,4},{6,7},{7,6},{8,9},{9,8},{10,11... | collective-permute-start | bytes 1769480 | tf_op jit(solution)/shard_map/ppermute | solution.py:531
  5.5 18.6 %copy-start.2 = (bf16[384,768]{1,0:T(8,128)(2,1)S(1)}, bf16[384,768]{1,0:T(8,128)(2,1)}, u32[]{:S(2)}) copy-start(bf16[384,768]{1,0:T(8,128)(2,1)} %refs_8_.3) | copy-start | bytes 1769476
  18.1 12.4 %copy-start.5 = (f32[258,384]{1,0:T(8,128)}, f32[258,384]{1,0:T(8,128)S(1)}, u32[]{:S(2)}) copy-start(f32[258,384]{1,0:T(8,128)S(1)} %get-tuple-element.132.refs_7_.refs_3_) | copy-start | bytes 1188868
  18.1 20.8 %copy-start.6 = (f32[258,384]{1,0:T(8,128)}, f32[258,384]{1,0:T(8,128)S(1)}, u32[]{:S(2)}) copy-start(f32[258,384]{1,0:T(8,128)S(1)} %get-tuple-element.137.refs_7_.refs_4_) | copy-start | bytes 1188868
  18.1 12.4 %collective-permute-start.5 = (f32[258,384]{1,0:T(8,128)S(1)}, f32[258,384]{1,0:T(8,128)S(1)}, u32[]{:S(2)}, u32[]{:S(2)}) collective-permute-start(f32[258,384]{1,0:T(8,128)S(1)} %get-tuple-element.132.refs_7_.refs_3_), channel_id=1, source_target_pairs={{0,1},{1,0},{2,3},{3,2},{4,5},{5,4},{6,7},{7,6},{8,9},{9,8},{10,11... | collective-permute-start | bytes 1188872 | tf_op jit(solution)/shard_map/ppermute | solution.py:531
  18.2 20.7 %collective-permute-start.7 = (f32[258,384]{1,0:T(8,128)S(1)}, f32[258,384]{1,0:T(8,128)S(1)}, u32[]{:S(2)}, u32[]{:S(2)}) collective-permute-start(f32[258,384]{1,0:T(8,128)S(1)} %get-tuple-element.137.refs_7_.refs_4_), channel_id=1, source_target_pairs={{0,1},{1,0},{2,3},{3,2},{4,5},{5,4},{6,7},{7,6},{8,9},{9,8},{10,11... | collective-permute-start | bytes 1188872 | tf_op jit(solution)/shard_map/ppermute | solution.py:531
  21.6 2.4 %collective-permute-start = (f32[192,768]{1,0:T(8,128)}, f32[192,768]{1,0:T(8,128)}, u32[]{:S(2)}, u32[]{:S(2)}) collective-permute-start(f32[192,768]{1,0:T(8,128)} %param.1), channel_id=1, source_target_pairs={{0,2},{2,0},{4,6},{6,4},{8,10},{10,8},{12,14},{14,12},{16,18},{18,... | collective-permute-start | bytes 1769480 | tf_op jit(solution)/shard_map/cond/branch_1_fun/ppermute | solution.py:533
  24.0 6.5 %copy-start = (bf16[768,1536]{1,0:T(8,128)(2,1)S(1)}, bf16[768,1536]{1,0:T(8,128)(2,1)}, u32[]{:S(2)}) copy-start(bf16[768,1536]{1,0:T(8,128)(2,1)} %refs_10_.3) | copy-start | bytes 7077892
  24.0 6.5 %copy-start.11 = (bf16[1536,768]{1,0:T(8,128)(2,1)S(1)}, bf16[1536,768]{1,0:T(8,128)(2,1)}, u32[]{:S(2)}) copy-start(bf16[1536,768]{1,0:T(8,128)(2,1)} %refs_11_.3) | copy-start | bytes 7077892
  36.5 25.0 %collective-permute-start.9 = (f32[258,768]{1,0:T(8,128)}, f32[258,768]{1,0:T(8,128)}, u32[]{:S(2)}, u32[]{:S(2)}) collective-permute-start(f32[258,768]{1,0:T(8,128)} %get-tuple-element.147.refs_0_), channel_id=1, source_target_pairs={{0,1},{1,0},{2,3},{3,2},{4,5},{5,4},{6,7},{7,6},{8,9},{9,8},{10,11... | collective-permute-start | bytes 2377736 | tf_op jit(solution)/shard_map/ppermute | solution.py:531
  44.9 6.1 %copy-start.13 = (bf16[258,1536]{1,0:T(8,128)(2,1)S(1)}, bf16[258,1536]{1,0:T(8,128)(2,1)}, u32[]{:S(2)}) copy-start(bf16[258,1536]{1,0:T(8,128)(2,1)} %get-tuple-element.136.refs_3_) | copy-start | bytes 2377732
  45.0 6.1 %copy-start.14 = (bf16[258,1536]{1,0:T(8,128)(2,1)S(1)}, bf16[258,1536]{1,0:T(8,128)(2,1)}, u32[]{:S(2)}) copy-start(bf16[258,1536]{1,0:T(8,128)(2,1)} %get-tuple-element.139.refs_4_) | copy-start | bytes 2377732
  51.2 4.9 %collective-permute-start.1 = (f32[384,1536]{1,0:T(8,128)}, f32[384,1536]{1,0:T(8,128)}, u32[]{:S(2)}, u32[]{:S(2)}) collective-permute-start(f32[384,1536]{1,0:T(8,128)} %get-tuple-element.20), channel_id=1, source_target_pairs={{0,2},{2,0},{4,6},{6,4},{8,10},{10,8},{12,14},{14,12},{16,18},{18,... | collective-permute-start | bytes 7077896 | tf_op jit(solution)/shard_map/cond/branch_1_fun/ppermute | solution.py:478
  56.2 5.3 %copy-start.1 = (bf16[3,768,384]{2,1,0:T(8,128)(2,1)S(1)}, bf16[3,768,384]{2,1,0:T(8,128)(2,1)}, u32[]{:S(2)}) copy-start(bf16[3,768,384]{2,1,0:T(8,128)(2,1)} %refs_9_.3) | copy-start | bytes 5308420
  59.5 39.3 %collective-permute-start.8 = (f32[192,1536]{1,0:T(8,128)}, f32[192,1536]{1,0:T(8,128)}, u32[]{:S(2)}, u32[]{:S(2)}) collective-permute-start(f32[192,1536]{1,0:T(8,128)} %get-tuple-element.146), channel_id=1, source_target_pairs={{0,4},{2,6},{4,0},{6,2},{8,12},{10,14},{12,8},{14,10},{16,20},{18,... | collective-permute-start | bytes 3538952 | tf_op jit(solution)/shard_map/ppermute | solution.py:419
  61.0 26.2 %collective-permute-start.11 = (f32[258,768]{1,0:T(8,128)}, f32[258,768]{1,0:T(8,128)}, u32[]{:S(2)}, u32[]{:S(2)}) collective-permute-start(f32[258,768]{1,0:T(8,128)} %get-tuple-element.153.refs_0_), channel_id=1, source_target_pairs={{0,1},{1,0},{2,3},{3,2},{4,5},{5,4},{6,7},{7,6},{8,9},{9,8},{10,11... | collective-permute-start | bytes 2377736 | tf_op jit(solution)/shard_map/ppermute | solution.py:531
  61.5 10.7 %copy-start.12 = (bf16[2,258,768]{2,1,0:T(8,128)(2,1)S(1)}, bf16[2,258,768]{2,1,0:T(8,128)(2,1)}, u32[]{:S(2)}) copy-start(bf16[2,258,768]{2,1,0:T(8,128)(2,1)} %get-tuple-element.171) | copy-start | bytes 2377732
  70.6 28.1 %collective-permute-start.10 = (f32[258,768]{1,0:T(8,128)}, f32[258,768]{1,0:T(8,128)}, u32[]{:S(2)}, u32[]{:S(2)}) collective-permute-start(f32[258,768]{1,0:T(8,128)} %get-tuple-element.152.refs_2_), channel_id=1, source_target_pairs={{0,1},{1,0},{2,3},{3,2},{4,5},{5,4},{6,7},{7,6},{8,9},{9,8},{10,11... | collective-permute-start | bytes 2377736 | tf_op jit(solution)/shard_map/ppermute | solution.py:531
  79.0 4.9 %collective-permute-start.2 = (f32[384,1536]{1,0:T(8,128)}, f32[384,1536]{1,0:T(8,128)}, u32[]{:S(2)}, u32[]{:S(2)}) collective-permute-start(f32[384,1536]{1,0:T(8,128)} %param.5), channel_id=1, source_target_pairs={{0,2},{2,0},{4,6},{6,4},{8,10},{10,8},{12,14},{14,12},{16,18},{18,... | collective-permute-start | bytes 7077896 | tf_op jit(solution)/shard_map/cond/branch_1_fun/ppermute | solution.py:478
  96.2 14.6 %collective-permute-start.13 = (f32[8,1536]{1,0:T(8,128)S(1)}, f32[8,1536]{1,0:T(8,128)S(1)}, u32[]{:S(2)}, u32[]{:S(2)}) collective-permute-start(f32[8,1536]{1,0:T(8,128)S(1)} %get-tuple-element.178), channel_id=1, source_target_pairs={{0,1},{1,0},{2,3},{3,2},{4,5},{5,4},{6,7},{7,6},{8,9},{9,8},{10,11... | collective-permute-start | bytes 147464 | tf_op jit(solution)/shard_map/ppermute | solution.py:531
  96.7 29.9 %collective-permute-start.18 = (f32[192,1536]{1,0:T(8,128)}, f32[192,1536]{1,0:T(8,128)S(1)}, u32[]{:S(2)}, u32[]{:S(2)}) collective-permute-start(f32[192,1536]{1,0:T(8,128)} %get-tuple-element.195), channel_id=1, source_target_pairs={{0,4},{2,6},{4,0},{6,2},{8,12},{10,14},{12,8},{14,10},{16,20},{18,... | collective-permute-start | bytes 3538952 | tf_op jit(solution)/shard_map/ppermute | solution.py:419
  97.2 34.0 %collective-permute-start.17 = (f32[258,768]{1,0:T(8,128)}, f32[258,768]{1,0:T(8,128)S(1)}, u32[]{:S(2)}, u32[]{:S(2)}) collective-permute-start(f32[258,768]{1,0:T(8,128)} %get-tuple-element.193.refs_2_), channel_id=1, source_target_pairs={{0,1},{1,0},{2,3},{3,2},{4,5},{5,4},{6,7},{7,6},{8,9},{9,8},{10,11... | collective-permute-start | bytes 2377736 | tf_op jit(solution)/shard_map/ppermute | solution.py:531
  98.7 4.5 %copy-start.7 = (f32[8,768]{1,0:T(8,128)S(1)}, f32[8,768]{1,0:T(8,128)}, u32[]{:S(2)}) copy-start(f32[8,768]{1,0:T(8,128)} %get-tuple-element.174.refs_9_) | copy-start | bytes 73732
  98.7 4.5 %copy-start.8 = (f32[8,768]{1,0:T(8,128)S(1)}, f32[8,768]{1,0:T(8,128)}, u32[]{:S(2)}) copy-start(f32[8,768]{1,0:T(8,128)} %get-tuple-element.175.refs_10_) | copy-start | bytes 73732
  98.7 4.5 %copy-start.9 = (f32[8,768]{1,0:T(8,128)S(1)}, f32[8,768]{1,0:T(8,128)}, u32[]{:S(2)}) copy-start(f32[8,768]{1,0:T(8,128)} %get-tuple-element.176.refs_11_) | copy-start | bytes 73732
  98.7 4.5 %copy-start.10 = (f32[8,768]{1,0:T(8,128)S(1)}, f32[8,768]{1,0:T(8,128)}, u32[]{:S(2)}) copy-start(f32[8,768]{1,0:T(8,128)} %get-tuple-element.177.refs_12_) | copy-start | bytes 73732
  101.6 22.5 %collective-permute-start.15 = (f32[96,1536]{1,0:T(8,128)}, f32[96,1536]{1,0:T(8,128)}, u32[]{:S(2)}, u32[]{:S(2)}) collective-permute-start(f32[96,1536]{1,0:T(8,128)} %get-tuple-element.186), channel_id=1, source_target_pairs={{0,8},{2,10},{4,12},{6,14},{8,0},{10,2},{12,4},{14,6},{16,24},{18,... | collective-permute-start | bytes 1769480 | tf_op jit(solution)/shard_map/ppermute | solution.py:419
  110.8 5.1 %collective-permute-start.3 = (f32[392,1536]{1,0:T(8,128)}, f32[392,1536]{1,0:T(8,128)}, u32[]{:S(2)}, u32[]{:S(2)}) collective-permute-start(f32[392,1536]{1,0:T(8,128)} %get-tuple-element.24), channel_id=1, source_target_pairs={{0,2},{2,0},{4,6},{6,4},{8,10},{10,8},{12,14},{14,12},{16,18},{18,... | collective-permute-start | bytes 7225352 | tf_op jit(solution)/shard_map/cond/branch_1_fun/ppermute | solution.py:478
  110.9 4.4 %collective-permute-start.4 = (f32[8,1536]{1,0:T(8,128)S(1)}, f32[8,1536]{1,0:T(8,128)}, u32[]{:S(2)}, u32[]{:S(2)}) collective-permute-start(f32[8,1536]{1,0:T(8,128)S(1)} %get-tuple-element.25), channel_id=1, source_target_pairs={{0,2},{2,0},{4,6},{6,4},{8,10},{10,8},{12,14},{14,12},{16,18},{18,... | collective-permute-start | bytes 147464 | tf_op jit(solution)/shard_map/cond/branch_1_fun/ppermute | solution.py:478
  117.7 26.9 %collective-permute-start.14 = (f32[200,768]{1,0:T(8,128)S(1)}, f32[200,768]{1,0:T(8,128)S(1)}, u32[]{:S(2)}, u32[]{:S(2)}) collective-permute-start(f32[200,768]{1,0:T(8,128)S(1)} %get-tuple-element.185), channel_id=1, source_target_pairs={{0,4},{2,6},{4,0},{6,2},{8,12},{10,14},{12,8},{14,10},{16,20},{18,... | collective-permute-start | bytes 1843208 | tf_op jit(solution)/shard_map/ppermute | solution.py:419
  121.1 33.8 %collective-permute-start.20 = (f32[192,768]{1,0:T(8,128)S(1)}, f32[192,768]{1,0:T(8,128)S(1)}, u32[]{:S(2)}, u32[]{:S(2)}) collective-permute-start(f32[192,768]{1,0:T(8,128)S(1)} %get-tuple-element.201), channel_id=1, source_target_pairs={{0,4},{2,6},{4,0},{6,2},{8,12},{10,14},{12,8},{14,10},{16,20},{18,... | collective-permute-start | bytes 1769480 | tf_op jit(solution)/shard_map/ppermute | solution.py:419
  124.2 56.3 %collective-permute-start.12 = (f32[528,768]{1,0:T(8,128)}, f32[528,768]{1,0:T(8,128)}, u32[]{:S(2)}, u32[]{:S(2)}) collective-permute-start(f32[528,768]{1,0:T(8,128)} %get-tuple-element.168.refs_0_), channel_id=1, source_target_pairs={{0,1},{1,0},{2,3},{3,2},{4,5},{5,4},{6,7},{7,6},{8,9},{9,8},{10,11... | collective-permute-start | bytes 4866056 | tf_op jit(solution)/shard_map/ppermute | solution.py:531
  126.6 15.5 %collective-permute-start.16 = (f32[48,1536]{1,0:T(8,128)S(1)}, f32[48,1536]{1,0:T(8,128)S(1)}, u32[]{:S(2)}, u32[]{:S(2)}) collective-permute-start(f32[48,1536]{1,0:T(8,128)S(1)} %get-tuple-element.192), channel_id=1, source_target_pairs={{0,16},{2,18},{4,20},{6,22},{8,24},{10,26},{12,28},{14,30},{16,0},... | collective-permute-start | bytes 884744 | tf_op jit(solution)/shard_map/ppermute | solution.py:419
  131.1 22.0 %collective-permute-start.21 = (f32[96,1536]{1,0:T(8,128)S(1)}, f32[96,1536]{1,0:T(8,128)S(1)}, u32[]{:S(2)}, u32[]{:S(2)}) collective-permute-start(f32[96,1536]{1,0:T(8,128)S(1)} %get-tuple-element.202), channel_id=1, source_target_pairs={{0,8},{2,10},{4,12},{6,14},{8,0},{10,2},{12,4},{14,6},{16,24},{18,... | collective-permute-start | bytes 1769480 | tf_op jit(solution)/shard_map/ppermute | solution.py:419
  146.3 15.7 %collective-permute-start.19 = (f32[104,768]{1,0:T(8,128)S(1)}, f32[104,768]{1,0:T(8,128)S(1)}, u32[]{:S(2)}, u32[]{:S(2)}) collective-permute-start(f32[104,768]{1,0:T(8,128)S(1)} %get-tuple-element.200), channel_id=1, source_target_pairs={{0,8},{2,10},{4,12},{6,14},{8,0},{10,2},{12,4},{14,6},{16,24},{18,... | collective-permute-start | bytes 958472 | tf_op jit(solution)/shard_map/ppermute | solution.py:419
  154.9 17.3 %collective-permute-start.24 = (f32[48,1536]{1,0:T(8,128)S(1)}, f32[48,1536]{1,0:T(8,128)S(1)}, u32[]{:S(2)}, u32[]{:S(2)}) collective-permute-start(f32[48,1536]{1,0:T(8,128)S(1)} %get-tuple-element.208), channel_id=1, source_target_pairs={{0,16},{2,18},{4,20},{6,22},{8,24},{10,26},{12,28},{14,30},{16,0},... | collective-permute-start | bytes 884744 | tf_op jit(solution)/shard_map/ppermute | solution.py:419
  156.6 18.0 %collective-permute-start.23 = (f32[96,768]{1,0:T(8,128)S(1)}, f32[96,768]{1,0:T(8,128)S(1)}, u32[]{:S(2)}, u32[]{:S(2)}) collective-permute-start(f32[96,768]{1,0:T(8,128)S(1)} %get-tuple-element.207), channel_id=1, source_target_pairs={{0,8},{2,10},{4,12},{6,14},{8,0},{10,2},{12,4},{14,6},{16,24},{18,... | collective-permute-start | bytes 884744 | tf_op jit(solution)/shard_map/ppermute | solution.py:419
  163.6 13.4 %collective-permute-start.22 = (f32[56,768]{1,0:T(8,128)S(1)}, f32[56,768]{1,0:T(8,128)S(1)}, u32[]{:S(2)}, u32[]{:S(2)}) collective-permute-start(f32[56,768]{1,0:T(8,128)S(1)} %get-tuple-element.206), channel_id=1, source_target_pairs={{0,16},{2,18},{4,20},{6,22},{8,24},{10,26},{12,28},{14,30},{16,0},... | collective-permute-start | bytes 516104 | tf_op jit(solution)/shard_map/ppermute | solution.py:419
  176.2 6.6 %collective-permute-start.25 = (f32[48,768]{1,0:T(8,128)S(1)}, f32[48,768]{1,0:T(8,128)S(1)}, u32[]{:S(2)}, u32[]{:S(2)}) collective-permute-start(f32[48,768]{1,0:T(8,128)S(1)} %get-tuple-element.217), channel_id=1, source_target_pairs={{0,16},{2,18},{4,20},{6,22},{8,24},{10,26},{12,28},{14,30},{16,0},... | collective-permute-start | bytes 442376 | tf_op jit(solution)/shard_map/ppermute | solution.py:419
  177.0 3.5 %copy-start.3 = (f32[258,768]{1,0:T(8,128)S(1)}, f32[258,768]{1,0:T(8,128)}, u32[]{:S(2)}) copy-start(f32[258,768]{1,0:T(8,128)} %get-tuple-element.154.refs_2_.refs_4_) | copy-start | bytes 2377732
  177.0 3.5 %copy-start.4 = (f32[258,768]{1,0:T(8,128)S(1)}, f32[258,768]{1,0:T(8,128)}, u32[]{:S(2)}) copy-start(f32[258,768]{1,0:T(8,128)} %get-tuple-element.148.refs_2_.refs_3_) | copy-start | bytes 2377732

commit v2 on v1

--- a/solution.py
+++ b/solution.py
@@ -65,7 +65,7 @@
 ANYWHERE = pl.BlockSpec(memory_space=pl.ANY)
 
 
-def kernel(body, args, specs, outs, vmem, name, grid=1, out_specs=None, scratch=(), deep=(), scalar=0):
+def kernel(body, args, specs, outs, vmem, name, grid=1, out_specs=None, scratch=(), deep=(), scalar=0, cost=31):
     args = [pltpu.with_memory_space_constraint(a, pltpu.HBM) if i in deep else a for i, a in enumerate(args)]
     return pl.pallas_call(
         body,
@@ -78,7 +78,7 @@
             scratch_shapes=list(scratch),
         ),
         compiler_params=pltpu.CompilerParams(vmem_limit_bytes=vmem * MIB),
-        cost_estimate=pl.CostEstimate(flops=1 << 31, bytes_accessed=1, transcendentals=0),
+        cost_estimate=pl.CostEstimate(flops=1 << cost, bytes_accessed=1, transcendentals=0),
         name=name,
     )(*args)
 
@@ -115,10 +115,10 @@
     return vector[...].reshape(1, -1)
 
 
-def side_masks():
+def side_masks(value=1.0):
     lane = lax.broadcasted_iota(jnp.int32, (1, PAIR), 1)
-    low = jnp.where(lane < HEAD_DIM, 1.0, 0.0)
-    return low.astype(BF16), (1.0 - low).astype(BF16)
+    low = jnp.where(lane < HEAD_DIM, value, 0.0)
+    return low.astype(BF16), (value - low).astype(BF16)
 
 
 def attend_body(images, pick, patch, extra, weight, gain, shift, *refs):
@@ -137,7 +137,7 @@
     first_out[...] = first
     for j in range(3):
         qkv_out[:, j * inner : (j + 1) * inner] = mm(first, weight[j]).astype(BF16)
-    masks = side_masks()
+    masks = side_masks(HEAD_DIM**-0.5)
     lane = lax.broadcasted_iota(jnp.int32, (rows, PAIR), 1)
     logs = jnp.zeros((rows, PAIR), F32)
     for pair in range(inner // PAIR):
@@ -146,11 +146,11 @@
         v = qkv_out[:, 2 * inner + pair * PAIR : 2 * inner + (pair + 1) * PAIR]
         sides = []
         for side in range(2):
-            scores = mm_nt(q * masks[side], k) * (HEAD_DIM**-0.5)
+            scores = mm_nt(q * masks[side], k)
             top = jnp.max(scores, -1, keepdims=True)
             expo = jnp.exp(scores - top)
             total = jnp.sum(expo, -1, keepdims=True)
-            sides.append(mm((expo / total).astype(BF16), v))
+            sides.append(mm((expo * (1.0 / total)).astype(BF16), v))
             logs = jnp.where(lane == 2 * pair + side, top + jnp.log(total), logs)
         mixed = jnp.where(lane < HEAD_DIM, sides[0], sides[1]).astype(BF16).astype(F32)
         for b, out in enumerate(mixed_outs):
@@ -226,6 +226,7 @@
     small_out[5:6, :] = jnp.sum(attn.astype(F32), 0, keepdims=True)
     mixed = mm_nt(attn, out_weight[...]).astype(BF16)
     masks = side_masks()
+    scaled = side_masks(HEAD_DIM**-0.5)
     lane = lax.broadcasted_iota(jnp.int32, (rows, PAIR), 1)
     scale = HEAD_DIM**-0.5
     for pair in range(inner // PAIR):
@@ -240,7 +241,7 @@
         for side in range(2):
             half = slice(side * HEAD_DIM, (side + 1) * HEAD_DIM)
             head = 2 * pair + side
-            scores = mm_nt(q * masks[side], k) * scale
+            scores = mm_nt(q * scaled[side], k)
             probs = jnp.exp(scores - logs[:, head : head + 1])
             dv.append(mm(dm_t[half, :], probs.astype(BF16)))
             prob_grad = mm_nt(dm * masks[side], v)
@@ -438,13 +439,13 @@
 
 
 def weight_sum(chain, ids, dp, name, chunk, sets, smalls=(), cross=None, beside=None, parts=1, order=(1, 2, 3)):
-    width = sets[0][0][0].shape[1]
+    width = sets[0][0].shape[-1] if not isinstance(sets[0][0], list) else sets[0][0][0].shape[1]
     columns = sum(rights[0].shape[1] for _, rights in sets)
     size = columns // parts
     if not folded(dp):
         products = [sum(mm_tn(left, right.astype(BF16)) for left, right in zip(*pair)) for pair in sets]
         full = jnp.concatenate(products, 1)
-        small = sum(smalls) + cross if smalls else None
+        small = sum(smalls) + lax.ppermute(cross[:, :width], "mp", SWAP) if smalls else None
         pieces = [
             Plain(full[:, i * size : (i + 1) * size], small if i == 0 else None) for i in range(parts)
         ]
@@ -452,14 +453,19 @@
     args, specs, layout, begin = [], [], [], 0
     for lefts, rights in sets:
         steps = rights[0].shape[1] // chunk
-        args += [*lefts, *rights]
-        specs += [whole(v) for v in lefts]
+        if isinstance(lefts, list):
+            args += lefts
+            specs += [whole(v) for v in lefts]
+        else:
+            args += [lefts] * lefts.shape[0]
+            specs += [one_of(lefts, b) for b in range(lefts.shape[0])]
+        args += rights
         for v in rights:
             block = lambda j, begin=begin, steps=steps: (0, jnp.clip(j - begin, 0, steps - 1))
             specs.append(pl.BlockSpec((v.shape[0], chunk), block))
-        layout.append((len(lefts), steps))
+        layout.append((len(rights), steps))
         begin += steps
-    images, rows = len(sets[0][0]), sets[0][0][0].shape[0]
+    images, rows = len(sets[0][1]), sets[0][1][0].shape[0]
     spare = 8 * pl.cdiv(images * (rows % 8), 8)
     depth = images * (rows // 8 * 8) + spare
     dims = (width // 2 + (8 if smalls else 0), columns)
@@ -477,8 +483,11 @@
     )
     swap = lambda v: lax.ppermute(v, "dp", flips(dp, 0))
     if cross is not None:
-        got, distant = chain.at_once(ids, lambda v, c: (swap(v), swap(c)), send, cross)
-        crosses, done = (cross, distant), None
+        pairs = [((d, m), (d ^ 1, m ^ 1)) for d in range(dp) for m in range(2)]
+        corners = [(2 * p[0] + p[1], 2 * q[0] + q[1]) for p, q in pairs]
+        moves = lambda v, c: (swap(v), lax.ppermute(c, "mp", SWAP), lax.ppermute(c, ("dp", "mp"), corners))
+        got, *crosses = chain.at_once(ids, moves, send, cross)
+        done = None
     elif beside:
         got, done = chain.at_once(ids, lambda v: (swap(v), beside()), send)
         crosses = None
@@ -551,13 +560,17 @@
         stacks + flat, 40, "attend", grid=images,
         out_specs=[each(o.shape) for o in stacks] + [whole(o) for o in flat], deep=range(6),
     )
-    mixed_others = [across(m) for m in mixeds]
+    mixed_others = [across(mixeds[0])]
     (distant,) = chain.at_once(ids, core_swap, near)
     (full,) = chain.call(
         join_body, [ids, out_weight, near, distant],
         [scalars(), whole(out_weight), whole(near), whole(distant)],
         [shape((2 * inner, width), BF16)], 16, "join",
     )
+
+    for b in range(1, images):
+        mixeds[b] = chain.hold(mixeds[b])
+        mixed_others.append(across(mixeds[b]))
 
     middles, seconds, hiddens, uppers, norms, smalls, norm_others = [], [], [], [], [], [], []
     for b in every:
@@ -582,8 +595,7 @@
             [shape((padded, width))], 32, "branch",
         )[0]
 
-    dys = [cotangent[b] for b in every]
-    (down_sum,), down_part = weight_sum(chain, ids, dp, "down", 512, [(dys, hiddens)], beside=branch)
+    (down_sum,), down_part = weight_sum(chain, ids, dp, "down", 512, [(cotangent, hiddens)], beside=branch)
     down_sum.step()
 
     grads, attns, backs, firsts_part, crosses, part_others = [], [], [], [], [], []
@@ -597,24 +609,19 @@
             backward_body, args, specs,
             [far((rows, width)), far((rows, width), BF16), far((rows, 3 * inner), BF16),
              shape((rows, width)), far((8, width)), shape((8, hidden_width))],
-            44, f"backward{b}", deep=(2, 3, 4, 5, 7),
+            44, f"backward{b}", deep=(2, 3, 4, 5, 7), cost=33,
         )
         for kept, one in zip((grads, attns, backs, firsts_part, smalls, crosses), got):
             kept.append(one)
-        if b == images - 1:
-            cross = across(crosses[-1])
         part_others.append(across(firsts_part[b]))
         if b == 0:
             (up_sum,), _ = weight_sum(chain, ids, dp, "up", 512, [(seconds, uppers)])
             up_sum.step()
     part_others[0] = chain.hold(part_others[0])
     down_sum.step()
-    down_part = chain.hold(down_part)
-    down_other = across(down_part)
-    sets = [(attns, mixeds), ([firsts[b] for b in every], backs)]
+    sets = [(attns, mixeds), (firsts, backs)]
     (out_sum, qkv_sum), _ = weight_sum(
-        chain, ids, dp, "last", 384, sets, [*smalls, crosses[-1][:, :width]],
-        cross if folded(dp) else cross[:, :width], parts=2,
+        chain, ids, dp, "last", 384, sets, [*smalls, crosses[-1][:, :width]], crosses[-1], parts=2,
     )
 
     def input_of(b):
@@ -626,13 +633,15 @@
         )[0]
 
     out_sum.step()
+    down_sum.step()
+    up_sum.step()
     qkv_sum.step()
     input_grads = [input_of(b) for b in range(images - 1)]
-    down_sum.step()
-    up_sum.step()
+    out_sum.step()
     input_grads.append(input_of(images - 1))
+    down_part = chain.hold(down_part)
+    down_other = across(down_part)
     (down_total,) = down_sum.finish()
-    out_sum.step()
     up_sum.step()
     qkv_sum.step()
     out_sum.step()

time: 187 us -> 180 us (0.963)
  waiting for transfers between devices: 47.7 us -> 43.3 us
  local copies, waits for them, and re-layouts: 8.63 us -> 5.65 us
    ppermute x12, waiting for transfers between devices: 27.2 us -> 21.8 us  [step(): lax.ppermute(send, 'dp', flips(self.dp, bit))]
    ppermute x4 -> x3, waiting for transfers between devices: 11.6 us -> 7.18 us  [weight_sum(): swap = lambda v: lax.ppermute(v, 'dp', flips(dp, 0))]
    ppermute x0 -> x2, waiting for transfers between devices: none -> 3 us  [the longest x1 2.85 us: weight_sum(): lax.ppermute(c, 'mp', SWAP)]
    ppermute x9 -> x8, waiting for transfers between devices: 6.53 us -> 9.18 us  [per_device(): across = lambda v: lax.ppermute(v, 'mp', SWAP)]
    squeeze x2 -> x0, local copies, waits for them, and re-layouts: 1.9 us -> none  [the longest x1 0.96 us: per_device(): sets = [(attns, mixeds), ([firsts[b] for b in every], backs)]]
    ppermute x9 -> x8, starting transfers between devices: 9.69 us -> 8.56 us  [per_device(): across = lambda v: lax.ppermute(v, 'mp', SWAP)]
    unnamed x33 -> x55, local copies, waits for them, and re-layouts: 4.73 us -> 3.65 us
  transfers between devices with their start and end apart: 26 -> 26, of which waited for: 12 -> 14; matrix products, arithmetic and copies ran while one was open for 4% -> 2% of each run, Pallas kernels for 56% -> 58%
where the time goes in v2:
time: 180 us; the launch traced here: 179 us
  Pallas kernels  106 us (59%)
  waiting for transfers between devices  43.3 us (24%)
  starting transfers between devices  20.7 us (12%)
  local copies, waits for them, and re-layouts  5.65 us (3%)
  other arithmetic  1.9 us (1%)
    pallas_call x29, Pallas kernels, kernel(): pl.pallas_call(body, out_shape=tuple(outs), grid_spec=pltpu.PrefetchScala...  106 us
    ppermute x12, waiting for transfers between devices, step(): lax.ppermute(send, 'dp', flips(self.dp, bit))  21.8 us
    ppermute x12, starting transfers between devices, step(): lax.ppermute(send, 'dp', flips(self.dp, bit))  10.1 us
    ppermute x8, waiting for transfers between devices, per_device(): across = lambda v: lax.ppermute(v, 'mp', SWAP)  9.18 us
    ppermute x8, starting transfers between devices, per_device(): across = lambda v: lax.ppermute(v, 'mp', SWAP)  8.56 us
    ppermute x3, waiting for transfers between devices, weight_sum(): swap = lambda v: lax.ppermute(v, 'dp', flips(dp, 0))  7.18 us
    unnamed x55, local copies, waits for them, and re-layouts  3.65 us
  transfers between devices with their start and end apart: 26, of which 14 were waited for; matrix products, arithmetic and copies ran while one was open for 2% of the time, Pallas kernels for 58%

profile of v2, /device:TPU:0, one launch (start us, length us, event | category | flops | bytes accessed | tf_op | source)
XLA Modules:
  0.0 178.6 jit_solution(15790372695706576874)
XLA Ops:
  1.7 3.0 %collective-permute-start.7 = (f32[192,768]{1,0:T(8,128)S(1)}, f32[192,768]{1,0:T(8,128)S(1)}, u32[]{:S(2)}, u32[]{:S(2)}) collective-permute-start(f32[192,768]{1,0:T(8,128)S(1)} %dynamic-slice_convert_fusion), channel_id=1, source_target_pairs={{0,1},{1,0},{2,3},{3,2},{4,5},{5,4},{6,7},{7,6},{8,9},{9,8},{10,11... | collective-permute-start | bytes 1769480 | tf_op jit(solution)/shard_map/ppermute | solution.py:540
  4.7 12.6 %attend.1 = (f32[2,258,768]{2,1,0:T(8,128)}, bf16[2,258,768]{2,1,0:T(8,128)(2,1)}, bf16[2,258,1152]{2,1,0:T(8,128)(2,1)}, f32[2,258,128]{2,1,0:T(8,128)}, f32[25...) custom-call(s32[2,256]{1,0:T(2,128)} %refs_0_.3, bf16[2,1024,768]{2,1,0:T(8,128)(2,1)} %refs_1_.3, ...), custom_call_target="tpu_custom_call" | custom-call | flops 2147483648 | bytes 1 | tf_op jit(solution)/shard_map/attend/pallas_call | solution.py:70
  18.0 2.1 %conditional.4 = (f32[192,768]{1,0:T(8,128)}) conditional(s32[]{:T(128)} %bitcast.5, () %tuple.40, f32[192,768]{1,0:T(8,128)S(1)} %collective-permute-done.7.refs_2_), branch_computations={%region_0.1_spmd, %region_1.2_spmd} | conditional | bytes 2359344 | solution.py:110
  18.0 2.1 %collective-permute-done = f32[192,768]{1,0:T(8,128)} collective-permute-done((f32[192,768]{1,0:T(8,128)S(1)}, f32[192,768]{1,0:T(8,128)}, u32[]{:S(2)}, u32[]{:S(2)}) %collective-permute-start) | collective-permute-done | bytes 589856 | tf_op jit(solution)/shard_map/cond/branch_1_fun/ppermute | solution.py:542
  21.5 1.8 %collective-permute-start.8 = (f32[258,384]{1,0:T(8,128)S(1)}, f32[258,384]{1,0:T(8,128)S(1)}, u32[]{:S(2)}, u32[]{:S(2)}) collective-permute-start(f32[258,384]{1,0:T(8,128)S(1)} %get-tuple-element.142.refs_7_.refs_4_), channel_id=1, source_target_pairs={{0,1},{1,0},{2,3},{3,2},{4,5},{5,4},{6,7},{7,6},{8,9},{9,8},{10,11... | collective-permute-start | bytes 1188872 | tf_op jit(solution)/shard_map/ppermute | solution.py:540
  23.4 6.3 %collective-permute-done.6.refs_8_ = f32[258,384]{1,0:T(8,128)S(1)} collective-permute-done((f32[258,384]{1,0:T(8,128)S(1)}, f32[258,384]{1,0:T(8,128)S(1)}, u32[]{:S(2)}, u32[]{:S(2)}) %collective-permute-start.6) | collective-permute-done | bytes 396320 | tf_op jit(solution)/shard_map/ppermute | solution.py:540
  29.7 6.0 %forward0.1 = (f32[258,768]{1,0:T(8,128)}, bf16[258,768]{1,0:T(8,128)(2,1)}, bf16[258,1536]{1,0:T(8,128)(2,1)}, bf16[258,1536]{1,0:T(8,128)(2,1)}, f32[258,768]{...) custom-call(s32[5]{0:T(128)S(1)} %stack.44.refs_0_, f32[2,258,768]{2,1,0:T(8,128)} %get-tuple-element.134.refs_1_.refs_5_, ...), custom_call_target="tpu_custom_call" | custom-call | flops 2147483648 | bytes 1 | tf_op jit(solution)/shard_map/forward0/pallas_call | solution.py:70
  35.7 2.4 %collective-permute-done.8.refs_8_ = f32[258,384]{1,0:T(8,128)S(1)} collective-permute-done((f32[258,384]{1,0:T(8,128)S(1)}, f32[258,384]{1,0:T(8,128)S(1)}, u32[]{:S(2)}, u32[]{:S(2)}) %collective-permute-start.8) | collective-permute-done | bytes 396320 | tf_op jit(solution)/shard_map/ppermute | solution.py:540
  38.1 6.0 %forward1.1 = (f32[258,768]{1,0:T(8,128)}, bf16[258,768]{1,0:T(8,128)(2,1)}, bf16[258,1536]{1,0:T(8,128)(2,1)}, bf16[258,1536]{1,0:T(8,128)(2,1)}, f32[258,768]{...) custom-call(s32[5]{0:T(128)S(1)} %stack.44.refs_0_, f32[2,258,768]{2,1,0:T(8,128)} %get-tuple-element.134.refs_1_.refs_5_, ...), custom_call_target="tpu_custom_call" | custom-call | flops 2147483648 | bytes 1 | tf_op jit(solution)/shard_map/forward1/pallas_call | solution.py:70
  44.1 6.1 %down_grads.1 = (f32[384,1536]{1,0:T(8,128)}, f32[384,1536]{1,0:T(8,128)}, f32[8,128]{1,0:T(8,128)S(1)}) custom-call(s32[5]{0:T(128)S(1)} %stack.44.refs_0_, bf16[2,258,768]{2,1,0:T(8,128)(2,1)} %copy-done.1, bf16[2,258,768]{2,1,0:T(8,128)(2,1)} %copy-done.1, bf16[258,1536]{1,0:T(8,128)(2,1)} %get-tuple-element.141.refs_3_, ...), custom_call_target="tpu_custom_call" | custom-call | flops 2147483648 | bytes 1 | tf_op jit(solution)/shard_map/down_grads/pallas_call | solution.py:70
  50.3 5.1 %conditional.5 = (f32[384,1536]{1,0:T(8,128)}, f32[528,768]{1,0:T(8,128)}) conditional(s32[]{:T(128)} %bitcast.5, () %tuple.39, (f32[384,1536]{1,0:T(8,128)}, bf16[258,1536]{1,0:T(8,128)(2,1)S(1)}, bf16[258,1536]{1,0:T(8,128)(2,1)S(1)}, bf16[1536,768]{1,0:T(8,128)(2,1)S(1)}) %tuple.67), branch_computations={%region_2.3_spmd, %region_3.4_spmd} | conditional | flops 2147483648 | bytes 9437241 | solution.py:110
  50.5 2.6 %branch.1 = f32[528,768]{1,0:T(8,128)} custom-call(bf16[258,1536]{1,0:T(8,128)(2,1)S(1)} %get-tuple-element.21.refs_0_, bf16[258,1536]{1,0:T(8,128)(2,1)S(1)} %get-tuple-element.22.refs_1_, bf16[1536,768]{1,0:T(8,128)(2,1)S(1)} %get-tuple-element.23.refs_2_), custom_call_target="tpu_custom_call" | custom-call | flops 2147483648 | bytes 1 | tf_op jit(solution)/shard_map/cond/branch_1_fun/branch/pallas_call | solution.py:70
  53.2 2.2 %collective-permute-done.1 = f32[384,1536]{1,0:T(8,128)} collective-permute-done((f32[384,1536]{1,0:T(8,128)}, f32[384,1536]{1,0:T(8,128)}, u32[]{:S(2)}, u32[]{:S(2)}) %collective-permute-start.1) | collective-permute-done | bytes 2359328 | tf_op jit(solution)/shard_map/cond/branch_1_fun/ppermute | solution.py:484
  55.4 3.5 %down0_step1.1 = (f32[192,1536]{1,0:T(8,128)}, f32[8,128]{1,0:T(8,128)S(1)}) custom-call(s32[5]{0:T(128)S(1)} %stack.44.refs_0_, f32[384,1536]{1,0:T(8,128)} %get-tuple-element.154.refs_1_, f32[384,1536]{1,0:T(8,128)} %get-tuple-element.155.refs_2_, f32[8,128]{1,0:T(8,128)S(1)} %get-tuple-element.156.refs_3_), custom_call_target="tpu_custom_call" | custom-call | flops 2147483648 | bytes 1 | tf_op jit(solution)/shard_map/down0_step1/pallas_call | solution.py:70
  58.9 1.7 collective-permute-start.12
  60.7 8.7 %backward0.1 = (f32[258,768]{1,0:T(8,128)}, bf16[258,768]{1,0:T(8,128)(2,1)}, bf16[258,1152]{1,0:T(8,128)(2,1)}, f32[258,768]{1,0:T(8,128)S(1)}, f32[8,768]{1,0:...) custom-call(f32[258,768]{1,0:T(8,128)} %get-tuple-element.152.refs_0_, ...), custom_call_target="tpu_custom_call" | custom-call | flops 8589934592 | bytes 1 | tf_op jit(solution)/shard_map/backward0/pallas_call | solution.py:70
  70.9 5.9 %up_grads.1 = (f32[384,1536]{1,0:T(8,128)}, f32[384,1536]{1,0:T(8,128)}, f32[8,128]{1,0:T(8,128)S(1)}) custom-call(s32[5]{0:T(128)S(1)} %stack.44.refs_0_, bf16[258,768]{1,0:T(8,128)(2,1)} %get-tuple-element.159.refs_1_, bf16[258,768]{1,0:T(8,128)(2,1)} %get-tuple-element.160.refs_2_, bf16[258,1536]{1,0:T(8,128)(2,1)} %get-tuple-element.161.refs_3_, ...), custom_call_target="tpu_custom_call" | custom-call | flops 2147483648 | bytes 1 | tf_op jit(solution)/shard_map/up_grads/pallas_call | solution.py:70
  76.8 4.9 %conditional.6 = (f32[384,1536]{1,0:T(8,128)}) conditional(s32[]{:T(128)} %bitcast.5, () %tuple.43, f32[384,1536]{1,0:T(8,128)} %get-tuple-element.165), branch_computations={%region_4.5_spmd, %region_5.6_spmd} | conditional | bytes 9437232 | solution.py:110
  76.8 4.9 %collective-permute-done.2 = f32[384,1536]{1,0:T(8,128)} collective-permute-done((f32[384,1536]{1,0:T(8,128)}, f32[384,1536]{1,0:T(8,128)}, u32[]{:S(2)}, u32[]{:S(2)}) %collective-permute-start.2) | collective-permute-done | bytes 2359328 | tf_op jit(solution)/shard_map/cond/branch_1_fun/ppermute | solution.py:484
  81.7 3.3 %up0_step1.1 = (f32[192,1536]{1,0:T(8,128)}, f32[8,128]{1,0:T(8,128)S(1)}) custom-call(s32[5]{0:T(128)S(1)} %stack.44.refs_0_, f32[384,1536]{1,0:T(8,128)} %get-tuple-element.164.refs_1_, f32[384,1536]{1,0:T(8,128)} %get-tuple-element.263.refs_2_, f32[8,128]{1,0:T(8,128)S(1)} %get-tuple-element.166.refs_3_), custom_call_target="tpu_custom_call" | custom-call | flops 2147483648 | bytes 1 | tf_op jit(solution)/shard_map/up0_step1/pallas_call | solution.py:70
  85.6 8.7 %backward1.1 = (f32[258,768]{1,0:T(8,128)}, bf16[258,768]{1,0:T(8,128)(2,1)}, bf16[258,1152]{1,0:T(8,128)(2,1)}, f32[258,768]{1,0:T(8,128)S(1)}, f32[8,768]{1,0:...) custom-call(f32[258,768]{1,0:T(8,128)} %get-tuple-element.148.refs_0_, f32[258,768]{1,0:T(8,128)} %collective-permute-done.9.refs_1_, ...), custom_call_target="tpu_custom_call" | custom-call | flops 8589934592 | bytes 1 | tf_op jit(solution)/shard_map/backward1/pallas_call | solution.py:70
  94.4 2.9 %down0_step2.1 = (f32[96,1536]{1,0:T(8,128)}, f32[8,128]{1,0:T(8,128)S(1)}) custom-call(s32[5]{0:T(128)S(1)} %stack.44.refs_0_, f32[384,1536]{1,0:T(8,128)} %get-tuple-element.154.refs_1_, f32[384,1536]{1,0:T(8,128)} %get-tuple-element.155.refs_2_, f32[192,1536]{1,0:T(8,128)S(1)} %collective-permute-done.12.refs_3_, f32[8,128]{1,0:T(8,128)S(1)} %get-tuple-element.183.refs_4_), custom_call_target="tpu_custom_call" | custom-call | flops 2147483648 | bytes 1 | tf_op jit(solution)/shard_map/down0_step2/pallas_call | solution.py:70
  97.3 1.6 collective-permute-start.16
  98.8 7.5 %last_grads.1 = (f32[392,1536]{1,0:T(8,128)}, f32[392,1536]{1,0:T(8,128)}, f32[8,128]{1,0:T(8,128)S(1)}) custom-call(s32[5]{0:T(128)S(1)} %stack.44.refs_0_, bf16[258,768]{1,0:T(8,128)(2,1)} %get-tuple-element.170.refs_1_, bf16[258,768]{1,0:T(8,128)(2,1)} %get-tuple-element.171.refs_2_, f32[258,384]{1,0:T(8,128)} %copy-done.3, f32[258,384]{1,0:T(8,128)} %copy-done.4, ...), custom_call_target="tpu_custom_call" | custom-call | flops 2147483648 | bytes 1 | tf_op jit(solution)/shard_map/last_grads/pallas_call | solution.py:70
  106.4 5.0 %conditional.7 = (f32[392,1536]{1,0:T(8,128)}, f32[8,1536]{1,0:T(8,128)}, f32[8,1536]{1,0:T(8,128)}) conditional(s32[]{:T(128)} %bitcast.5, () %tuple.45, (f32[392,1536]{1,0:T(8,128)}, f32[8,1536]{1,0:T(8,128)S(1)}) %tuple.46), branch_computations={%region_6.7_spmd, %region_7.8_spmd} | conditional | bytes 10027152 | solution.py:110
  108.3 2.9 %collective-permute-done.4 = f32[8,1536]{1,0:T(8,128)} collective-permute-done((f32[8,1536]{1,0:T(8,128)S(1)}, f32[8,1536]{1,0:T(8,128)}, u32[]{:S(2)}, u32[]{:S(2)}) %collective-permute-start.4) | collective-permute-done | bytes 49184 | tf_op jit(solution)/shard_map/cond/branch_1_fun/ppermute | solution.py:488
  112.4 1.9 %last0_step1.1 = (f32[200,768]{1,0:T(8,128)S(1)}, f32[8,128]{1,0:T(8,128)S(1)}) custom-call(s32[5]{0:T(128)S(1)} %stack.44.refs_0_, f32[392,1536]{1,0:T(8,128)} %get-tuple-element.185.refs_1_.refs_3_.refs_4_.refs_5_.refs_6_, f32[392,1536]{1,0:T(8,128)} %get-tuple-element.187.refs_2_.refs_4_.refs_5_.refs_6_.refs_7_, ...), custom_call_target="tpu_custom_call" | custom-call | flops 2147483648 | bytes 1 | tf_op jit(solution)/shard_map/last0_step1/pallas_call | solution.py:70
  115.8 1.7 down0_step3.1
  117.5 2.6 %collective-permute-start.21 = (f32[48,1536]{1,0:T(8,128)S(1)}, f32[48,1536]{1,0:T(8,128)S(1)}, u32[]{:S(2)}, u32[]{:S(2)}) collective-permute-start(f32[48,1536]{1,0:T(8,128)S(1)} %get-tuple-element.207), channel_id=1, source_target_pairs={{0,16},{2,18},{4,20},{6,22},{8,24},{10,26},{12,28},{14,30},{16,0},... | collective-permute-start | bytes 884744 | tf_op jit(solution)/shard_map/ppermute | solution.py:420
  120.2 2.1 %up0_step2.1 = (f32[96,1536]{1,0:T(8,128)S(1)}, f32[8,128]{1,0:T(8,128)S(1)}) custom-call(s32[5]{0:T(128)S(1)} %stack.44.refs_0_, f32[384,1536]{1,0:T(8,128)} %get-tuple-element.164.refs_1_, f32[384,1536]{1,0:T(8,128)} %get-tuple-element.263.refs_2_, f32[192,1536]{1,0:T(8,128)} %collective-permute-done.15.refs_3_, f32[8,128]{1,0:T(8,128)S(1)} %get-tuple-element.197.refs_4_), custom_call_target="tpu_custom_call" | custom-call | flops 2147483648 | bytes 1 | tf_op jit(solution)/shard_map/up0_step2/pallas_call | solution.py:70
  122.8 1.9 %last1_step1.1 = (f32[192,768]{1,0:T(8,128)S(1)}, f32[8,128]{1,0:T(8,128)S(1)}) custom-call(s32[5]{0:T(128)S(1)} %stack.44.refs_0_, f32[392,1536]{1,0:T(8,128)} %get-tuple-element.185.refs_1_.refs_3_.refs_4_.refs_5_.refs_6_, f32[392,1536]{1,0:T(8,128)} %get-tuple-element.187.refs_2_.refs_4_.refs_5_.refs_6_.refs_7_, f32[8,128]{1,0:T(8,128)S(1)} %get-tuple-element.198.refs_3_), custom_call_target="tpu_custom_call" | custom-call | flops 2147483648 | bytes 1 | tf_op jit(solution)/shard_map/last1_step1/pallas_call | solution.py:70
  125.2 2.2 %input0.1 = (f32[258,768]{1,0:T(8,128)S(1)}, f32[8,128]{1,0:T(8,128)S(1)}) custom-call(f32[768]{0:T(1024)} %refs_0_.5, f32[2,258,768]{2,1,0:T(8,128)} %get-tuple-element.134.refs_1_.refs_5_, f32[258,768]{1,0:T(8,128)S(1)} %get-tuple-element.181.refs_2_, f32[258,768]{1,0:T(8,128)} %collective-permute-done.13.refs_3_, f32[258,768]{1,0:T(8,128)} %get-tuple-element.193.refs_4_, ...), custom_call_target="tpu_custom_call" | custom-call | flops 2147483648 | bytes 1 | tf_op jit(solution)/shard_map/input0/pallas_call | solution.py:70
  127.4 3.6 %collective-permute-done.14.refs_3_.refs_8_.refs_9_.refs_10_ = f32[200,768]{1,0:T(8,128)S(1)} collective-permute-done((f32[200,768]{1,0:T(8,128)S(1)}, f32[200,768]{1,0:T(8,128)S(1)}, u32[]{:S(2)}, u32[]{:S(2)}) %collective-permute-start.14) | collective-permute-done | bytes 614432 | tf_op jit(solution)/shard_map/ppermute | solution.py:420
  131.0 1.7 last0_step2.1
  132.7 1.9 %input1.1 = (f32[258,768]{1,0:T(8,128)S(1)}, f32[8,128]{1,0:T(8,128)S(1)}) custom-call(f32[768]{0:T(1024)} %refs_0_.5, f32[2,258,768]{2,1,0:T(8,128)} %get-tuple-element.134.refs_1_.refs_5_, f32[258,768]{1,0:T(8,128)S(1)} %copy-done.13, f32[258,768]{1,0:T(8,128)S(1)} %collective-permute-done.11.refs_3_, f32[258,768]{1,0:T(8,128)} %get-tuple-element.169.refs_4_, ...), custom_call_target="tpu_custom_call" | custom-call | flops 2147483648 | bytes 1 | tf_op jit(solution)/shard_map/input1/pallas_call | solution.py:70
  136.4 2.0 %copy.35 = f32[2,258,768]{2,0,1:T(2,128)} copy(f32[2,258,768]{2,1,0:T(8,128)S(1)} %pad_maximum_fusion) | data formatting | bytes 3170304
  138.4 2.5 %down0_last.1 = (f32[48,1536]{1,0:T(8,128)}, f32[8,128]{1,0:T(8,128)S(1)}) custom-call(s32[5]{0:T(128)S(1)} %stack.44.refs_0_, f32[384,1536]{1,0:T(8,128)} %get-tuple-element.154.refs_1_, f32[384,1536]{1,0:T(8,128)} %get-tuple-element.155.refs_2_, f32[192,1536]{1,0:T(8,128)S(1)} %copy-done.9, f32[96,1536]{1,0:T(8,128)} %collective-permute-done.16.refs_4_, ...), custom_call_target="tpu_custom_call" | custom-call | flops 2147483648 | bytes 1 | tf_op jit(solution)/shard_map/down0_last/pallas_call | solution.py:70
  140.9 3.9 %collective-permute-done.20.refs_4_ = f32[96,1536]{1,0:T(8,128)S(1)} collective-permute-done((f32[96,1536]{1,0:T(8,128)S(1)}, f32[96,1536]{1,0:T(8,128)S(1)}, u32[]{:S(2)}, u32[]{:S(2)}) %collective-permute-start.20) | collective-permute-done | bytes 589856 | tf_op jit(solution)/shard_map/ppermute | solution.py:420
  144.8 1.8 up0_step3.1
  146.6 1.7 last1_step2.1
  148.6 4.6 %collective-permute-done.18.refs_4_.refs_10_.refs_11_ = f32[104,768]{1,0:T(8,128)S(1)} collective-permute-done((f32[104,768]{1,0:T(8,128)S(1)}, f32[104,768]{1,0:T(8,128)S(1)}, u32[]{:S(2)}, u32[]{:S(2)}) %collective-permute-start.18) | collective-permute-done | bytes 319520 | tf_op jit(solution)/shard_map/ppermute | solution.py:420
  153.2 1.6 last0_step3.1
  154.9 8.8 %collective-permute-done.24.refs_5_ = f32[48,1536]{1,0:T(8,128)S(1)} collective-permute-done((f32[48,1536]{1,0:T(8,128)S(1)}, f32[48,1536]{1,0:T(8,128)S(1)}, u32[]{:S(2)}, u32[]{:S(2)}) %collective-permute-start.24) | collective-permute-done | bytes 294944 | tf_op jit(solution)/shard_map/ppermute | solution.py:420
  163.6 2.5 %up0_last.1 = (f32[48,1536]{1,0:T(8,128)}, f32[8,128]{1,0:T(8,128)S(1)}) custom-call(s32[5]{0:T(128)S(1)} %stack.44.refs_0_, f32[384,1536]{1,0:T(8,128)} %get-tuple-element.164.refs_1_, f32[384,1536]{1,0:T(8,128)} %get-tuple-element.263.refs_2_, f32[192,1536]{1,0:T(8,128)} %collective-permute-done.15.refs_3_, ...), custom_call_target="tpu_custom_call" | custom-call | flops 2147483648 | bytes 1 | tf_op jit(solution)/shard_map/up0_last/pallas_call | solution.py:70
  166.2 2.2 %last1_step3.1 = (f32[48,768]{1,0:T(8,128)}, f32[8,128]{1,0:T(8,128)S(1)}) custom-call(s32[5]{0:T(128)S(1)} %stack.44.refs_0_, f32[392,1536]{1,0:T(8,128)} %get-tuple-element.185.refs_1_.refs_3_.refs_4_.refs_5_.refs_6_, f32[392,1536]{1,0:T(8,128)} %get-tuple-element.187.refs_2_.refs_4_.refs_5_.refs_6_.refs_7_, ...), custom_call_target="tpu_custom_call" | custom-call | flops 2147483648 | bytes 1 | tf_op jit(solution)/shard_map/last1_step3/pallas_call | solution.py:70
  168.4 1.6 last0_last.1
  172.0 1.9 %output.1 = (bf16[2,258,768]{2,1,0:T(8,128)(2,1)S(1)}, f32[8,128]{1,0:T(8,128)S(1)}) custom-call(f32[528,768]{1,0:T(8,128)} %get-tuple-element.203.refs_0_, f32[528,768]{1,0:T(8,128)S(1)} %collective-permute-done.17.refs_1_, f32[768]{0:T(1024)} %refs_2_.6, f32[258,768]{1,0:T(8,128)S(1)} %copy-done.10, f32[258,768]{1,0:T(8,128)S(1)} %copy-done.11, ...), custom_call_target="tpu_custom_call" | custom-call | flops 2147483648 | bytes 1 | tf_op jit(solution)/shard_map/output/pallas_call | solution.py:70
  174.8 1.7 last1_last.1
  (103 shorter events, 18.4 us)
Async XLA Ops:
  1.7 16.4 %collective-permute-start.7 = (f32[192,768]{1,0:T(8,128)S(1)}, f32[192,768]{1,0:T(8,128)S(1)}, u32[]{:S(2)}, u32[]{:S(2)}) collective-permute-start(f32[192,768]{1,0:T(8,128)S(1)} %dynamic-slice_convert_fusion), channel_id=1, source_target_pairs={{0,1},{1,0},{2,3},{3,2},{4,5},{5,4},{6,7},{7,6},{8,9},{9,8},{10,11... | collective-permute-start | bytes 1769480 | tf_op jit(solution)/shard_map/ppermute | solution.py:540
  4.7 15.5 %copy-start.5 = (bf16[384,768]{1,0:T(8,128)(2,1)S(1)}, bf16[384,768]{1,0:T(8,128)(2,1)}, u32[]{:S(2)}) copy-start(bf16[384,768]{1,0:T(8,128)(2,1)} %refs_8_.3) | copy-start | bytes 1769476
  17.3 12.4 %copy-start.3 = (f32[258,384]{1,0:T(8,128)}, f32[258,384]{1,0:T(8,128)S(1)}, u32[]{:S(2)}) copy-start(f32[258,384]{1,0:T(8,128)S(1)} %get-tuple-element.135.refs_7_.refs_3_) | copy-start | bytes 1188868
  17.3 20.8 %copy-start.4 = (f32[258,384]{1,0:T(8,128)}, f32[258,384]{1,0:T(8,128)S(1)}, u32[]{:S(2)}) copy-start(f32[258,384]{1,0:T(8,128)S(1)} %get-tuple-element.142.refs_7_.refs_4_) | copy-start | bytes 1188868
  17.3 12.4 %collective-permute-start.6 = (f32[258,384]{1,0:T(8,128)S(1)}, f32[258,384]{1,0:T(8,128)S(1)}, u32[]{:S(2)}, u32[]{:S(2)}) collective-permute-start(f32[258,384]{1,0:T(8,128)S(1)} %get-tuple-element.135.refs_7_.refs_3_), channel_id=1, source_target_pairs={{0,1},{1,0},{2,3},{3,2},{4,5},{5,4},{6,7},{7,6},{8,9},{9,8},{10,11... | collective-permute-start | bytes 1188872 | tf_op jit(solution)/shard_map/ppermute | solution.py:540
  18.0 2.1 %collective-permute-start = (f32[192,768]{1,0:T(8,128)S(1)}, f32[192,768]{1,0:T(8,128)}, u32[]{:S(2)}, u32[]{:S(2)}) collective-permute-start(f32[192,768]{1,0:T(8,128)S(1)} %param.1), channel_id=1, source_target_pairs={{0,2},{2,0},{4,6},{6,4},{8,10},{10,8},{12,14},{14,12},{16,18},{18,... | collective-permute-start | bytes 1769480 | tf_op jit(solution)/shard_map/cond/branch_1_fun/ppermute | solution.py:542
  20.2 3.2 %copy-start.23 = (bf16[2,258,768]{2,0,1:T(2,128)(2,1)S(1)}, bf16[2,258,768]{2,0,1:T(2,128)(2,1)}, u32[]{:S(2)}) copy-start(bf16[2,258,768]{2,0,1:T(2,128)(2,1)} %param.37) | copy-start | bytes 2377732
  20.2 9.5 %copy-start = (bf16[768,1536]{1,0:T(8,128)(2,1)S(1)}, bf16[768,1536]{1,0:T(8,128)(2,1)}, u32[]{:S(2)}) copy-start(bf16[768,1536]{1,0:T(8,128)(2,1)} %refs_10_.3) | copy-start | bytes 7077892
  20.2 9.5 %copy-start.22 = (bf16[1536,768]{1,0:T(8,128)(2,1)S(1)}, bf16[1536,768]{1,0:T(8,128)(2,1)}, u32[]{:S(2)}) copy-start(bf16[1536,768]{1,0:T(8,128)(2,1)} %refs_11_.3) | copy-start | bytes 7077892
  21.5 16.6 %collective-permute-start.8 = (f32[258,384]{1,0:T(8,128)S(1)}, f32[258,384]{1,0:T(8,128)S(1)}, u32[]{:S(2)}, u32[]{:S(2)}) collective-permute-start(f32[258,384]{1,0:T(8,128)S(1)} %get-tuple-element.142.refs_7_.refs_4_), channel_id=1, source_target_pairs={{0,1},{1,0},{2,3},{3,2},{4,5},{5,4},{6,7},{7,6},{8,9},{9,8},{10,11... | collective-permute-start | bytes 1188872 | tf_op jit(solution)/shard_map/ppermute | solution.py:540
  23.4 14.7 %copy-start.1 = (bf16[2,258,768]{2,1,0:T(8,128)(2,1)}, bf16[2,258,768]{2,1,0:T(8,128)(2,1)S(1)}, u32[]{:S(2)}) copy-start(bf16[2,258,768]{2,1,0:T(8,128)(2,1)S(1)} %copy.30.refs_2_.refs_1_.refs_6_) | copy-start | bytes 2377732
  35.7 25.0 %collective-permute-start.10 = (f32[258,768]{1,0:T(8,128)}, f32[258,768]{1,0:T(8,128)}, u32[]{:S(2)}, u32[]{:S(2)}) collective-permute-start(f32[258,768]{1,0:T(8,128)} %get-tuple-element.152.refs_0_), channel_id=1, source_target_pairs={{0,1},{1,0},{2,3},{3,2},{4,5},{5,4},{6,7},{7,6},{8,9},{9,8},{10,11... | collective-permute-start | bytes 2377736 | tf_op jit(solution)/shard_map/ppermute | solution.py:540
  44.1 6.1 %copy-start.24 = (bf16[258,1536]{1,0:T(8,128)(2,1)S(1)}, bf16[258,1536]{1,0:T(8,128)(2,1)}, u32[]{:S(2)}) copy-start(bf16[258,1536]{1,0:T(8,128)(2,1)} %get-tuple-element.141.refs_3_) | copy-start | bytes 2377732
  44.1 6.1 %copy-start.25 = (bf16[258,1536]{1,0:T(8,128)(2,1)S(1)}, bf16[258,1536]{1,0:T(8,128)(2,1)}, u32[]{:S(2)}) copy-start(bf16[258,1536]{1,0:T(8,128)(2,1)} %get-tuple-element.144.refs_4_) | copy-start | bytes 2377732
  50.2 35.4 %collective-permute-start.9 = (f32[258,768]{1,0:T(8,128)}, f32[258,768]{1,0:T(8,128)}, u32[]{:S(2)}, u32[]{:S(2)}) collective-permute-start(f32[258,768]{1,0:T(8,128)} %get-tuple-element.148.refs_0_), channel_id=1, source_target_pairs={{0,1},{1,0},{2,3},{3,2},{4,5},{5,4},{6,7},{7,6},{8,9},{9,8},{10,11... | collective-permute-start | bytes 2377736 | tf_op jit(solution)/shard_map/ppermute | solution.py:540
  50.5 4.9 %collective-permute-start.1 = (f32[384,1536]{1,0:T(8,128)}, f32[384,1536]{1,0:T(8,128)}, u32[]{:S(2)}, u32[]{:S(2)}) collective-permute-start(f32[384,1536]{1,0:T(8,128)} %get-tuple-element.20), channel_id=1, source_target_pairs={{0,2},{2,0},{4,6},{6,4},{8,10},{10,8},{12,14},{14,12},{16,18},{18,... | collective-permute-start | bytes 7077896 | tf_op jit(solution)/shard_map/cond/branch_1_fun/ppermute | solution.py:484
  55.4 5.2 %copy-start.2 = (bf16[2,258,768]{2,1,0:T(8,128)(2,1)S(1)}, bf16[2,258,768]{2,1,0:T(8,128)(2,1)}, u32[]{:S(2)}) copy-start(bf16[2,258,768]{2,1,0:T(8,128)(2,1)} %copy-done.1) | copy-start | bytes 2377732
  55.4 5.2 %copy-start.6 = (bf16[3,768,384]{2,1,0:T(8,128)(2,1)S(1)}, bf16[3,768,384]{2,1,0:T(8,128)(2,1)}, u32[]{:S(2)}) copy-start(bf16[3,768,384]{2,1,0:T(8,128)(2,1)} %refs_9_.3) | copy-start | bytes 5308420
  58.9 35.4 %collective-permute-start.12 = (f32[192,1536]{1,0:T(8,128)}, f32[192,1536]{1,0:T(8,128)S(1)}, u32[]{:S(2)}, u32[]{:S(2)}) collective-permute-start(f32[192,1536]{1,0:T(8,128)} %get-tuple-element.180), channel_id=1, source_target_pairs={{0,4},{2,6},{4,0},{6,2},{8,12},{10,14},{12,8},{14,10},{16,20},{18,... | collective-permute-start | bytes 3538952 | tf_op jit(solution)/shard_map/ppermute | solution.py:420
  69.4 24.9 %collective-permute-start.13 = (f32[258,768]{1,0:T(8,128)S(1)}, f32[258,768]{1,0:T(8,128)}, u32[]{:S(2)}, u32[]{:S(2)}) collective-permute-start(f32[258,768]{1,0:T(8,128)S(1)} %get-tuple-element.181.refs_2_), channel_id=1, source_target_pairs={{0,1},{1,0},{2,3},{3,2},{4,5},{5,4},{6,7},{7,6},{8,9},{9,8},{10,11... | collective-permute-start | bytes 2377736 | tf_op jit(solution)/shard_map/ppermute | solution.py:540
  76.8 4.9 %collective-permute-start.2 = (f32[384,1536]{1,0:T(8,128)}, f32[384,1536]{1,0:T(8,128)}, u32[]{:S(2)}, u32[]{:S(2)}) collective-permute-start(f32[384,1536]{1,0:T(8,128)} %param.5), channel_id=1, source_target_pairs={{0,2},{2,0},{4,6},{6,4},{8,10},{10,8},{12,14},{14,12},{16,18},{18,... | collective-permute-start | bytes 7077896 | tf_op jit(solution)/shard_map/cond/branch_1_fun/ppermute | solution.py:484
  81.7 3.9 %copy-start.7 = (bf16[3,768,384]{2,1,0:T(8,128)(2,1)S(1)}, bf16[3,768,384]{2,1,0:T(8,128)(2,1)}, u32[]{:S(2)}) copy-start(bf16[3,768,384]{2,1,0:T(8,128)(2,1)} %refs_9_.3) | copy-start | bytes 5308420
  85.0 35.2 %collective-permute-start.15 = (f32[192,1536]{1,0:T(8,128)}, f32[192,1536]{1,0:T(8,128)}, u32[]{:S(2)}, u32[]{:S(2)}) collective-permute-start(f32[192,1536]{1,0:T(8,128)} %get-tuple-element.194), channel_id=1, source_target_pairs={{0,4},{2,6},{4,0},{6,2},{8,12},{10,14},{12,8},{14,10},{16,20},{18,... | collective-permute-start | bytes 3538952 | tf_op jit(solution)/shard_map/ppermute | solution.py:420
  94.3 2.9 %copy-start.12 = (f32[258,768]{1,0:T(8,128)}, f32[258,768]{1,0:T(8,128)S(1)}, u32[]{:S(2)}) copy-start(f32[258,768]{1,0:T(8,128)S(1)} %get-tuple-element.168.refs_2_) | copy-start | bytes 2377732
  94.3 4.5 %copy-start.18 = (f32[8,768]{1,0:T(8,128)S(1)}, f32[8,768]{1,0:T(8,128)}, u32[]{:S(2)}) copy-start(f32[8,768]{1,0:T(8,128)} %get-tuple-element.175.refs_9_) | copy-start | bytes 73732
  94.3 4.5 %copy-start.19 = (f32[8,768]{1,0:T(8,128)S(1)}, f32[8,768]{1,0:T(8,128)}, u32[]{:S(2)}) copy-start(f32[8,768]{1,0:T(8,128)} %get-tuple-element.176.refs_10_) | copy-start | bytes 73732
  94.3 4.5 %copy-start.20 = (f32[8,768]{1,0:T(8,128)S(1)}, f32[8,768]{1,0:T(8,128)}, u32[]{:S(2)}) copy-start(f32[8,768]{1,0:T(8,128)} %get-tuple-element.177.refs_11_) | copy-start | bytes 73732
  94.4 4.5 %copy-start.21 = (f32[8,768]{1,0:T(8,128)S(1)}, f32[8,768]{1,0:T(8,128)}, u32[]{:S(2)}) copy-start(f32[8,768]{1,0:T(8,128)} %get-tuple-element.178.refs_12_) | copy-start | bytes 73732
  94.4 21.4 %copy-start.8 = (f32[192,1536]{1,0:T(8,128)}, f32[192,1536]{1,0:T(8,128)S(1)}, u32[]{:S(2)}) copy-start(f32[192,1536]{1,0:T(8,128)S(1)} %collective-permute-done.12.refs_3_) | copy-start | bytes 3538948
  97.3 18.5 %collective-permute-start.16 = (f32[96,1536]{1,0:T(8,128)}, f32[96,1536]{1,0:T(8,128)}, u32[]{:S(2)}, u32[]{:S(2)}) collective-permute-start(f32[96,1536]{1,0:T(8,128)} %get-tuple-element.195), channel_id=1, source_target_pairs={{0,8},{2,10},{4,12},{6,14},{8,0},{10,2},{12,4},{14,6},{16,24},{18,... | collective-permute-start | bytes 1769480 | tf_op jit(solution)/shard_map/ppermute | solution.py:420
  106.4 5.0 %copy-start.13 = (f32[258,768]{1,0:T(8,128)S(1)}, f32[258,768]{1,0:T(8,128)}, u32[]{:S(2)}) copy-start(f32[258,768]{1,0:T(8,128)} %copy-done.12) | copy-start | bytes 2377732
  106.4 5.0 %collective-permute-start.3 = (f32[392,1536]{1,0:T(8,128)}, f32[392,1536]{1,0:T(8,128)}, u32[]{:S(2)}, u32[]{:S(2)}) collective-permute-start(f32[392,1536]{1,0:T(8,128)} %get-tuple-element.24), channel_id=1, source_target_pairs={{0,2},{2,0},{4,6},{6,4},{8,10},{10,8},{12,14},{14,12},{16,18},{18,... | collective-permute-start | bytes 7225352 | tf_op jit(solution)/shard_map/cond/branch_1_fun/ppermute | solution.py:484
  106.5 4.7 %collective-permute-start.4 = (f32[8,1536]{1,0:T(8,128)S(1)}, f32[8,1536]{1,0:T(8,128)}, u32[]{:S(2)}, u32[]{:S(2)}) collective-permute-start(f32[8,1536]{1,0:T(8,128)S(1)} %get-tuple-element.25), channel_id=1, source_target_pairs={{0,1},{1,0},{2,3},{3,2},{4,5},{5,4},{6,7},{7,6},{8,9},{9,8},{10,11... | collective-permute-start | bytes 147464 | tf_op jit(solution)/shard_map/cond/branch_1_fun/ppermute | solution.py:488
  107.0 4.3 %collective-permute-start.5 = (f32[8,1536]{1,0:T(8,128)S(1)}, f32[8,1536]{1,0:T(8,128)}, u32[]{:S(2)}, u32[]{:S(2)}) collective-permute-start(f32[8,1536]{1,0:T(8,128)S(1)} %get-tuple-element.25), channel_id=1, source_target_pairs={{0,3},{1,2},{2,1},{3,0},{4,7},{5,6},{6,5},{7,4},{8,11},{9,10},{10,... | collective-permute-start | bytes 147464 | tf_op jit(solution)/shard_map/cond/branch_1_fun/ppermute | solution.py:488
  111.4 21.3 %collective-permute-start.11 = (f32[258,768]{1,0:T(8,128)S(1)}, f32[258,768]{1,0:T(8,128)S(1)}, u32[]{:S(2)}, u32[]{:S(2)}) collective-permute-start(f32[258,768]{1,0:T(8,128)S(1)} %copy-done.13), channel_id=1, source_target_pairs={{0,1},{1,0},{2,3},{3,2},{4,5},{5,4},{6,7},{7,6},{8,9},{9,8},{10,11... | collective-permute-start | bytes 2377736 | tf_op jit(solution)/shard_map/ppermute | solution.py:540
  114.2 16.8 %collective-permute-start.14 = (f32[200,768]{1,0:T(8,128)S(1)}, f32[200,768]{1,0:T(8,128)S(1)}, u32[]{:S(2)}, u32[]{:S(2)}) collective-permute-start(f32[200,768]{1,0:T(8,128)S(1)} %get-tuple-element.191), channel_id=1, source_target_pairs={{0,4},{2,6},{4,0},{6,2},{8,12},{10,14},{12,8},{14,10},{16,20},{18,... | collective-permute-start | bytes 1843208 | tf_op jit(solution)/shard_map/ppermute | solution.py:420
  117.5 20.8 %collective-permute-start.21 = (f32[48,1536]{1,0:T(8,128)S(1)}, f32[48,1536]{1,0:T(8,128)S(1)}, u32[]{:S(2)}, u32[]{:S(2)}) collective-permute-start(f32[48,1536]{1,0:T(8,128)S(1)} %get-tuple-element.207), channel_id=1, source_target_pairs={{0,16},{2,18},{4,20},{6,22},{8,24},{10,26},{12,28},{14,30},{16,0},... | collective-permute-start | bytes 884744 | tf_op jit(solution)/shard_map/ppermute | solution.py:420
  122.2 22.5 %collective-permute-start.20 = (f32[96,1536]{1,0:T(8,128)S(1)}, f32[96,1536]{1,0:T(8,128)S(1)}, u32[]{:S(2)}, u32[]{:S(2)}) collective-permute-start(f32[96,1536]{1,0:T(8,128)S(1)} %get-tuple-element.206), channel_id=1, source_target_pairs={{0,8},{2,10},{4,12},{6,14},{8,0},{10,2},{12,4},{14,6},{16,24},{18,... | collective-permute-start | bytes 1769480 | tf_op jit(solution)/shard_map/ppermute | solution.py:420
  124.6 22.0 %collective-permute-start.19 = (f32[192,768]{1,0:T(8,128)S(1)}, f32[192,768]{1,0:T(8,128)S(1)}, u32[]{:S(2)}, u32[]{:S(2)}) collective-permute-start(f32[192,768]{1,0:T(8,128)S(1)} %get-tuple-element.205), channel_id=1, source_target_pairs={{0,4},{2,6},{4,0},{6,2},{8,12},{10,14},{12,8},{14,10},{16,20},{18,... | collective-permute-start | bytes 1769480 | tf_op jit(solution)/shard_map/ppermute | solution.py:420
  134.6 18.6 %collective-permute-start.18 = (f32[104,768]{1,0:T(8,128)S(1)}, f32[104,768]{1,0:T(8,128)S(1)}, u32[]{:S(2)}, u32[]{:S(2)}) collective-permute-start(f32[104,768]{1,0:T(8,128)S(1)} %get-tuple-element.204), channel_id=1, source_target_pairs={{0,8},{2,10},{4,12},{6,14},{8,0},{10,2},{12,4},{14,6},{16,24},{18,... | collective-permute-start | bytes 958472 | tf_op jit(solution)/shard_map/ppermute | solution.py:420
  135.2 36.8 %collective-permute-start.17 = (f32[528,768]{1,0:T(8,128)}, f32[528,768]{1,0:T(8,128)S(1)}, u32[]{:S(2)}, u32[]{:S(2)}) collective-permute-start(f32[528,768]{1,0:T(8,128)} %get-tuple-element.203.refs_0_), channel_id=1, source_target_pairs={{0,1},{1,0},{2,3},{3,2},{4,5},{5,4},{6,7},{7,6},{8,9},{9,8},{10,11... | collective-permute-start | bytes 4866056 | tf_op jit(solution)/shard_map/ppermute | solution.py:540
  146.5 17.1 %collective-permute-start.24 = (f32[48,1536]{1,0:T(8,128)S(1)}, f32[48,1536]{1,0:T(8,128)S(1)}, u32[]{:S(2)}, u32[]{:S(2)}) collective-permute-start(f32[48,1536]{1,0:T(8,128)S(1)} %get-tuple-element.214), channel_id=1, source_target_pairs={{0,16},{2,18},{4,20},{6,22},{8,24},{10,26},{12,28},{14,30},{16,0},... | collective-permute-start | bytes 884744 | tf_op jit(solution)/shard_map/ppermute | solution.py:420
  146.6 19.5 %copy-start.14 = (f32[192,768]{1,0:T(8,128)}, f32[192,768]{1,0:T(8,128)S(1)}, u32[]{:S(2)}) copy-start(f32[192,768]{1,0:T(8,128)S(1)} %collective-permute-done.19.refs_3_) | copy-start | bytes 1769476
  148.3 17.8 %collective-permute-start.23 = (f32[96,768]{1,0:T(8,128)S(1)}, f32[96,768]{1,0:T(8,128)S(1)}, u32[]{:S(2)}, u32[]{:S(2)}) collective-permute-start(f32[96,768]{1,0:T(8,128)S(1)} %get-tuple-element.213), channel_id=1, source_target_pairs={{0,8},{2,10},{4,12},{6,14},{8,0},{10,2},{12,4},{14,6},{16,24},{18,... | collective-permute-start | bytes 884744 | tf_op jit(solution)/shard_map/ppermute | solution.py:420
  154.8 13.6 %collective-permute-start.22 = (f32[56,768]{1,0:T(8,128)S(1)}, f32[56,768]{1,0:T(8,128)S(1)}, u32[]{:S(2)}, u32[]{:S(2)}) collective-permute-start(f32[56,768]{1,0:T(8,128)S(1)} %get-tuple-element.212), channel_id=1, source_target_pairs={{0,16},{2,18},{4,20},{6,22},{8,24},{10,26},{12,28},{14,30},{16,0},... | collective-permute-start | bytes 516104 | tf_op jit(solution)/shard_map/ppermute | solution.py:420
  168.4 6.4 %collective-permute-start.25 = (f32[48,768]{1,0:T(8,128)}, f32[48,768]{1,0:T(8,128)}, u32[]{:S(2)}, u32[]{:S(2)}) collective-permute-start(f32[48,768]{1,0:T(8,128)} %get-tuple-element.223), channel_id=1, source_target_pairs={{0,16},{2,18},{4,20},{6,22},{8,24},{10,26},{12,28},{14,30},{16,0},... | collective-permute-start | bytes 442376 | tf_op jit(solution)/shard_map/ppermute | solution.py:420
  168.4 3.6 %copy-start.10 = (f32[258,768]{1,0:T(8,128)S(1)}, f32[258,768]{1,0:T(8,128)}, u32[]{:S(2)}) copy-start(f32[258,768]{1,0:T(8,128)} %get-tuple-element.153.refs_2_.refs_3_) | copy-start | bytes 2377732
  168.4 3.6 %copy-start.11 = (f32[258,768]{1,0:T(8,128)S(1)}, f32[258,768]{1,0:T(8,128)}, u32[]{:S(2)}) copy-start(f32[258,768]{1,0:T(8,128)} %get-tuple-element.149.refs_2_.refs_4_) | copy-start | bytes 2377732
  (4 other events, 9.8 us)

commit v3 on v2

--- a/solution.py
+++ b/solution.py
@@ -121,13 +121,11 @@
     return low.astype(BF16), (value - low).astype(BF16)
 
 
-def attend_body(images, pick, patch, extra, weight, gain, shift, *refs):
-    seq_out, first_out, qkv_out, log_out, *mixed_outs = refs
+def attend_body(image, pick, patch, extra, weight, gain, shift, seq_out, first_out, qkv_out, log_out, mixed_out):
     rows, width = seq_out.shape
-    inner = mixed_outs[0].shape[1]
-    image = pl.program_id(0)
+    inner = mixed_out.shape[1]
     extras, picks = extra.shape[1], pick.shape[1]
-    spread = jnp.broadcast_to(pick[pl.ds(image, 1), :].astype(F32), (128, picks))
+    spread = jnp.broadcast_to(pick[image : image + 1, :].astype(F32), (128, picks))
     column = spread.T[:, 0:1].astype(jnp.int32)
     hot = lax.broadcasted_iota(jnp.int32, (picks, patch.shape[0]), 1) == column
     seq_out[extras:, :] = mm(jnp.where(hot, 1.0, 0.0).astype(BF16), patch[...])
@@ -153,23 +151,19 @@
             sides.append(mm((expo * (1.0 / total)).astype(BF16), v))
             logs = jnp.where(lane == 2 * pair + side, top + jnp.log(total), logs)
         mixed = jnp.where(lane < HEAD_DIM, sides[0], sides[1]).astype(BF16).astype(F32)
-        for b, out in enumerate(mixed_outs):
-            @pl.when(image == b)
-            def _(out=out, mixed=mixed, pair=pair):
-                out[:, pair * PAIR : (pair + 1) * PAIR] = mixed
+        mixed_out[:, pair * PAIR : (pair + 1) * PAIR] = mixed
     log_out[...] = logs
 
 
-def join_body(ids, mine, near, far, full_out):
+def join_body(ids, mine, *refs):
+    *quarters, full_out = refs
     half = mine.shape[0]
-    part = near.shape[0]
-    mp = ids[4]
-    core = ids[0]
-    own = pl.multiple_of(mp * half, part)
-    other = pl.multiple_of((1 - mp) * half, part)
-    full_out[pl.ds(own, half), :] = mine[...]
-    full_out[pl.ds(pl.multiple_of(other + core * part, part), part), :] = near[...].astype(BF16)
-    full_out[pl.ds(pl.multiple_of(other + (1 - core) * part, part), part), :] = far[...].astype(BF16)
+    part = quarters[0].shape[0]
+    other = (1 - ids[4]) * half
+    full_out[pl.ds(pl.multiple_of(ids[4] * half, part), half), :] = mine[...]
+    for i, quarter in enumerate(quarters):
+        place = ((ids[1] ^ (i & 1)) * 2 + (ids[0] ^ (i >> 1))) * part
+        full_out[pl.ds(pl.multiple_of(other + place, part), part), :] = quarter[...].astype(BF16)
 
 
 def forward_body(
@@ -539,46 +533,44 @@
     ids = lax.optimization_barrier(ids.astype(jnp.int32))
     across = lambda v: lax.ppermute(v, "mp", SWAP)
 
-    core_swap = lambda v: (lax.ppermute(v, "dp", flips(dp, 0)),)
     chain = Chain()
-
-    quarter = inner // 2
-    piece = lax.dynamic_slice_in_dim(out_weight, core * quarter, quarter, 0).astype(F32)
+    every = range(images)
+
+    quarter = inner // 4
+    piece = lax.dynamic_slice_in_dim(out_weight, place % 4 * quarter, quarter, 0).astype(F32)
     near = across(piece)
 
-    every = range(images)
-    args = [visible, patches, extra_tokens, qkv_weight, first_gain, first_shift]
-    each = lambda dims: pl.BlockSpec((None, *dims[1:]), lambda j: (j,) + (0,) * (len(dims) - 1))
-    stacks = [
-        far((images, rows, width)), far((images, rows, width), BF16), far((images, rows, 3 * inner), BF16),
-        far((images, rows, PAIR)),
-    ]
-    flat = [shape((rows, inner))] * images
-    seqs, firsts, qkvs, logs, *mixeds = chain.call(
-        partial(attend_body, images), args,
-        [whole(visible), each(patches.shape)] + [whole(a) for a in args[2:]],
-        stacks + flat, 40, "attend", grid=images,
-        out_specs=[each(o.shape) for o in stacks] + [whole(o) for o in flat], deep=range(6),
-    )
-    mixed_others = [across(mixeds[0])]
-    (distant,) = chain.at_once(ids, core_swap, near)
+    seqs, firsts, qkvs, logs, mixeds, mixed_others = [], [], [], [], [], []
+    for b in every:
+        args = [visible, patches, extra_tokens, qkv_weight, first_gain, first_shift]
+        got = chain.call(
+            partial(attend_body, b), args,
+            [whole(visible), one_of(patches, b)] + [whole(a) for a in args[2:]],
+            [far((rows, width)), far((rows, width), BF16), far((rows, 3 * inner), BF16),
+             far((rows, PAIR)), shape((rows, inner))],
+            40, f"attend{b}", deep=range(6),
+        )
+        for kept, one in zip((seqs, firsts, qkvs, logs, mixeds), got):
+            kept.append(one)
+        mixed_others.append(across(mixeds[b]))
+        if b == 0:
+            near = chain.hold(near)
+            beyond = lax.ppermute(near, "dp", flips(dp, 1))
+    swaps = lambda *vs: tuple(lax.ppermute(v, "dp", flips(dp, 0)) for v in vs)
+    quarters = [near, beyond, *chain.at_once(ids, swaps, near, beyond)]
     (full,) = chain.call(
-        join_body, [ids, out_weight, near, distant],
-        [scalars(), whole(out_weight), whole(near), whole(distant)],
+        join_body, [ids, out_weight, *quarters],
+        [scalars(), whole(out_weight)] + [whole(q) for q in quarters],
         [shape((2 * inner, width), BF16)], 16, "join",
     )
 
-    for b in range(1, images):
-        mixeds[b] = chain.hold(mixeds[b])
-        mixed_others.append(across(mixeds[b]))
-
     middles, seconds, hiddens, uppers, norms, smalls, norm_others = [], [], [], [], [], [], []
     for b in every:
-        args = [ids, seqs, cotangent, out_bias, second_gain, second_shift, up_bias,
+        args = [ids, seqs[b], cotangent, out_bias, second_gain, second_shift, up_bias,
                 mixeds[b], mixed_others[b], full, up_weight, down_weight]
         got = chain.call(
             forward_body, args,
-            [scalars(), one_of(seqs, b), one_of(cotangent, b)] + [whole(a) for a in args[3:]],
+            [scalars(), whole(seqs[b]), one_of(cotangent, b)] + [whole(a) for a in args[3:]],
             [far((rows, width)), far((rows, width), BF16), far((rows, hidden_width), BF16),
              far((rows, hidden_width), BF16), shape((rows, width)), far((8, width))],
             44, f"forward{b}", deep=(1, 3, 4, 5, 6),
@@ -595,16 +587,15 @@
             [shape((padded, width))], 32, "branch",
         )[0]
 
-    (down_sum,), down_part = weight_sum(chain, ids, dp, "down", 512, [(cotangent, hiddens)], beside=branch)
+    (down_sum,), down_part = weight_sum(chain, ids, dp, "down", 768, [(cotangent, hiddens)], beside=branch)
     down_sum.step()
 
     grads, attns, backs, firsts_part, crosses, part_others = [], [], [], [], [], []
     for b in every:
-        args = [norms[b], norm_others[b], middles[b], qkvs, logs, seqs, cotangent, second_gain,
+        args = [norms[b], norm_others[b], middles[b], qkvs[b], logs[b], seqs[b], cotangent, second_gain,
                 out_weight, qkv_weight, *crosses[-1:]]
         specs = [whole(a) for a in args]
-        for i in (3, 4, 5, 6):
-            specs[i] = one_of(args[i], b)
+        specs[6] = one_of(cotangent, b)
         got = chain.call(
             backward_body, args, specs,
             [far((rows, width)), far((rows, width), BF16), far((rows, 3 * inner), BF16),
@@ -615,7 +606,7 @@
             kept.append(one)
         part_others.append(across(firsts_part[b]))
         if b == 0:
-            (up_sum,), _ = weight_sum(chain, ids, dp, "up", 512, [(seconds, uppers)])
+            (up_sum,), _ = weight_sum(chain, ids, dp, "up", 768, [(seconds, uppers)])
             up_sum.step()
     part_others[0] = chain.hold(part_others[0])
     down_sum.step()
@@ -625,11 +616,9 @@
     )
 
     def input_of(b):
-        args = [first_gain, seqs, firsts_part[b], part_others[b], grads[b]]
-        specs = [whole(a) for a in args]
-        specs[1] = one_of(seqs, b)
+        args = [first_gain, seqs[b], firsts_part[b], part_others[b], grads[b]]
         return chain.call(
-            input_body, args, specs, [shape((rows, width))], 32, f"input{b}", deep=(0, 1, 4)
+            input_body, args, [whole(a) for a in args], [shape((rows, width))], 32, f"input{b}", deep=(0, 1, 4)
         )[0]
 
     out_sum.step()

time: 180 us -> 175 us (0.972)
  waiting for transfers between devices: 43.3 us -> 33 us
  starting transfers between devices: 20.7 us -> 25.7 us
  local copies, waits for them, and re-layouts: 5.65 us -> 7.98 us
    ppermute x8, waiting for transfers between devices: 9.18 us -> 1.41 us  [per_device(): across = lambda v: lax.ppermute(v, 'mp', SWAP)]
    ppermute x8, starting transfers between devices: 8.56 us -> 10.9 us  [per_device(): across = lambda v: lax.ppermute(v, 'mp', SWAP)]
    unnamed x55 -> x51, local copies, waits for them, and re-layouts: 3.65 us -> 5.98 us
    ppermute x12, waiting for transfers between devices: 21.8 us -> 19.5 us  [step(): lax.ppermute(send, 'dp', flips(self.dp, bit))]
    ppermute x1 -> x3, starting transfers between devices: 0.01 us -> 2.22 us  [the longest x1 1.71 us: per_device(): beyond = lax.ppermute(near, 'dp', flips(dp, 1))]
    pallas_call x29 -> x30, Pallas kernels: 106 us -> 105 us  [kernel(): pl.pallas_call(body, out_shape=tuple(outs), grid_spec=pltpu.PrefetchScala...]
  transfers between devices with their start and end apart: 26 -> 28, of which waited for: 14 -> 15; matrix products, arithmetic and copies ran while one was open for 2% -> 2% of each run, Pallas kernels for 58% -> 59%
where the time goes in v3:
time: 175 us; the launch traced here: 174 us
  Pallas kernels  105 us (60%)
  waiting for transfers between devices  33 us (19%)
  starting transfers between devices  25.7 us (15%)
  local copies, waits for them, and re-layouts  7.98 us (5%)
  other arithmetic  1.83 us (1%)
    pallas_call x30, Pallas kernels, kernel(): pl.pallas_call(body, out_shape=tuple(outs), grid_spec=pltpu.PrefetchScala...  105 us
    ppermute x12, waiting for transfers between devices, step(): lax.ppermute(send, 'dp', flips(self.dp, bit))  19.5 us
    ppermute x8, starting transfers between devices, per_device(): across = lambda v: lax.ppermute(v, 'mp', SWAP)  10.9 us
    ppermute x12, starting transfers between devices, step(): lax.ppermute(send, 'dp', flips(self.dp, bit))  10.7 us
    ppermute x3, waiting for transfers between devices, weight_sum(): swap = lambda v: lax.ppermute(v, 'dp', flips(dp, 0))  7.16 us
    unnamed x51, local copies, waits for them, and re-layouts  5.98 us
  transfers between devices with their start and end apart: 28, of which 15 were waited for; matrix products, arithmetic and copies ran while one was open for 2% of the time, Pallas kernels for 59%

profile of v3, /device:TPU:0, one launch (start us, length us, event | category | flops | bytes accessed | tf_op | source)
XLA Modules:
  0.0 174.3 jit_solution(5633152042014763650)
XLA Ops:
  1.6 3.0 %collective-permute-start.8 = (f32[96,768]{1,0:T(8,128)S(1)}, f32[96,768]{1,0:T(8,128)}, u32[]{:S(2)}, u32[]{:S(2)}) collective-permute-start(f32[96,768]{1,0:T(8,128)S(1)} %dynamic-slice_convert_fusion), channel_id=1, source_target_pairs={{0,1},{1,0},{2,3},{3,2},{4,5},{5,4},{6,7},{7,6},{8,9},{9,8},{10,11... | collective-permute-start | bytes 884744 | tf_op jit(solution)/shard_map/ppermute | solution.py:534
  4.6 6.1 %attend0.1 = (f32[258,768]{1,0:T(8,128)}, bf16[258,768]{1,0:T(8,128)(2,1)}, bf16[258,1152]{1,0:T(8,128)(2,1)}, f32[258,128]{1,0:T(8,128)}, f32[258,384]{1,0:T(8,128)S(1)}, /*index=5*/f32[8,128]{1,0:T(8,128)S(1)}) custom-call(s32[2,256]{1,0:T(2,128)} %refs_0_.5, bf16[2,1024,768]{2,1,0:T(8,128)(2,1)} %refs_1_.5, bf16[2,2,768]{2,1,0:T(2,128)(2,1)} %refs_2_.7, ...), custom_call_target="tpu_custom_call" | custom-call | flops 2147483648 | bytes 1 | tf_op jit(solution)/shard_map/attend0/pallas_call | solution.py:70
  11.7 1.7 collective-permute-start.9
  13.5 1.5 collective-permute-start.7
  15.2 6.4 %attend1.1 = (f32[258,768]{1,0:T(8,128)}, bf16[258,768]{1,0:T(8,128)(2,1)}, bf16[258,1152]{1,0:T(8,128)(2,1)}, f32[258,128]{1,0:T(8,128)}, f32[258,384]{1,0:T(8,128)S(1)}, /*index=5*/f32[8,128]{1,0:T(8,128)S(1)}) custom-call(s32[2,256]{1,0:T(2,128)} %refs_0_.5, bf16[2,1024,768]{2,1,0:T(8,128)(2,1)} %refs_1_.5, bf16[2,2,768]{2,1,0:T(2,128)(2,1)} %refs_2_.7, ...), custom_call_target="tpu_custom_call" | custom-call | flops 2147483648 | bytes 1 | tf_op jit(solution)/shard_map/attend1/pallas_call | solution.py:70
  22.1 2.3 %conditional.4 = (f32[96,768]{1,0:T(8,128)}, f32[96,768]{1,0:T(8,128)}) conditional(s32[]{:T(128)} %bitcast.5, () %tuple.43, (f32[96,768]{1,0:T(8,128)}, f32[96,768]{1,0:T(8,128)}) %tuple.44), branch_computations={%region_0.1_spmd, %region_1.2_spmd} | conditional | bytes 2359392 | solution.py:110
  27.2 5.9 %forward0.1 = (f32[258,768]{1,0:T(8,128)}, bf16[258,768]{1,0:T(8,128)(2,1)}, bf16[258,1536]{1,0:T(8,128)(2,1)}, bf16[258,1536]{1,0:T(8,128)(2,1)}, f32[258,768]{...) custom-call(s32[5]{0:T(128)S(1)} %stack.44.refs_0_, f32[258,768]{1,0:T(8,128)} %get-tuple-element.143.refs_1_.refs_5_, ...), custom_call_target="tpu_custom_call" | custom-call | flops 2147483648 | bytes 1 | tf_op jit(solution)/shard_map/forward0/pallas_call | solution.py:70
  34.6 6.0 %forward1.1 = (f32[258,768]{1,0:T(8,128)}, bf16[258,768]{1,0:T(8,128)(2,1)}, bf16[258,1536]{1,0:T(8,128)(2,1)}, bf16[258,1536]{1,0:T(8,128)(2,1)}, f32[258,768]{...) custom-call(s32[5]{0:T(128)S(1)} %stack.44.refs_0_, f32[258,768]{1,0:T(8,128)} %get-tuple-element.154.refs_1_.refs_5_, ...), custom_call_target="tpu_custom_call" | custom-call | flops 2147483648 | bytes 1 | tf_op jit(solution)/shard_map/forward1/pallas_call | solution.py:70
  40.6 5.6 %down_grads.1 = (f32[384,1536]{1,0:T(8,128)}, f32[384,1536]{1,0:T(8,128)}, f32[8,128]{1,0:T(8,128)S(1)}) custom-call(s32[5]{0:T(128)S(1)} %stack.44.refs_0_, bf16[2,258,768]{2,1,0:T(8,128)(2,1)} %copy-done.1, bf16[2,258,768]{2,1,0:T(8,128)(2,1)} %copy-done.1, bf16[258,1536]{1,0:T(8,128)(2,1)} %get-tuple-element.153.refs_3_, ...), custom_call_target="tpu_custom_call" | custom-call | flops 2147483648 | bytes 1 | tf_op jit(solution)/shard_map/down_grads/pallas_call | solution.py:70
  46.8 4.9 %conditional.5 = (f32[384,1536]{1,0:T(8,128)}, f32[528,768]{1,0:T(8,128)}) conditional(s32[]{:T(128)} %bitcast.5, () %tuple.41, (f32[384,1536]{1,0:T(8,128)}, bf16[258,1536]{1,0:T(8,128)(2,1)S(1)}, bf16[258,1536]{1,0:T(8,128)(2,1)S(1)}, bf16[1536,768]{1,0:T(8,128)(2,1)S(1)}) %tuple.70), branch_computations={%region_2.3_spmd, %region_3.4_spmd} | conditional | flops 2147483648 | bytes 9437241 | solution.py:110
  46.8 2.7 %branch.1 = f32[528,768]{1,0:T(8,128)} custom-call(bf16[258,1536]{1,0:T(8,128)(2,1)S(1)} %get-tuple-element.23.refs_0_, bf16[258,1536]{1,0:T(8,128)(2,1)S(1)} %get-tuple-element.24.refs_1_, bf16[1536,768]{1,0:T(8,128)(2,1)S(1)} %get-tuple-element.25.refs_2_), custom_call_target="tpu_custom_call" | custom-call | flops 2147483648 | bytes 1 | tf_op jit(solution)/shard_map/cond/branch_1_fun/branch/pallas_call | solution.py:70
  49.5 2.2 %collective-permute-done.2 = f32[384,1536]{1,0:T(8,128)} collective-permute-done((f32[384,1536]{1,0:T(8,128)}, f32[384,1536]{1,0:T(8,128)}, u32[]{:S(2)}, u32[]{:S(2)}) %collective-permute-start.2) | collective-permute-done | bytes 2359328 | tf_op jit(solution)/shard_map/cond/branch_1_fun/ppermute | solution.py:478
  51.7 3.5 %down0_step1.1 = (f32[192,1536]{1,0:T(8,128)}, f32[8,128]{1,0:T(8,128)S(1)}) custom-call(s32[5]{0:T(128)S(1)} %stack.44.refs_0_, f32[384,1536]{1,0:T(8,128)} %get-tuple-element.169.refs_1_, f32[384,1536]{1,0:T(8,128)} %get-tuple-element.170.refs_2_, f32[8,128]{1,0:T(8,128)S(1)} %get-tuple-element.171.refs_3_), custom_call_target="tpu_custom_call" | custom-call | flops 2147483648 | bytes 1 | tf_op jit(solution)/shard_map/down0_step1/pallas_call | solution.py:70
  55.6 9.1 %backward0.1 = (f32[258,768]{1,0:T(8,128)}, bf16[258,768]{1,0:T(8,128)(2,1)}, bf16[258,1152]{1,0:T(8,128)(2,1)}, f32[258,768]{1,0:T(8,128)}, f32[8,768]{1,0:T(8,...) custom-call(f32[258,768]{1,0:T(8,128)} %get-tuple-element.165.refs_0_, f32[258,768]{1,0:T(8,128)} %collective-permute-done.12.refs_1_, ...), custom_call_target="tpu_custom_call" | custom-call | flops 8589934592 | bytes 1 | tf_op jit(solution)/shard_map/backward0/pallas_call | solution.py:70
  64.6 1.7 collective-permute-start.15
  66.4 5.5 %up_grads.1 = (f32[384,1536]{1,0:T(8,128)}, f32[384,1536]{1,0:T(8,128)}, f32[8,128]{1,0:T(8,128)S(1)}) custom-call(s32[5]{0:T(128)S(1)} %stack.44.refs_0_, bf16[258,768]{1,0:T(8,128)(2,1)} %get-tuple-element.174.refs_1_, bf16[258,768]{1,0:T(8,128)(2,1)} %get-tuple-element.175.refs_2_, bf16[258,1536]{1,0:T(8,128)(2,1)} %get-tuple-element.176.refs_3_, ...), custom_call_target="tpu_custom_call" | custom-call | flops 2147483648 | bytes 1 | tf_op jit(solution)/shard_map/up_grads/pallas_call | solution.py:70
  71.8 4.9 %conditional.6 = (f32[384,1536]{1,0:T(8,128)}) conditional(s32[]{:T(128)} %bitcast.5, () %tuple.46, f32[384,1536]{1,0:T(8,128)} %get-tuple-element.180), branch_computations={%region_4.5_spmd, %region_5.6_spmd} | conditional | bytes 9437232 | solution.py:110
  71.9 4.9 %collective-permute-done.3 = f32[384,1536]{1,0:T(8,128)} collective-permute-done((f32[384,1536]{1,0:T(8,128)}, f32[384,1536]{1,0:T(8,128)}, u32[]{:S(2)}, u32[]{:S(2)}) %collective-permute-start.3) | collective-permute-done | bytes 2359328 | tf_op jit(solution)/shard_map/cond/branch_1_fun/ppermute | solution.py:478
  76.7 3.3 %up0_step1.1 = (f32[192,1536]{1,0:T(8,128)}, f32[8,128]{1,0:T(8,128)S(1)}) custom-call(s32[5]{0:T(128)S(1)} %stack.44.refs_0_, f32[384,1536]{1,0:T(8,128)} %get-tuple-element.179.refs_1_, f32[384,1536]{1,0:T(8,128)} %get-tuple-element.282.refs_2_, f32[8,128]{1,0:T(8,128)S(1)} %get-tuple-element.181.refs_3_), custom_call_target="tpu_custom_call" | custom-call | flops 2147483648 | bytes 1 | tf_op jit(solution)/shard_map/up0_step1/pallas_call | solution.py:70
  81.6 8.6 %backward1.1 = (f32[258,768]{1,0:T(8,128)}, bf16[258,768]{1,0:T(8,128)(2,1)}, bf16[258,1152]{1,0:T(8,128)(2,1)}, f32[258,768]{1,0:T(8,128)S(1)}, f32[8,768]{1,0:...) custom-call(f32[258,768]{1,0:T(8,128)} %get-tuple-element.161.refs_0_, ...), custom_call_target="tpu_custom_call" | custom-call | flops 8589934592 | bytes 1 | tf_op jit(solution)/shard_map/backward1/pallas_call | solution.py:70
  90.3 2.9 %down0_step2.1 = (f32[96,1536]{1,0:T(8,128)}, f32[8,128]{1,0:T(8,128)S(1)}) custom-call(s32[5]{0:T(128)S(1)} %stack.44.refs_0_, f32[384,1536]{1,0:T(8,128)} %get-tuple-element.169.refs_1_, f32[384,1536]{1,0:T(8,128)} %get-tuple-element.170.refs_2_, f32[192,1536]{1,0:T(8,128)S(1)} %collective-permute-done.14.refs_3_, f32[8,128]{1,0:T(8,128)S(1)} %get-tuple-element.199.refs_4_), custom_call_target="tpu_custom_call" | custom-call | flops 2147483648 | bytes 1 | tf_op jit(solution)/shard_map/down0_step2/pallas_call | solution.py:70
  93.1 1.6 collective-permute-start.18
  94.8 7.6 %last_grads.1 = (f32[392,1536]{1,0:T(8,128)}, f32[392,1536]{1,0:T(8,128)}, f32[8,128]{1,0:T(8,128)S(1)}) custom-call(s32[5]{0:T(128)S(1)} %stack.44.refs_0_, bf16[258,768]{1,0:T(8,128)(2,1)} %get-tuple-element.185.refs_1_, bf16[258,768]{1,0:T(8,128)(2,1)} %get-tuple-element.186.refs_2_, f32[258,384]{1,0:T(8,128)} %copy-done.3, f32[258,384]{1,0:T(8,128)} %copy-done.4, ...), custom_call_target="tpu_custom_call" | custom-call | flops 2147483648 | bytes 1 | tf_op jit(solution)/shard_map/last_grads/pallas_call | solution.py:70
  102.4 5.0 %conditional.7 = (f32[392,1536]{1,0:T(8,128)}, f32[8,1536]{1,0:T(8,128)}, f32[8,1536]{1,0:T(8,128)}) conditional(s32[]{:T(128)} %bitcast.5, () %tuple.48, (f32[392,1536]{1,0:T(8,128)}, f32[8,1536]{1,0:T(8,128)S(1)}) %tuple.49), branch_computations={%region_6.7_spmd, %region_7.8_spmd} | conditional | bytes 10027152 | solution.py:110
  104.4 2.9 %collective-permute-done.5 = f32[8,1536]{1,0:T(8,128)} collective-permute-done((f32[8,1536]{1,0:T(8,128)S(1)}, f32[8,1536]{1,0:T(8,128)}, u32[]{:S(2)}, u32[]{:S(2)}) %collective-permute-start.5) | collective-permute-done | bytes 49184 | tf_op jit(solution)/shard_map/cond/branch_1_fun/ppermute | solution.py:482
  108.4 1.9 %last0_step1.1 = (f32[200,768]{1,0:T(8,128)S(1)}, f32[8,128]{1,0:T(8,128)S(1)}) custom-call(s32[5]{0:T(128)S(1)} %stack.44.refs_0_, f32[392,1536]{1,0:T(8,128)} %get-tuple-element.201.refs_1_.refs_3_.refs_4_.refs_5_.refs_6_, f32[392,1536]{1,0:T(8,128)} %get-tuple-element.203.refs_2_.refs_4_.refs_5_.refs_6_.refs_7_, ...), custom_call_target="tpu_custom_call" | custom-call | flops 2147483648 | bytes 1 | tf_op jit(solution)/shard_map/last0_step1/pallas_call | solution.py:70
  110.9 1.8 %down0_step3.1 = (f32[48,1536]{1,0:T(8,128)S(1)}, f32[8,128]{1,0:T(8,128)S(1)}) custom-call(s32[5]{0:T(128)S(1)} %stack.44.refs_0_, f32[384,1536]{1,0:T(8,128)} %get-tuple-element.169.refs_1_, f32[384,1536]{1,0:T(8,128)} %get-tuple-element.170.refs_2_, f32[192,1536]{1,0:T(8,128)S(1)} %collective-permute-done.14.refs_3_, ...), custom_call_target="tpu_custom_call" | custom-call | flops 2147483648 | bytes 1 | tf_op jit(solution)/shard_map/down0_step3/pallas_call | solution.py:70
  112.6 2.7 %collective-permute-start.23 = (f32[48,1536]{1,0:T(8,128)S(1)}, f32[48,1536]{1,0:T(8,128)S(1)}, u32[]{:S(2)}, u32[]{:S(2)}) collective-permute-start(f32[48,1536]{1,0:T(8,128)S(1)} %get-tuple-element.223), channel_id=1, source_target_pairs={{0,16},{2,18},{4,20},{6,22},{8,24},{10,26},{12,28},{14,30},{16,0},... | collective-permute-start | bytes 884744 | tf_op jit(solution)/shard_map/ppermute | solution.py:414
  115.3 2.1 %up0_step2.1 = (f32[96,1536]{1,0:T(8,128)S(1)}, f32[8,128]{1,0:T(8,128)S(1)}) custom-call(s32[5]{0:T(128)S(1)} %stack.44.refs_0_, f32[384,1536]{1,0:T(8,128)} %get-tuple-element.179.refs_1_, f32[384,1536]{1,0:T(8,128)} %get-tuple-element.282.refs_2_, f32[192,1536]{1,0:T(8,128)} %collective-permute-done.17.refs_3_, f32[8,128]{1,0:T(8,128)S(1)} %get-tuple-element.213.refs_4_), custom_call_target="tpu_custom_call" | custom-call | flops 2147483648 | bytes 1 | tf_op jit(solution)/shard_map/up0_step2/pallas_call | solution.py:70
  117.9 1.9 %last1_step1.1 = (f32[192,768]{1,0:T(8,128)S(1)}, f32[8,128]{1,0:T(8,128)S(1)}) custom-call(s32[5]{0:T(128)S(1)} %stack.44.refs_0_, f32[392,1536]{1,0:T(8,128)} %get-tuple-element.201.refs_1_.refs_3_.refs_4_.refs_5_.refs_6_, f32[392,1536]{1,0:T(8,128)} %get-tuple-element.203.refs_2_.refs_4_.refs_5_.refs_6_.refs_7_, f32[8,128]{1,0:T(8,128)S(1)} %get-tuple-element.214.refs_3_), custom_call_target="tpu_custom_call" | custom-call | flops 2147483648 | bytes 1 | tf_op jit(solution)/shard_map/last1_step1/pallas_call | solution.py:70
  119.7 1.6 collective-permute-start.21
  121.3 2.4 %input0.1 = (f32[258,768]{1,0:T(8,128)S(1)}, f32[8,128]{1,0:T(8,128)S(1)}) custom-call(f32[768]{0:T(1024)} %refs_0_.7, f32[258,768]{1,0:T(8,128)} %get-tuple-element.143.refs_1_.refs_5_, f32[258,768]{1,0:T(8,128)} %get-tuple-element.197.refs_2_, f32[258,768]{1,0:T(8,128)} %collective-permute-done.15.refs_3_, f32[258,768]{1,0:T(8,128)} %get-tuple-element.209.refs_4_, ...), custom_call_target="tpu_custom_call" | custom-call | flops 2147483648 | bytes 1 | tf_op jit(solution)/shard_map/input0/pallas_call | solution.py:70
  123.7 3.3 %collective-permute-done.16.refs_3_.refs_8_.refs_9_.refs_10_ = f32[200,768]{1,0:T(8,128)S(1)} collective-permute-done((f32[200,768]{1,0:T(8,128)S(1)}, f32[200,768]{1,0:T(8,128)S(1)}, u32[]{:S(2)}, u32[]{:S(2)}) %collective-permute-start.16) | collective-permute-done | bytes 614432 | tf_op jit(solution)/shard_map/ppermute | solution.py:414
  127.0 1.7 last0_step2.1
  128.7 1.9 %input1.1 = (f32[258,768]{1,0:T(8,128)S(1)}, f32[8,128]{1,0:T(8,128)S(1)}) custom-call(f32[768]{0:T(1024)} %refs_0_.7, f32[258,768]{1,0:T(8,128)} %get-tuple-element.154.refs_1_.refs_5_, f32[258,768]{1,0:T(8,128)S(1)} %copy-done.13, f32[258,768]{1,0:T(8,128)S(1)} %collective-permute-done.13.refs_3_, f32[258,768]{1,0:T(8,128)} %get-tuple-element.184.refs_4_, ...), custom_call_target="tpu_custom_call" | custom-call | flops 2147483648 | bytes 1 | tf_op jit(solution)/shard_map/input1/pallas_call | solution.py:70
  132.4 2.0 %copy.35 = f32[2,258,768]{2,0,1:T(2,128)} copy(f32[2,258,768]{2,1,0:T(8,128)S(1)} %pad_maximum_fusion) | data formatting | bytes 3170304
  134.4 2.5 %down0_last.1 = (f32[48,1536]{1,0:T(8,128)}, f32[8,128]{1,0:T(8,128)S(1)}) custom-call(s32[5]{0:T(128)S(1)} %stack.44.refs_0_, f32[384,1536]{1,0:T(8,128)} %get-tuple-element.169.refs_1_, f32[384,1536]{1,0:T(8,128)} %get-tuple-element.170.refs_2_, f32[192,1536]{1,0:T(8,128)S(1)} %copy-done.9, f32[96,1536]{1,0:T(8,128)} %collective-permute-done.18.refs_4_, ...), custom_call_target="tpu_custom_call" | custom-call | flops 2147483648 | bytes 1 | tf_op jit(solution)/shard_map/down0_last/pallas_call | solution.py:70
  136.9 3.0 %collective-permute-done.22.refs_4_ = f32[96,1536]{1,0:T(8,128)S(1)} collective-permute-done((f32[96,1536]{1,0:T(8,128)S(1)}, f32[96,1536]{1,0:T(8,128)S(1)}, u32[]{:S(2)}, u32[]{:S(2)}) %collective-permute-start.22) | collective-permute-done | bytes 589856 | tf_op jit(solution)/shard_map/ppermute | solution.py:414
  139.9 1.7 up0_step3.1
  141.7 1.7 last1_step2.1
  144.6 3.7 %collective-permute-done.20.refs_4_.refs_10_.refs_11_ = f32[104,768]{1,0:T(8,128)S(1)} collective-permute-done((f32[104,768]{1,0:T(8,128)S(1)}, f32[104,768]{1,0:T(8,128)S(1)}, u32[]{:S(2)}, u32[]{:S(2)}) %collective-permute-start.20) | collective-permute-done | bytes 319520 | tf_op jit(solution)/shard_map/ppermute | solution.py:414
  148.3 1.6 last0_step3.1
  150.0 8.7 %collective-permute-done.26.refs_5_ = f32[48,1536]{1,0:T(8,128)S(1)} collective-permute-done((f32[48,1536]{1,0:T(8,128)S(1)}, f32[48,1536]{1,0:T(8,128)S(1)}, u32[]{:S(2)}, u32[]{:S(2)}) %collective-permute-start.26) | collective-permute-done | bytes 294944 | tf_op jit(solution)/shard_map/ppermute | solution.py:414
  158.7 2.5 %up0_last.1 = (f32[48,1536]{1,0:T(8,128)}, f32[8,128]{1,0:T(8,128)S(1)}) custom-call(s32[5]{0:T(128)S(1)} %stack.44.refs_0_, f32[384,1536]{1,0:T(8,128)} %get-tuple-element.179.refs_1_, f32[384,1536]{1,0:T(8,128)} %get-tuple-element.282.refs_2_, f32[192,1536]{1,0:T(8,128)} %collective-permute-done.17.refs_3_, ...), custom_call_target="tpu_custom_call" | custom-call | flops 2147483648 | bytes 1 | tf_op jit(solution)/shard_map/up0_last/pallas_call | solution.py:70
  161.2 1.6 last1_step3.1
  163.4 1.6 last0_last.1
  168.5 1.8 %output.1 = (bf16[2,258,768]{2,1,0:T(8,128)(2,1)S(1)}, f32[8,128]{1,0:T(8,128)S(1)}) custom-call(f32[528,768]{1,0:T(8,128)} %get-tuple-element.219.refs_0_, f32[528,768]{1,0:T(8,128)S(1)} %collective-permute-done.19.refs_1_, f32[768]{0:T(1024)} %refs_2_.8, f32[258,768]{1,0:T(8,128)S(1)} %copy-done.10, f32[258,768]{1,0:T(8,128)S(1)} %copy-done.11, ...), custom_call_target="tpu_custom_call" | custom-call | flops 2147483648 | bytes 1 | tf_op jit(solution)/shard_map/output/pallas_call | solution.py:70
  170.5 1.6 last1_last.1
  (104 shorter events, 25.5 us)
Async XLA Ops:
  1.6 10.1 %collective-permute-start.8 = (f32[96,768]{1,0:T(8,128)S(1)}, f32[96,768]{1,0:T(8,128)}, u32[]{:S(2)}, u32[]{:S(2)}) collective-permute-start(f32[96,768]{1,0:T(8,128)S(1)} %dynamic-slice_convert_fusion), channel_id=1, source_target_pairs={{0,1},{1,0},{2,3},{3,2},{4,5},{5,4},{6,7},{7,6},{8,9},{9,8},{10,11... | collective-permute-start | bytes 884744 | tf_op jit(solution)/shard_map/ppermute | solution.py:534
  4.6 10.5 %copy-start.21 = (bf16[2,258,768]{2,0,1:T(2,128)(2,1)S(1)}, bf16[2,258,768]{2,0,1:T(2,128)(2,1)}, u32[]{:S(2)}) copy-start(bf16[2,258,768]{2,0,1:T(2,128)(2,1)} %param.37) | copy-start | bytes 2377732
  10.8 15.2 %copy-start.3 = (f32[258,384]{1,0:T(8,128)}, f32[258,384]{1,0:T(8,128)S(1)}, u32[]{:S(2)}) copy-start(f32[258,384]{1,0:T(8,128)S(1)} %get-tuple-element.144.refs_7_.refs_3_) | copy-start | bytes 1188868
  11.7 10.4 %collective-permute-start.9 = (f32[96,768]{1,0:T(8,128)}, f32[96,768]{1,0:T(8,128)}, u32[]{:S(2)}, u32[]{:S(2)}) collective-permute-start(f32[96,768]{1,0:T(8,128)} %collective-permute-done.8.refs_2_), channel_id=1, source_target_pairs={{0,4},{2,6},{4,0},{6,2},{8,12},{10,14},{12,8},{14,10},{16,20},{18,... | collective-permute-start | bytes 884744 | tf_op jit(solution)/shard_map/ppermute | solution.py:558
  13.5 12.5 %collective-permute-start.7 = (f32[258,384]{1,0:T(8,128)S(1)}, f32[258,384]{1,0:T(8,128)S(1)}, u32[]{:S(2)}, u32[]{:S(2)}) collective-permute-start(f32[258,384]{1,0:T(8,128)S(1)} %get-tuple-element.144.refs_7_.refs_3_), channel_id=1, source_target_pairs={{0,1},{1,0},{2,3},{3,2},{4,5},{5,4},{6,7},{7,6},{8,9},{9,8},{10,11... | collective-permute-start | bytes 1188872 | tf_op jit(solution)/shard_map/ppermute | solution.py:534
  15.2 19.4 %copy-start.1 = (bf16[2,258,768]{2,1,0:T(8,128)(2,1)}, bf16[2,258,768]{2,1,0:T(8,128)(2,1)S(1)}, u32[]{:S(2)}) copy-start(bf16[2,258,768]{2,1,0:T(8,128)(2,1)S(1)} %copy.30.refs_2_.refs_1_.refs_6_) | copy-start | bytes 2377732
  15.2 9.2 %copy-start.5 = (bf16[384,768]{1,0:T(8,128)(2,1)S(1)}, bf16[384,768]{1,0:T(8,128)(2,1)}, u32[]{:S(2)}) copy-start(bf16[384,768]{1,0:T(8,128)(2,1)} %refs_8_.3) | copy-start | bytes 1769476
  21.6 13.0 %copy-start.4 = (f32[258,384]{1,0:T(8,128)}, f32[258,384]{1,0:T(8,128)S(1)}, u32[]{:S(2)}) copy-start(f32[258,384]{1,0:T(8,128)S(1)} %get-tuple-element.155.refs_7_.refs_4_) | copy-start | bytes 1188868
  21.6 13.0 %collective-permute-start.10 = (f32[258,384]{1,0:T(8,128)S(1)}, f32[258,384]{1,0:T(8,128)S(1)}, u32[]{:S(2)}, u32[]{:S(2)}) collective-permute-start(f32[258,384]{1,0:T(8,128)S(1)} %get-tuple-element.155.refs_7_.refs_4_), channel_id=1, source_target_pairs={{0,1},{1,0},{2,3},{3,2},{4,5},{5,4},{6,7},{7,6},{8,9},{9,8},{10,11... | collective-permute-start | bytes 1188872 | tf_op jit(solution)/shard_map/ppermute | solution.py:534
  22.1 1.9 %collective-permute-start = (f32[96,768]{1,0:T(8,128)}, f32[96,768]{1,0:T(8,128)}, u32[]{:S(2)}, u32[]{:S(2)}) collective-permute-start(f32[96,768]{1,0:T(8,128)} %get-tuple-element.20), channel_id=1, source_target_pairs={{0,2},{2,0},{4,6},{6,4},{8,10},{10,8},{12,14},{14,12},{16,18},{18,... | collective-permute-start | bytes 884744 | tf_op jit(solution)/shard_map/cond/branch_1_fun/ppermute | solution.py:559
  22.1 2.3 %collective-permute-start.1 = (f32[96,768]{1,0:T(8,128)}, f32[96,768]{1,0:T(8,128)}, u32[]{:S(2)}, u32[]{:S(2)}) collective-permute-start(f32[96,768]{1,0:T(8,128)} %get-tuple-element.21), channel_id=1, source_target_pairs={{0,2},{2,0},{4,6},{6,4},{8,10},{10,8},{12,14},{14,12},{16,18},{18,... | collective-permute-start | bytes 884744 | tf_op jit(solution)/shard_map/cond/branch_1_fun/ppermute | solution.py:559
  24.5 2.7 %copy-start.20 = (bf16[1536,768]{1,0:T(8,128)(2,1)S(1)}, bf16[1536,768]{1,0:T(8,128)(2,1)}, u32[]{:S(2)}) copy-start(bf16[1536,768]{1,0:T(8,128)(2,1)} %refs_11_.3) | copy-start | bytes 7077892
  33.1 22.4 %collective-permute-start.12 = (f32[258,768]{1,0:T(8,128)}, f32[258,768]{1,0:T(8,128)}, u32[]{:S(2)}, u32[]{:S(2)}) collective-permute-start(f32[258,768]{1,0:T(8,128)} %get-tuple-element.165.refs_0_), channel_id=1, source_target_pairs={{0,1},{1,0},{2,3},{3,2},{4,5},{5,4},{6,7},{7,6},{8,9},{9,8},{10,11... | collective-permute-start | bytes 2377736 | tf_op jit(solution)/shard_map/ppermute | solution.py:534
  40.6 5.6 %copy-start.22 = (bf16[258,1536]{1,0:T(8,128)(2,1)S(1)}, bf16[258,1536]{1,0:T(8,128)(2,1)}, u32[]{:S(2)}) copy-start(bf16[258,1536]{1,0:T(8,128)(2,1)} %get-tuple-element.153.refs_3_) | copy-start | bytes 2377732
  40.6 5.6 %copy-start.23 = (bf16[258,1536]{1,0:T(8,128)(2,1)S(1)}, bf16[258,1536]{1,0:T(8,128)(2,1)}, u32[]{:S(2)}) copy-start(bf16[258,1536]{1,0:T(8,128)(2,1)} %get-tuple-element.157.refs_4_) | copy-start | bytes 2377732
  46.2 35.3 %collective-permute-start.11 = (f32[258,768]{1,0:T(8,128)}, f32[258,768]{1,0:T(8,128)}, u32[]{:S(2)}, u32[]{:S(2)}) collective-permute-start(f32[258,768]{1,0:T(8,128)} %get-tuple-element.161.refs_0_), channel_id=1, source_target_pairs={{0,1},{1,0},{2,3},{3,2},{4,5},{5,4},{6,7},{7,6},{8,9},{9,8},{10,11... | collective-permute-start | bytes 2377736 | tf_op jit(solution)/shard_map/ppermute | solution.py:534
  46.8 4.9 %collective-permute-start.2 = (f32[384,1536]{1,0:T(8,128)}, f32[384,1536]{1,0:T(8,128)}, u32[]{:S(2)}, u32[]{:S(2)}) collective-permute-start(f32[384,1536]{1,0:T(8,128)} %get-tuple-element.22), channel_id=1, source_target_pairs={{0,2},{2,0},{4,6},{6,4},{8,10},{10,8},{12,14},{14,12},{16,18},{18,... | collective-permute-start | bytes 7077896 | tf_op jit(solution)/shard_map/cond/branch_1_fun/ppermute | solution.py:478
  51.7 3.9 %copy-start.2 = (bf16[2,258,768]{2,1,0:T(8,128)(2,1)S(1)}, bf16[2,258,768]{2,1,0:T(8,128)(2,1)}, u32[]{:S(2)}) copy-start(bf16[2,258,768]{2,1,0:T(8,128)(2,1)} %copy-done.1) | copy-start | bytes 2377732
  51.7 3.9 %copy-start.6 = (bf16[3,768,384]{2,1,0:T(8,128)(2,1)S(1)}, bf16[3,768,384]{2,1,0:T(8,128)(2,1)}, u32[]{:S(2)}) copy-start(bf16[3,768,384]{2,1,0:T(8,128)(2,1)} %refs_9_.3) | copy-start | bytes 5308420
  55.2 35.0 %collective-permute-start.14 = (f32[192,1536]{1,0:T(8,128)}, f32[192,1536]{1,0:T(8,128)S(1)}, u32[]{:S(2)}, u32[]{:S(2)}) collective-permute-start(f32[192,1536]{1,0:T(8,128)} %get-tuple-element.196), channel_id=1, source_target_pairs={{0,4},{2,6},{4,0},{6,2},{8,12},{10,14},{12,8},{14,10},{16,20},{18,... | collective-permute-start | bytes 3538952 | tf_op jit(solution)/shard_map/ppermute | solution.py:414
  64.6 25.6 %collective-permute-start.15 = (f32[258,768]{1,0:T(8,128)}, f32[258,768]{1,0:T(8,128)}, u32[]{:S(2)}, u32[]{:S(2)}) collective-permute-start(f32[258,768]{1,0:T(8,128)} %get-tuple-element.197.refs_2_), channel_id=1, source_target_pairs={{0,1},{1,0},{2,3},{3,2},{4,5},{5,4},{6,7},{7,6},{8,9},{9,8},{10,11... | collective-permute-start | bytes 2377736 | tf_op jit(solution)/shard_map/ppermute | solution.py:534
  71.8 4.9 %collective-permute-start.3 = (f32[384,1536]{1,0:T(8,128)}, f32[384,1536]{1,0:T(8,128)}, u32[]{:S(2)}, u32[]{:S(2)}) collective-permute-start(f32[384,1536]{1,0:T(8,128)} %param.5), channel_id=1, source_target_pairs={{0,2},{2,0},{4,6},{6,4},{8,10},{10,8},{12,14},{14,12},{16,18},{18,... | collective-permute-start | bytes 7077896 | tf_op jit(solution)/shard_map/cond/branch_1_fun/ppermute | solution.py:478
  76.7 4.8 %copy-start.7 = (bf16[3,768,384]{2,1,0:T(8,128)(2,1)S(1)}, bf16[3,768,384]{2,1,0:T(8,128)(2,1)}, u32[]{:S(2)}) copy-start(bf16[3,768,384]{2,1,0:T(8,128)(2,1)} %refs_9_.3) | copy-start | bytes 5308420
  80.1 35.2 %collective-permute-start.17 = (f32[192,1536]{1,0:T(8,128)}, f32[192,1536]{1,0:T(8,128)}, u32[]{:S(2)}, u32[]{:S(2)}) collective-permute-start(f32[192,1536]{1,0:T(8,128)} %get-tuple-element.210), channel_id=1, source_target_pairs={{0,4},{2,6},{4,0},{6,2},{8,12},{10,14},{12,8},{14,10},{16,20},{18,... | collective-permute-start | bytes 3538952 | tf_op jit(solution)/shard_map/ppermute | solution.py:414
  90.2 2.9 %copy-start.12 = (f32[258,768]{1,0:T(8,128)}, f32[258,768]{1,0:T(8,128)S(1)}, u32[]{:S(2)}) copy-start(f32[258,768]{1,0:T(8,128)S(1)} %get-tuple-element.183.refs_2_) | copy-start | bytes 2377732
  90.2 4.5 %copy-start.16 = (f32[8,768]{1,0:T(8,128)S(1)}, f32[8,768]{1,0:T(8,128)}, u32[]{:S(2)}) copy-start(f32[8,768]{1,0:T(8,128)} %get-tuple-element.191.refs_9_) | copy-start | bytes 73732
  90.2 4.5 %copy-start.17 = (f32[8,768]{1,0:T(8,128)S(1)}, f32[8,768]{1,0:T(8,128)}, u32[]{:S(2)}) copy-start(f32[8,768]{1,0:T(8,128)} %get-tuple-element.192.refs_10_) | copy-start | bytes 73732
  90.2 4.5 %copy-start.18 = (f32[8,768]{1,0:T(8,128)S(1)}, f32[8,768]{1,0:T(8,128)}, u32[]{:S(2)}) copy-start(f32[8,768]{1,0:T(8,128)} %get-tuple-element.193.refs_11_) | copy-start | bytes 73732
  90.2 4.5 %copy-start.19 = (f32[8,768]{1,0:T(8,128)S(1)}, f32[8,768]{1,0:T(8,128)}, u32[]{:S(2)}) copy-start(f32[8,768]{1,0:T(8,128)} %get-tuple-element.194.refs_12_) | copy-start | bytes 73732
  90.3 20.6 %copy-start.8 = (f32[192,1536]{1,0:T(8,128)}, f32[192,1536]{1,0:T(8,128)S(1)}, u32[]{:S(2)}) copy-start(f32[192,1536]{1,0:T(8,128)S(1)} %collective-permute-done.14.refs_3_) | copy-start | bytes 3538948
  93.1 17.7 %collective-permute-start.18 = (f32[96,1536]{1,0:T(8,128)}, f32[96,1536]{1,0:T(8,128)}, u32[]{:S(2)}, u32[]{:S(2)}) collective-permute-start(f32[96,1536]{1,0:T(8,128)} %get-tuple-element.211), channel_id=1, source_target_pairs={{0,8},{2,10},{4,12},{6,14},{8,0},{10,2},{12,4},{14,6},{16,24},{18,... | collective-permute-start | bytes 1769480 | tf_op jit(solution)/shard_map/ppermute | solution.py:414
  102.4 5.0 %copy-start.13 = (f32[258,768]{1,0:T(8,128)S(1)}, f32[258,768]{1,0:T(8,128)}, u32[]{:S(2)}) copy-start(f32[258,768]{1,0:T(8,128)} %copy-done.12) | copy-start | bytes 2377732
  102.4 5.0 %collective-permute-start.4 = (f32[392,1536]{1,0:T(8,128)}, f32[392,1536]{1,0:T(8,128)}, u32[]{:S(2)}, u32[]{:S(2)}) collective-permute-start(f32[392,1536]{1,0:T(8,128)} %get-tuple-element.26), channel_id=1, source_target_pairs={{0,2},{2,0},{4,6},{6,4},{8,10},{10,8},{12,14},{14,12},{16,18},{18,... | collective-permute-start | bytes 7225352 | tf_op jit(solution)/shard_map/cond/branch_1_fun/ppermute | solution.py:478
  102.5 4.7 %collective-permute-start.5 = (f32[8,1536]{1,0:T(8,128)S(1)}, f32[8,1536]{1,0:T(8,128)}, u32[]{:S(2)}, u32[]{:S(2)}) collective-permute-start(f32[8,1536]{1,0:T(8,128)S(1)} %get-tuple-element.27), channel_id=1, source_target_pairs={{0,1},{1,0},{2,3},{3,2},{4,5},{5,4},{6,7},{7,6},{8,9},{9,8},{10,11... | collective-permute-start | bytes 147464 | tf_op jit(solution)/shard_map/cond/branch_1_fun/ppermute | solution.py:482
  103.1 4.3 %collective-permute-start.6 = (f32[8,1536]{1,0:T(8,128)S(1)}, f32[8,1536]{1,0:T(8,128)}, u32[]{:S(2)}, u32[]{:S(2)}) collective-permute-start(f32[8,1536]{1,0:T(8,128)S(1)} %get-tuple-element.27), channel_id=1, source_target_pairs={{0,3},{1,2},{2,1},{3,0},{4,7},{5,6},{6,5},{7,4},{8,11},{9,10},{10,... | collective-permute-start | bytes 147464 | tf_op jit(solution)/shard_map/cond/branch_1_fun/ppermute | solution.py:482
  107.4 21.3 %collective-permute-start.13 = (f32[258,768]{1,0:T(8,128)S(1)}, f32[258,768]{1,0:T(8,128)S(1)}, u32[]{:S(2)}, u32[]{:S(2)}) collective-permute-start(f32[258,768]{1,0:T(8,128)S(1)} %copy-done.13), channel_id=1, source_target_pairs={{0,1},{1,0},{2,3},{3,2},{4,5},{5,4},{6,7},{7,6},{8,9},{9,8},{10,11... | collective-permute-start | bytes 2377736 | tf_op jit(solution)/shard_map/ppermute | solution.py:534
  110.3 16.8 %collective-permute-start.16 = (f32[200,768]{1,0:T(8,128)S(1)}, f32[200,768]{1,0:T(8,128)S(1)}, u32[]{:S(2)}, u32[]{:S(2)}) collective-permute-start(f32[200,768]{1,0:T(8,128)S(1)} %get-tuple-element.207), channel_id=1, source_target_pairs={{0,4},{2,6},{4,0},{6,2},{8,12},{10,14},{12,8},{14,10},{16,20},{18,... | collective-permute-start | bytes 1843208 | tf_op jit(solution)/shard_map/ppermute | solution.py:414
  112.6 21.8 %collective-permute-start.23 = (f32[48,1536]{1,0:T(8,128)S(1)}, f32[48,1536]{1,0:T(8,128)S(1)}, u32[]{:S(2)}, u32[]{:S(2)}) collective-permute-start(f32[48,1536]{1,0:T(8,128)S(1)} %get-tuple-element.223), channel_id=1, source_target_pairs={{0,16},{2,18},{4,20},{6,22},{8,24},{10,26},{12,28},{14,30},{16,0},... | collective-permute-start | bytes 884744 | tf_op jit(solution)/shard_map/ppermute | solution.py:414
  117.3 22.5 %collective-permute-start.22 = (f32[96,1536]{1,0:T(8,128)S(1)}, f32[96,1536]{1,0:T(8,128)S(1)}, u32[]{:S(2)}, u32[]{:S(2)}) collective-permute-start(f32[96,1536]{1,0:T(8,128)S(1)} %get-tuple-element.222), channel_id=1, source_target_pairs={{0,8},{2,10},{4,12},{6,14},{8,0},{10,2},{12,4},{14,6},{16,24},{18,... | collective-permute-start | bytes 1769480 | tf_op jit(solution)/shard_map/ppermute | solution.py:414
  119.7 22.0 %collective-permute-start.21 = (f32[192,768]{1,0:T(8,128)S(1)}, f32[192,768]{1,0:T(8,128)S(1)}, u32[]{:S(2)}, u32[]{:S(2)}) collective-permute-start(f32[192,768]{1,0:T(8,128)S(1)} %get-tuple-element.221), channel_id=1, source_target_pairs={{0,4},{2,6},{4,0},{6,2},{8,12},{10,14},{12,8},{14,10},{16,20},{18,... | collective-permute-start | bytes 1769480 | tf_op jit(solution)/shard_map/ppermute | solution.py:414
  130.7 17.7 %collective-permute-start.20 = (f32[104,768]{1,0:T(8,128)S(1)}, f32[104,768]{1,0:T(8,128)S(1)}, u32[]{:S(2)}, u32[]{:S(2)}) collective-permute-start(f32[104,768]{1,0:T(8,128)S(1)} %get-tuple-element.220), channel_id=1, source_target_pairs={{0,8},{2,10},{4,12},{6,14},{8,0},{10,2},{12,4},{14,6},{16,24},{18,... | collective-permute-start | bytes 958472 | tf_op jit(solution)/shard_map/ppermute | solution.py:414
  131.2 36.2 %collective-permute-start.19 = (f32[528,768]{1,0:T(8,128)}, f32[528,768]{1,0:T(8,128)S(1)}, u32[]{:S(2)}, u32[]{:S(2)}) collective-permute-start(f32[528,768]{1,0:T(8,128)} %get-tuple-element.219.refs_0_), channel_id=1, source_target_pairs={{0,1},{1,0},{2,3},{3,2},{4,5},{5,4},{6,7},{7,6},{8,9},{9,8},{10,11... | collective-permute-start | bytes 4866056 | tf_op jit(solution)/shard_map/ppermute | solution.py:534
  141.6 17.1 %collective-permute-start.26 = (f32[48,1536]{1,0:T(8,128)S(1)}, f32[48,1536]{1,0:T(8,128)S(1)}, u32[]{:S(2)}, u32[]{:S(2)}) collective-permute-start(f32[48,1536]{1,0:T(8,128)S(1)} %get-tuple-element.230), channel_id=1, source_target_pairs={{0,16},{2,18},{4,20},{6,22},{8,24},{10,26},{12,28},{14,30},{16,0},... | collective-permute-start | bytes 884744 | tf_op jit(solution)/shard_map/ppermute | solution.py:414
  141.7 19.5 %copy-start.14 = (f32[192,768]{1,0:T(8,128)}, f32[192,768]{1,0:T(8,128)S(1)}, u32[]{:S(2)}) copy-start(f32[192,768]{1,0:T(8,128)S(1)} %collective-permute-done.21.refs_3_) | copy-start | bytes 1769476
  143.4 17.8 %collective-permute-start.25 = (f32[96,768]{1,0:T(8,128)S(1)}, f32[96,768]{1,0:T(8,128)S(1)}, u32[]{:S(2)}, u32[]{:S(2)}) collective-permute-start(f32[96,768]{1,0:T(8,128)S(1)} %get-tuple-element.229), channel_id=1, source_target_pairs={{0,8},{2,10},{4,12},{6,14},{8,0},{10,2},{12,4},{14,6},{16,24},{18,... | collective-permute-start | bytes 884744 | tf_op jit(solution)/shard_map/ppermute | solution.py:414
  149.9 13.5 %collective-permute-start.24 = (f32[56,768]{1,0:T(8,128)S(1)}, f32[56,768]{1,0:T(8,128)S(1)}, u32[]{:S(2)}, u32[]{:S(2)}) collective-permute-start(f32[56,768]{1,0:T(8,128)S(1)} %get-tuple-element.228), channel_id=1, source_target_pairs={{0,16},{2,18},{4,20},{6,22},{8,24},{10,26},{12,28},{14,30},{16,0},... | collective-permute-start | bytes 516104 | tf_op jit(solution)/shard_map/ppermute | solution.py:414
  162.8 7.7 %collective-permute-start.27 = (f32[48,768]{1,0:T(8,128)S(1)}, f32[48,768]{1,0:T(8,128)S(1)}, u32[]{:S(2)}, u32[]{:S(2)}) collective-permute-start(f32[48,768]{1,0:T(8,128)S(1)} %get-tuple-element.239), channel_id=1, source_target_pairs={{0,16},{2,18},{4,20},{6,22},{8,24},{10,26},{12,28},{14,30},{16,0},... | collective-permute-start | bytes 442376 | tf_op jit(solution)/shard_map/ppermute | solution.py:414
  163.4 3.9 %copy-start.10 = (f32[258,768]{1,0:T(8,128)S(1)}, f32[258,768]{1,0:T(8,128)}, u32[]{:S(2)}) copy-start(f32[258,768]{1,0:T(8,128)} %get-tuple-element.166.refs_2_.refs_3_) | copy-start | bytes 2377732
  (4 other events, 7.1 us)

commit v4 on v3

--- a/solution.py
+++ b/solution.py
@@ -183,7 +183,7 @@
     second_out[...] = second
     grad = dy[...].astype(BF16)
     small_out[...] = jnp.zeros_like(small_out)
-    chunk = 512
+    chunk = 768
     biases = line(up_bias)
     norm = jnp.zeros((rows, width), F32)
     for start in range(0, up.shape[1], chunk):
@@ -299,7 +299,7 @@
     even = ids[0] == 0
 
     def turn(value, start):
-        columns = value.astype(F32).T
+        columns = value.T
         stop = start + value.shape[0]
         for place in range(8):
             source = 0
@@ -622,8 +622,8 @@
         )[0]
 
     out_sum.step()
+    up_sum.step()
     down_sum.step()
-    up_sum.step()
     qkv_sum.step()
     input_grads = [input_of(b) for b in range(images - 1)]
     out_sum.step()
@@ -640,7 +640,7 @@
     args = [down_part, down_other, down_bias, *middles]
     (output,) = chain.call(
         partial(output_body, images), args, [whole(a) for a in args],
-        [shape((images, rows, width), BF16)], 32, "output", deep=(2,),
+        [shape((images, rows, width), BF16)], 32, "output", deep=(2, 3, 4),
     )
     (qkv_total,) = qkv_sum.finish()
     small = small[:, :width]

time: 175 us -> 174 us (level)
  waiting for transfers between devices: 33 us -> 27.6 us
  starting transfers between devices: 25.7 us -> 30.8 us
    ppermute x12, waiting for transfers between devices: 19.5 us -> 12.8 us  [step(): lax.ppermute(send, 'dp', flips(self.dp, bit))]
    ppermute x12, starting transfers between devices: 10.7 us -> 15.8 us  [step(): lax.ppermute(send, 'dp', flips(self.dp, bit))]
    unnamed x51 -> x47, local copies, waits for them, and re-layouts: 5.98 us -> 4.83 us
  transfers between devices with their start and end apart: 28 -> 28, of which waited for: 15 -> 13; matrix products, arithmetic and copies ran while one was open for 2% -> 2% of each run, Pallas kernels for 59% -> 60%
where the time goes in v4:
time: 174 us; the launch traced here: 173 us
  Pallas kernels  105 us (60%)
  starting transfers between devices  30.8 us (18%)
  waiting for transfers between devices  27.6 us (16%)
  local copies, waits for them, and re-layouts  6.83 us (4%)
  other arithmetic  1.83 us (1%)
    pallas_call x30, Pallas kernels, kernel(): pl.pallas_call(body, out_shape=tuple(outs), grid_spec=pltpu.PrefetchScala...  105 us
    ppermute x12, starting transfers between devices, step(): lax.ppermute(send, 'dp', flips(self.dp, bit))  15.8 us
    ppermute x12, waiting for transfers between devices, step(): lax.ppermute(send, 'dp', flips(self.dp, bit))  12.8 us
    ppermute x8, starting transfers between devices, per_device(): across = lambda v: lax.ppermute(v, 'mp', SWAP)  10.9 us
    ppermute x3, waiting for transfers between devices, weight_sum(): swap = lambda v: lax.ppermute(v, 'dp', flips(dp, 0))  7.16 us
    unnamed x47, local copies, waits for them, and re-layouts  4.83 us
  transfers between devices with their start and end apart: 28, of which 13 were waited for; matrix products, arithmetic and copies ran while one was open for 2% of the time, Pallas kernels for 60%

profile of v4, /device:TPU:0, one launch (start us, length us, event | category | flops | bytes accessed | tf_op | source)
XLA Modules:
  0.0 172.8 jit_solution(17502255617913185473)
XLA Ops:
  1.6 3.0 %collective-permute-start.8 = (f32[96,768]{1,0:T(8,128)S(1)}, f32[96,768]{1,0:T(8,128)}, u32[]{:S(2)}, u32[]{:S(2)}) collective-permute-start(f32[96,768]{1,0:T(8,128)S(1)} %dynamic-slice_convert_fusion), channel_id=1, source_target_pairs={{0,1},{1,0},{2,3},{3,2},{4,5},{5,4},{6,7},{7,6},{8,9},{9,8},{10,11... | collective-permute-start | bytes 884744 | tf_op jit(solution)/shard_map/ppermute | solution.py:534
  4.6 6.1 %attend0.1 = (f32[258,768]{1,0:T(8,128)}, bf16[258,768]{1,0:T(8,128)(2,1)}, bf16[258,1152]{1,0:T(8,128)(2,1)}, f32[258,128]{1,0:T(8,128)}, f32[258,384]{1,0:T(8,128)S(1)}, /*index=5*/f32[8,128]{1,0:T(8,128)S(1)}) custom-call(s32[2,256]{1,0:T(2,128)} %refs_0_.5, bf16[2,1024,768]{2,1,0:T(8,128)(2,1)} %refs_1_.5, bf16[2,2,768]{2,1,0:T(2,128)(2,1)} %refs_2_.7, ...), custom_call_target="tpu_custom_call" | custom-call | flops 2147483648 | bytes 1 | tf_op jit(solution)/shard_map/attend0/pallas_call | solution.py:70
  11.7 1.7 collective-permute-start.9
  15.2 6.4 %attend1.1 = (f32[258,768]{1,0:T(8,128)}, bf16[258,768]{1,0:T(8,128)(2,1)}, bf16[258,1152]{1,0:T(8,128)(2,1)}, f32[258,128]{1,0:T(8,128)}, f32[258,384]{1,0:T(8,128)S(1)}, /*index=5*/f32[8,128]{1,0:T(8,128)S(1)}) custom-call(s32[2,256]{1,0:T(2,128)} %refs_0_.5, bf16[2,1024,768]{2,1,0:T(8,128)(2,1)} %refs_1_.5, bf16[2,2,768]{2,1,0:T(2,128)(2,1)} %refs_2_.7, ...), custom_call_target="tpu_custom_call" | custom-call | flops 2147483648 | bytes 1 | tf_op jit(solution)/shard_map/attend1/pallas_call | solution.py:70
  22.1 2.3 %conditional.4 = (f32[96,768]{1,0:T(8,128)}, f32[96,768]{1,0:T(8,128)}) conditional(s32[]{:T(128)} %bitcast.5, () %tuple.43, (f32[96,768]{1,0:T(8,128)}, f32[96,768]{1,0:T(8,128)}) %tuple.44), branch_computations={%region_0.1_spmd, %region_1.2_spmd} | conditional | bytes 2359392 | solution.py:110
  27.2 5.6 %forward0.1 = (f32[258,768]{1,0:T(8,128)}, bf16[258,768]{1,0:T(8,128)(2,1)}, bf16[258,1536]{1,0:T(8,128)(2,1)}, bf16[258,1536]{1,0:T(8,128)(2,1)}, f32[258,768]{...) custom-call(s32[5]{0:T(128)S(1)} %stack.44.refs_0_, f32[258,768]{1,0:T(8,128)} %get-tuple-element.143.refs_1_.refs_5_, ...), custom_call_target="tpu_custom_call" | custom-call | flops 2147483648 | bytes 1 | tf_op jit(solution)/shard_map/forward0/pallas_call | solution.py:70
  34.3 5.6 %forward1.1 = (f32[258,768]{1,0:T(8,128)}, bf16[258,768]{1,0:T(8,128)(2,1)}, bf16[258,1536]{1,0:T(8,128)(2,1)}, bf16[258,1536]{1,0:T(8,128)(2,1)}, f32[258,768]{...) custom-call(s32[5]{0:T(128)S(1)} %stack.44.refs_0_, f32[258,768]{1,0:T(8,128)} %get-tuple-element.154.refs_1_.refs_5_, ...), custom_call_target="tpu_custom_call" | custom-call | flops 2147483648 | bytes 1 | tf_op jit(solution)/shard_map/forward1/pallas_call | solution.py:70
  40.0 5.7 %down_grads.1 = (f32[384,1536]{1,0:T(8,128)}, f32[384,1536]{1,0:T(8,128)}, f32[8,128]{1,0:T(8,128)S(1)}) custom-call(s32[5]{0:T(128)S(1)} %stack.44.refs_0_, bf16[2,258,768]{2,1,0:T(8,128)(2,1)} %copy-done.1, bf16[2,258,768]{2,1,0:T(8,128)(2,1)} %copy-done.1, bf16[258,1536]{1,0:T(8,128)(2,1)} %get-tuple-element.153.refs_3_, ...), custom_call_target="tpu_custom_call" | custom-call | flops 2147483648 | bytes 1 | tf_op jit(solution)/shard_map/down_grads/pallas_call | solution.py:70
  46.3 4.9 %conditional.5 = (f32[384,1536]{1,0:T(8,128)}, f32[528,768]{1,0:T(8,128)}) conditional(s32[]{:T(128)} %bitcast.5, () %tuple.41, (f32[384,1536]{1,0:T(8,128)}, bf16[258,1536]{1,0:T(8,128)(2,1)S(1)}, bf16[258,1536]{1,0:T(8,128)(2,1)S(1)}, bf16[1536,768]{1,0:T(8,128)(2,1)S(1)}) %tuple.70), branch_computations={%region_2.3_spmd, %region_3.4_spmd} | conditional | flops 2147483648 | bytes 9437241 | solution.py:110
  46.3 2.7 %branch.1 = f32[528,768]{1,0:T(8,128)} custom-call(bf16[258,1536]{1,0:T(8,128)(2,1)S(1)} %get-tuple-element.23.refs_0_, bf16[258,1536]{1,0:T(8,128)(2,1)S(1)} %get-tuple-element.24.refs_1_, bf16[1536,768]{1,0:T(8,128)(2,1)S(1)} %get-tuple-element.25.refs_2_), custom_call_target="tpu_custom_call" | custom-call | flops 2147483648 | bytes 1 | tf_op jit(solution)/shard_map/cond/branch_1_fun/branch/pallas_call | solution.py:70
  48.9 2.2 %collective-permute-done.2 = f32[384,1536]{1,0:T(8,128)} collective-permute-done((f32[384,1536]{1,0:T(8,128)}, f32[384,1536]{1,0:T(8,128)}, u32[]{:S(2)}, u32[]{:S(2)}) %collective-permute-start.2) | collective-permute-done | bytes 2359328 | tf_op jit(solution)/shard_map/cond/branch_1_fun/ppermute | solution.py:478
  51.2 3.5 %down0_step1.1 = (f32[192,1536]{1,0:T(8,128)}, f32[8,128]{1,0:T(8,128)S(1)}) custom-call(s32[5]{0:T(128)S(1)} %stack.44.refs_0_, f32[384,1536]{1,0:T(8,128)} %get-tuple-element.169.refs_1_, f32[384,1536]{1,0:T(8,128)} %get-tuple-element.170.refs_2_, f32[8,128]{1,0:T(8,128)S(1)} %get-tuple-element.171.refs_3_), custom_call_target="tpu_custom_call" | custom-call | flops 2147483648 | bytes 1 | tf_op jit(solution)/shard_map/down0_step1/pallas_call | solution.py:70
  55.0 9.1 %backward0.1 = (f32[258,768]{1,0:T(8,128)}, bf16[258,768]{1,0:T(8,128)(2,1)}, bf16[258,1152]{1,0:T(8,128)(2,1)}, f32[258,768]{1,0:T(8,128)}, f32[8,768]{1,0:T(8,...) custom-call(f32[258,768]{1,0:T(8,128)} %get-tuple-element.165.refs_0_, f32[258,768]{1,0:T(8,128)} %collective-permute-done.12.refs_1_, ...), custom_call_target="tpu_custom_call" | custom-call | flops 8589934592 | bytes 1 | tf_op jit(solution)/shard_map/backward0/pallas_call | solution.py:70
  64.1 1.7 %collective-permute-start.15 = (f32[258,768]{1,0:T(8,128)}, f32[258,768]{1,0:T(8,128)}, u32[]{:S(2)}, u32[]{:S(2)}) collective-permute-start(f32[258,768]{1,0:T(8,128)} %get-tuple-element.197.refs_2_), channel_id=1, source_target_pairs={{0,1},{1,0},{2,3},{3,2},{4,5},{5,4},{6,7},{7,6},{8,9},{9,8},{10,11... | collective-permute-start | bytes 2377736 | tf_op jit(solution)/shard_map/ppermute | solution.py:534
  65.8 5.5 %up_grads.1 = (f32[384,1536]{1,0:T(8,128)}, f32[384,1536]{1,0:T(8,128)}, f32[8,128]{1,0:T(8,128)S(1)}) custom-call(s32[5]{0:T(128)S(1)} %stack.44.refs_0_, bf16[258,768]{1,0:T(8,128)(2,1)} %get-tuple-element.174.refs_1_, bf16[258,768]{1,0:T(8,128)(2,1)} %get-tuple-element.175.refs_2_, bf16[258,1536]{1,0:T(8,128)(2,1)} %get-tuple-element.176.refs_3_, ...), custom_call_target="tpu_custom_call" | custom-call | flops 2147483648 | bytes 1 | tf_op jit(solution)/shard_map/up_grads/pallas_call | solution.py:70
  71.4 4.9 %conditional.6 = (f32[384,1536]{1,0:T(8,128)}) conditional(s32[]{:T(128)} %bitcast.5, () %tuple.46, f32[384,1536]{1,0:T(8,128)} %get-tuple-element.180), branch_computations={%region_4.5_spmd, %region_5.6_spmd} | conditional | bytes 9437232 | solution.py:110
  71.4 4.9 %collective-permute-done.3 = f32[384,1536]{1,0:T(8,128)} collective-permute-done((f32[384,1536]{1,0:T(8,128)}, f32[384,1536]{1,0:T(8,128)}, u32[]{:S(2)}, u32[]{:S(2)}) %collective-permute-start.3) | collective-permute-done | bytes 2359328 | tf_op jit(solution)/shard_map/cond/branch_1_fun/ppermute | solution.py:478
  76.2 3.3 %up0_step1.1 = (f32[192,1536]{1,0:T(8,128)}, f32[8,128]{1,0:T(8,128)S(1)}) custom-call(s32[5]{0:T(128)S(1)} %stack.44.refs_0_, f32[384,1536]{1,0:T(8,128)} %get-tuple-element.179.refs_1_, f32[384,1536]{1,0:T(8,128)} %get-tuple-element.282.refs_2_, f32[8,128]{1,0:T(8,128)S(1)} %get-tuple-element.181.refs_3_), custom_call_target="tpu_custom_call" | custom-call | flops 2147483648 | bytes 1 | tf_op jit(solution)/shard_map/up0_step1/pallas_call | solution.py:70
  81.1 8.6 %backward1.1 = (f32[258,768]{1,0:T(8,128)}, bf16[258,768]{1,0:T(8,128)(2,1)}, bf16[258,1152]{1,0:T(8,128)(2,1)}, f32[258,768]{1,0:T(8,128)S(1)}, f32[8,768]{1,0:...) custom-call(f32[258,768]{1,0:T(8,128)} %get-tuple-element.161.refs_0_, ...), custom_call_target="tpu_custom_call" | custom-call | flops 8589934592 | bytes 1 | tf_op jit(solution)/shard_map/backward1/pallas_call | solution.py:70
  89.8 2.8 %down0_step2.1 = (f32[96,1536]{1,0:T(8,128)}, f32[8,128]{1,0:T(8,128)S(1)}) custom-call(s32[5]{0:T(128)S(1)} %stack.44.refs_0_, f32[384,1536]{1,0:T(8,128)} %get-tuple-element.169.refs_1_, f32[384,1536]{1,0:T(8,128)} %get-tuple-element.170.refs_2_, f32[192,1536]{1,0:T(8,128)S(1)} %collective-permute-done.14.refs_3_, f32[8,128]{1,0:T(8,128)S(1)} %get-tuple-element.199.refs_4_), custom_call_target="tpu_custom_call" | custom-call | flops 2147483648 | bytes 1 | tf_op jit(solution)/shard_map/down0_step2/pallas_call | solution.py:70
  92.6 1.6 collective-permute-start.17
  94.2 7.5 %last_grads.1 = (f32[392,1536]{1,0:T(8,128)}, f32[392,1536]{1,0:T(8,128)}, f32[8,128]{1,0:T(8,128)S(1)}) custom-call(s32[5]{0:T(128)S(1)} %stack.44.refs_0_, bf16[258,768]{1,0:T(8,128)(2,1)} %get-tuple-element.185.refs_1_, bf16[258,768]{1,0:T(8,128)(2,1)} %get-tuple-element.186.refs_2_, f32[258,384]{1,0:T(8,128)} %copy-done.3, f32[258,384]{1,0:T(8,128)} %copy-done.4, ...), custom_call_target="tpu_custom_call" | custom-call | flops 2147483648 | bytes 1 | tf_op jit(solution)/shard_map/last_grads/pallas_call | solution.py:70
  101.7 5.0 %conditional.7 = (f32[392,1536]{1,0:T(8,128)}, f32[8,1536]{1,0:T(8,128)}, f32[8,1536]{1,0:T(8,128)}) conditional(s32[]{:T(128)} %bitcast.5, () %tuple.48, (f32[392,1536]{1,0:T(8,128)}, f32[8,1536]{1,0:T(8,128)S(1)}) %tuple.49), branch_computations={%region_6.7_spmd, %region_7.8_spmd} | conditional | bytes 10027152 | solution.py:110
  103.6 2.9 %collective-permute-done.5 = f32[8,1536]{1,0:T(8,128)} collective-permute-done((f32[8,1536]{1,0:T(8,128)S(1)}, f32[8,1536]{1,0:T(8,128)}, u32[]{:S(2)}, u32[]{:S(2)}) %collective-permute-start.5) | collective-permute-done | bytes 49184 | tf_op jit(solution)/shard_map/cond/branch_1_fun/ppermute | solution.py:482
  107.7 1.9 %last0_step1.1 = (f32[200,768]{1,0:T(8,128)S(1)}, f32[8,128]{1,0:T(8,128)S(1)}) custom-call(s32[5]{0:T(128)S(1)} %stack.44.refs_0_, f32[392,1536]{1,0:T(8,128)} %get-tuple-element.201.refs_1_.refs_3_.refs_4_.refs_5_.refs_6_, f32[392,1536]{1,0:T(8,128)} %get-tuple-element.203.refs_2_.refs_4_.refs_5_.refs_6_.refs_7_, ...), custom_call_target="tpu_custom_call" | custom-call | flops 2147483648 | bytes 1 | tf_op jit(solution)/shard_map/last0_step1/pallas_call | solution.py:70
  110.1 2.1 %up0_step2.1 = (f32[96,1536]{1,0:T(8,128)S(1)}, f32[8,128]{1,0:T(8,128)S(1)}) custom-call(s32[5]{0:T(128)S(1)} %stack.44.refs_0_, f32[384,1536]{1,0:T(8,128)} %get-tuple-element.179.refs_1_, f32[384,1536]{1,0:T(8,128)} %get-tuple-element.282.refs_2_, f32[192,1536]{1,0:T(8,128)} %collective-permute-done.18.refs_3_, f32[8,128]{1,0:T(8,128)S(1)} %get-tuple-element.212.refs_4_), custom_call_target="tpu_custom_call" | custom-call | flops 2147483648 | bytes 1 | tf_op jit(solution)/shard_map/up0_step2/pallas_call | solution.py:70
  112.7 1.8 %down0_step3.1 = (f32[48,1536]{1,0:T(8,128)S(1)}, f32[8,128]{1,0:T(8,128)S(1)}) custom-call(s32[5]{0:T(128)S(1)} %stack.44.refs_0_, f32[384,1536]{1,0:T(8,128)} %get-tuple-element.169.refs_1_, f32[384,1536]{1,0:T(8,128)} %get-tuple-element.170.refs_2_, f32[192,1536]{1,0:T(8,128)S(1)} %collective-permute-done.14.refs_3_, ...), custom_call_target="tpu_custom_call" | custom-call | flops 2147483648 | bytes 1 | tf_op jit(solution)/shard_map/down0_step3/pallas_call | solution.py:70
  114.5 2.7 %collective-permute-start.23 = (f32[48,1536]{1,0:T(8,128)S(1)}, f32[48,1536]{1,0:T(8,128)S(1)}, u32[]{:S(2)}, u32[]{:S(2)}) collective-permute-start(f32[48,1536]{1,0:T(8,128)S(1)} %get-tuple-element.223), channel_id=1, source_target_pairs={{0,16},{2,18},{4,20},{6,22},{8,24},{10,26},{12,28},{14,30},{16,0},... | collective-permute-start | bytes 884744 | tf_op jit(solution)/shard_map/ppermute | solution.py:414
  117.1 1.9 %last1_step1.1 = (f32[192,768]{1,0:T(8,128)S(1)}, f32[8,128]{1,0:T(8,128)S(1)}) custom-call(s32[5]{0:T(128)S(1)} %stack.44.refs_0_, f32[392,1536]{1,0:T(8,128)} %get-tuple-element.201.refs_1_.refs_3_.refs_4_.refs_5_.refs_6_, f32[392,1536]{1,0:T(8,128)} %get-tuple-element.203.refs_2_.refs_4_.refs_5_.refs_6_.refs_7_, f32[8,128]{1,0:T(8,128)S(1)} %get-tuple-element.214.refs_3_), custom_call_target="tpu_custom_call" | custom-call | flops 2147483648 | bytes 1 | tf_op jit(solution)/shard_map/last1_step1/pallas_call | solution.py:70
  120.6 2.4 %input0.1 = (f32[258,768]{1,0:T(8,128)S(1)}, f32[8,128]{1,0:T(8,128)S(1)}) custom-call(f32[768]{0:T(1024)} %refs_0_.7, f32[258,768]{1,0:T(8,128)} %get-tuple-element.143.refs_1_.refs_5_, f32[258,768]{1,0:T(8,128)} %get-tuple-element.197.refs_2_, f32[258,768]{1,0:T(8,128)} %collective-permute-done.15.refs_3_, f32[258,768]{1,0:T(8,128)} %get-tuple-element.209.refs_4_, ...), custom_call_target="tpu_custom_call" | custom-call | flops 2147483648 | bytes 1 | tf_op jit(solution)/shard_map/input0/pallas_call | solution.py:70
  122.9 3.3 %collective-permute-done.16.refs_3_.refs_8_.refs_9_.refs_10_ = f32[200,768]{1,0:T(8,128)S(1)} collective-permute-done((f32[200,768]{1,0:T(8,128)S(1)}, f32[200,768]{1,0:T(8,128)S(1)}, u32[]{:S(2)}, u32[]{:S(2)}) %collective-permute-start.16) | collective-permute-done | bytes 614432 | tf_op jit(solution)/shard_map/ppermute | solution.py:414
  126.3 1.7 last0_step2.1
  128.0 1.9 %input1.1 = (f32[258,768]{1,0:T(8,128)S(1)}, f32[8,128]{1,0:T(8,128)S(1)}) custom-call(f32[768]{0:T(1024)} %refs_0_.7, f32[258,768]{1,0:T(8,128)} %get-tuple-element.154.refs_1_.refs_5_, f32[258,768]{1,0:T(8,128)S(1)} %copy-done.11, f32[258,768]{1,0:T(8,128)S(1)} %collective-permute-done.13.refs_3_, f32[258,768]{1,0:T(8,128)} %get-tuple-element.184.refs_4_, ...), custom_call_target="tpu_custom_call" | custom-call | flops 2147483648 | bytes 1 | tf_op jit(solution)/shard_map/input1/pallas_call | solution.py:70
  131.7 2.0 %copy.35 = f32[2,258,768]{2,0,1:T(2,128)} copy(f32[2,258,768]{2,1,0:T(8,128)S(1)} %pad_maximum_fusion) | data formatting | bytes 3170304
  133.6 2.5 %down0_last.1 = (f32[48,1536]{1,0:T(8,128)}, f32[8,128]{1,0:T(8,128)S(1)}) custom-call(s32[5]{0:T(128)S(1)} %stack.44.refs_0_, f32[384,1536]{1,0:T(8,128)} %get-tuple-element.169.refs_1_, f32[384,1536]{1,0:T(8,128)} %get-tuple-element.170.refs_2_, f32[192,1536]{1,0:T(8,128)S(1)} %copy-done.9, f32[96,1536]{1,0:T(8,128)} %collective-permute-done.17.refs_4_, ...), custom_call_target="tpu_custom_call" | custom-call | flops 2147483648 | bytes 1 | tf_op jit(solution)/shard_map/down0_last/pallas_call | solution.py:70
  136.1 1.8 %up0_step3.1 = (f32[48,1536]{1,0:T(8,128)S(1)}, f32[8,128]{1,0:T(8,128)S(1)}) custom-call(s32[5]{0:T(128)S(1)} %stack.44.refs_0_, f32[384,1536]{1,0:T(8,128)} %get-tuple-element.179.refs_1_, f32[384,1536]{1,0:T(8,128)} %get-tuple-element.282.refs_2_, f32[192,1536]{1,0:T(8,128)} %collective-permute-done.18.refs_3_, ...), custom_call_target="tpu_custom_call" | custom-call | flops 2147483648 | bytes 1 | tf_op jit(solution)/shard_map/up0_step3/pallas_call | solution.py:70
  137.9 2.7 %collective-permute-start.26 = (f32[48,1536]{1,0:T(8,128)S(1)}, f32[48,1536]{1,0:T(8,128)S(1)}, u32[]{:S(2)}, u32[]{:S(2)}) collective-permute-start(f32[48,1536]{1,0:T(8,128)S(1)} %get-tuple-element.230), channel_id=1, source_target_pairs={{0,16},{2,18},{4,20},{6,22},{8,24},{10,26},{12,28},{14,30},{16,0},... | collective-permute-start | bytes 884744 | tf_op jit(solution)/shard_map/ppermute | solution.py:414
  140.6 1.7 last1_step2.1
  142.2 1.6 collective-permute-start.25
  144.2 1.6 last0_step3.1
  145.8 2.2 %collective-permute-start.24 = (f32[56,768]{1,0:T(8,128)S(1)}, f32[56,768]{1,0:T(8,128)S(1)}, u32[]{:S(2)}, u32[]{:S(2)}) collective-permute-start(f32[56,768]{1,0:T(8,128)S(1)} %get-tuple-element.228), channel_id=1, source_target_pairs={{0,16},{2,18},{4,20},{6,22},{8,24},{10,26},{12,28},{14,30},{16,0},... | collective-permute-start | bytes 516104 | tf_op jit(solution)/shard_map/ppermute | solution.py:414
  148.0 8.3 %collective-permute-done.26.refs_5_ = f32[48,1536]{1,0:T(8,128)S(1)} collective-permute-done((f32[48,1536]{1,0:T(8,128)S(1)}, f32[48,1536]{1,0:T(8,128)S(1)}, u32[]{:S(2)}, u32[]{:S(2)}) %collective-permute-start.26) | collective-permute-done | bytes 294944 | tf_op jit(solution)/shard_map/ppermute | solution.py:414
  156.3 2.5 %up0_last.1 = (f32[48,1536]{1,0:T(8,128)}, f32[8,128]{1,0:T(8,128)S(1)}) custom-call(s32[5]{0:T(128)S(1)} %stack.44.refs_0_, f32[384,1536]{1,0:T(8,128)} %get-tuple-element.179.refs_1_, f32[384,1536]{1,0:T(8,128)} %get-tuple-element.282.refs_2_, f32[192,1536]{1,0:T(8,128)} %collective-permute-done.18.refs_3_, ...), custom_call_target="tpu_custom_call" | custom-call | flops 2147483648 | bytes 1 | tf_op jit(solution)/shard_map/up0_last/pallas_call | solution.py:70
  158.8 1.6 last1_step3.1
  161.3 1.6 last0_last.1
  164.8 1.8 %collective-permute-done.19.refs_1_ = f32[528,768]{1,0:T(8,128)S(1)} collective-permute-done((f32[528,768]{1,0:T(8,128)}, f32[528,768]{1,0:T(8,128)S(1)}, u32[]{:S(2)}, u32[]{:S(2)}) %collective-permute-start.19) | collective-permute-done | bytes 1622048 | tf_op jit(solution)/shard_map/ppermute | solution.py:534
  166.6 2.3 %output.1 = (bf16[2,258,768]{2,1,0:T(8,128)(2,1)S(1)}, f32[8,128]{1,0:T(8,128)S(1)}) custom-call(f32[528,768]{1,0:T(8,128)} %get-tuple-element.219.refs_0_, f32[528,768]{1,0:T(8,128)S(1)} %collective-permute-done.19.refs_1_, f32[768]{0:T(1024)} %refs_2_.8, f32[258,768]{1,0:T(8,128)} %get-tuple-element.166.refs_2_.refs_3_, ...), custom_call_target="tpu_custom_call" | custom-call | flops 2147483648 | bytes 1 | tf_op jit(solution)/shard_map/output/pallas_call | solution.py:70
  169.0 1.6 last1_last.1
  (100 shorter events, 26.1 us)
Async XLA Ops:
  1.6 10.1 %collective-permute-start.8 = (f32[96,768]{1,0:T(8,128)S(1)}, f32[96,768]{1,0:T(8,128)}, u32[]{:S(2)}, u32[]{:S(2)}) collective-permute-start(f32[96,768]{1,0:T(8,128)S(1)} %dynamic-slice_convert_fusion), channel_id=1, source_target_pairs={{0,1},{1,0},{2,3},{3,2},{4,5},{5,4},{6,7},{7,6},{8,9},{9,8},{10,11... | collective-permute-start | bytes 884744 | tf_op jit(solution)/shard_map/ppermute | solution.py:534
  4.6 10.5 %copy-start.19 = (bf16[2,258,768]{2,0,1:T(2,128)(2,1)S(1)}, bf16[2,258,768]{2,0,1:T(2,128)(2,1)}, u32[]{:S(2)}) copy-start(bf16[2,258,768]{2,0,1:T(2,128)(2,1)} %param.37) | copy-start | bytes 2377732
  10.8 15.2 %copy-start.3 = (f32[258,384]{1,0:T(8,128)}, f32[258,384]{1,0:T(8,128)S(1)}, u32[]{:S(2)}) copy-start(f32[258,384]{1,0:T(8,128)S(1)} %get-tuple-element.144.refs_7_.refs_3_) | copy-start | bytes 1188868
  11.7 10.4 %collective-permute-start.9 = (f32[96,768]{1,0:T(8,128)}, f32[96,768]{1,0:T(8,128)}, u32[]{:S(2)}, u32[]{:S(2)}) collective-permute-start(f32[96,768]{1,0:T(8,128)} %collective-permute-done.8.refs_2_), channel_id=1, source_target_pairs={{0,4},{2,6},{4,0},{6,2},{8,12},{10,14},{12,8},{14,10},{16,20},{18,... | collective-permute-start | bytes 884744 | tf_op jit(solution)/shard_map/ppermute | solution.py:558
  13.5 12.5 %collective-permute-start.7 = (f32[258,384]{1,0:T(8,128)S(1)}, f32[258,384]{1,0:T(8,128)S(1)}, u32[]{:S(2)}, u32[]{:S(2)}) collective-permute-start(f32[258,384]{1,0:T(8,128)S(1)} %get-tuple-element.144.refs_7_.refs_3_), channel_id=1, source_target_pairs={{0,1},{1,0},{2,3},{3,2},{4,5},{5,4},{6,7},{7,6},{8,9},{9,8},{10,11... | collective-permute-start | bytes 1188872 | tf_op jit(solution)/shard_map/ppermute | solution.py:534
  15.2 19.1 %copy-start.1 = (bf16[2,258,768]{2,1,0:T(8,128)(2,1)}, bf16[2,258,768]{2,1,0:T(8,128)(2,1)S(1)}, u32[]{:S(2)}) copy-start(bf16[2,258,768]{2,1,0:T(8,128)(2,1)S(1)} %copy.30.refs_2_.refs_1_.refs_6_) | copy-start | bytes 2377732
  15.2 9.2 %copy-start.5 = (bf16[384,768]{1,0:T(8,128)(2,1)S(1)}, bf16[384,768]{1,0:T(8,128)(2,1)}, u32[]{:S(2)}) copy-start(bf16[384,768]{1,0:T(8,128)(2,1)} %refs_8_.3) | copy-start | bytes 1769476
  21.6 12.7 %copy-start.4 = (f32[258,384]{1,0:T(8,128)}, f32[258,384]{1,0:T(8,128)S(1)}, u32[]{:S(2)}) copy-start(f32[258,384]{1,0:T(8,128)S(1)} %get-tuple-element.155.refs_7_.refs_4_) | copy-start | bytes 1188868
  21.6 12.7 %collective-permute-start.10 = (f32[258,384]{1,0:T(8,128)S(1)}, f32[258,384]{1,0:T(8,128)S(1)}, u32[]{:S(2)}, u32[]{:S(2)}) collective-permute-start(f32[258,384]{1,0:T(8,128)S(1)} %get-tuple-element.155.refs_7_.refs_4_), channel_id=1, source_target_pairs={{0,1},{1,0},{2,3},{3,2},{4,5},{5,4},{6,7},{7,6},{8,9},{9,8},{10,11... | collective-permute-start | bytes 1188872 | tf_op jit(solution)/shard_map/ppermute | solution.py:534
  22.1 1.9 %collective-permute-start = (f32[96,768]{1,0:T(8,128)}, f32[96,768]{1,0:T(8,128)}, u32[]{:S(2)}, u32[]{:S(2)}) collective-permute-start(f32[96,768]{1,0:T(8,128)} %get-tuple-element.20), channel_id=1, source_target_pairs={{0,2},{2,0},{4,6},{6,4},{8,10},{10,8},{12,14},{14,12},{16,18},{18,... | collective-permute-start | bytes 884744 | tf_op jit(solution)/shard_map/cond/branch_1_fun/ppermute | solution.py:559
  22.1 2.3 %collective-permute-start.1 = (f32[96,768]{1,0:T(8,128)}, f32[96,768]{1,0:T(8,128)}, u32[]{:S(2)}, u32[]{:S(2)}) collective-permute-start(f32[96,768]{1,0:T(8,128)} %get-tuple-element.21), channel_id=1, source_target_pairs={{0,2},{2,0},{4,6},{6,4},{8,10},{10,8},{12,14},{14,12},{16,18},{18,... | collective-permute-start | bytes 884744 | tf_op jit(solution)/shard_map/cond/branch_1_fun/ppermute | solution.py:559
  24.5 2.7 %copy-start.18 = (bf16[1536,768]{1,0:T(8,128)(2,1)S(1)}, bf16[1536,768]{1,0:T(8,128)(2,1)}, u32[]{:S(2)}) copy-start(bf16[1536,768]{1,0:T(8,128)(2,1)} %refs_11_.3) | copy-start | bytes 7077892
  32.8 22.2 %collective-permute-start.12 = (f32[258,768]{1,0:T(8,128)}, f32[258,768]{1,0:T(8,128)}, u32[]{:S(2)}, u32[]{:S(2)}) collective-permute-start(f32[258,768]{1,0:T(8,128)} %get-tuple-element.165.refs_0_), channel_id=1, source_target_pairs={{0,1},{1,0},{2,3},{3,2},{4,5},{5,4},{6,7},{7,6},{8,9},{9,8},{10,11... | collective-permute-start | bytes 2377736 | tf_op jit(solution)/shard_map/ppermute | solution.py:534
  40.0 5.7 %copy-start.20 = (bf16[258,1536]{1,0:T(8,128)(2,1)S(1)}, bf16[258,1536]{1,0:T(8,128)(2,1)}, u32[]{:S(2)}) copy-start(bf16[258,1536]{1,0:T(8,128)(2,1)} %get-tuple-element.153.refs_3_) | copy-start | bytes 2377732
  40.0 5.7 %copy-start.21 = (bf16[258,1536]{1,0:T(8,128)(2,1)S(1)}, bf16[258,1536]{1,0:T(8,128)(2,1)}, u32[]{:S(2)}) copy-start(bf16[258,1536]{1,0:T(8,128)(2,1)} %get-tuple-element.157.refs_4_) | copy-start | bytes 2377732
  45.7 35.4 %collective-permute-start.11 = (f32[258,768]{1,0:T(8,128)}, f32[258,768]{1,0:T(8,128)}, u32[]{:S(2)}, u32[]{:S(2)}) collective-permute-start(f32[258,768]{1,0:T(8,128)} %get-tuple-element.161.refs_0_), channel_id=1, source_target_pairs={{0,1},{1,0},{2,3},{3,2},{4,5},{5,4},{6,7},{7,6},{8,9},{9,8},{10,11... | collective-permute-start | bytes 2377736 | tf_op jit(solution)/shard_map/ppermute | solution.py:534
  46.3 4.9 %collective-permute-start.2 = (f32[384,1536]{1,0:T(8,128)}, f32[384,1536]{1,0:T(8,128)}, u32[]{:S(2)}, u32[]{:S(2)}) collective-permute-start(f32[384,1536]{1,0:T(8,128)} %get-tuple-element.22), channel_id=1, source_target_pairs={{0,2},{2,0},{4,6},{6,4},{8,10},{10,8},{12,14},{14,12},{16,18},{18,... | collective-permute-start | bytes 7077896 | tf_op jit(solution)/shard_map/cond/branch_1_fun/ppermute | solution.py:478
  51.1 3.9 %copy-start.2 = (bf16[2,258,768]{2,1,0:T(8,128)(2,1)S(1)}, bf16[2,258,768]{2,1,0:T(8,128)(2,1)}, u32[]{:S(2)}) copy-start(bf16[2,258,768]{2,1,0:T(8,128)(2,1)} %copy-done.1) | copy-start | bytes 2377732
  51.1 3.9 %copy-start.6 = (bf16[3,768,384]{2,1,0:T(8,128)(2,1)S(1)}, bf16[3,768,384]{2,1,0:T(8,128)(2,1)}, u32[]{:S(2)}) copy-start(bf16[3,768,384]{2,1,0:T(8,128)(2,1)} %refs_9_.3) | copy-start | bytes 5308420
  54.7 35.1 %collective-permute-start.14 = (f32[192,1536]{1,0:T(8,128)}, f32[192,1536]{1,0:T(8,128)S(1)}, u32[]{:S(2)}, u32[]{:S(2)}) collective-permute-start(f32[192,1536]{1,0:T(8,128)} %get-tuple-element.196), channel_id=1, source_target_pairs={{0,4},{2,6},{4,0},{6,2},{8,12},{10,14},{12,8},{14,10},{16,20},{18,... | collective-permute-start | bytes 3538952 | tf_op jit(solution)/shard_map/ppermute | solution.py:414
  64.1 25.6 %collective-permute-start.15 = (f32[258,768]{1,0:T(8,128)}, f32[258,768]{1,0:T(8,128)}, u32[]{:S(2)}, u32[]{:S(2)}) collective-permute-start(f32[258,768]{1,0:T(8,128)} %get-tuple-element.197.refs_2_), channel_id=1, source_target_pairs={{0,1},{1,0},{2,3},{3,2},{4,5},{5,4},{6,7},{7,6},{8,9},{9,8},{10,11... | collective-permute-start | bytes 2377736 | tf_op jit(solution)/shard_map/ppermute | solution.py:534
  71.4 4.9 %collective-permute-start.3 = (f32[384,1536]{1,0:T(8,128)}, f32[384,1536]{1,0:T(8,128)}, u32[]{:S(2)}, u32[]{:S(2)}) collective-permute-start(f32[384,1536]{1,0:T(8,128)} %param.5), channel_id=1, source_target_pairs={{0,2},{2,0},{4,6},{6,4},{8,10},{10,8},{12,14},{14,12},{16,18},{18,... | collective-permute-start | bytes 7077896 | tf_op jit(solution)/shard_map/cond/branch_1_fun/ppermute | solution.py:478
  76.2 4.8 %copy-start.7 = (bf16[3,768,384]{2,1,0:T(8,128)(2,1)S(1)}, bf16[3,768,384]{2,1,0:T(8,128)(2,1)}, u32[]{:S(2)}) copy-start(bf16[3,768,384]{2,1,0:T(8,128)(2,1)} %refs_9_.3) | copy-start | bytes 5308420
  79.6 30.6 %collective-permute-start.18 = (f32[192,1536]{1,0:T(8,128)}, f32[192,1536]{1,0:T(8,128)}, u32[]{:S(2)}, u32[]{:S(2)}) collective-permute-start(f32[192,1536]{1,0:T(8,128)} %get-tuple-element.211), channel_id=1, source_target_pairs={{0,4},{2,6},{4,0},{6,2},{8,12},{10,14},{12,8},{14,10},{16,20},{18,... | collective-permute-start | bytes 3538952 | tf_op jit(solution)/shard_map/ppermute | solution.py:414
  89.7 2.9 %copy-start.10 = (f32[258,768]{1,0:T(8,128)}, f32[258,768]{1,0:T(8,128)S(1)}, u32[]{:S(2)}) copy-start(f32[258,768]{1,0:T(8,128)S(1)} %get-tuple-element.183.refs_2_) | copy-start | bytes 2377732
  89.7 4.5 %copy-start.14 = (f32[8,768]{1,0:T(8,128)S(1)}, f32[8,768]{1,0:T(8,128)}, u32[]{:S(2)}) copy-start(f32[8,768]{1,0:T(8,128)} %get-tuple-element.191.refs_9_) | copy-start | bytes 73732
  89.7 4.5 %copy-start.15 = (f32[8,768]{1,0:T(8,128)S(1)}, f32[8,768]{1,0:T(8,128)}, u32[]{:S(2)}) copy-start(f32[8,768]{1,0:T(8,128)} %get-tuple-element.192.refs_10_) | copy-start | bytes 73732
  89.7 4.5 %copy-start.16 = (f32[8,768]{1,0:T(8,128)S(1)}, f32[8,768]{1,0:T(8,128)}, u32[]{:S(2)}) copy-start(f32[8,768]{1,0:T(8,128)} %get-tuple-element.193.refs_11_) | copy-start | bytes 73732
  89.7 4.5 %copy-start.17 = (f32[8,768]{1,0:T(8,128)S(1)}, f32[8,768]{1,0:T(8,128)}, u32[]{:S(2)}) copy-start(f32[8,768]{1,0:T(8,128)} %get-tuple-element.194.refs_12_) | copy-start | bytes 73732
  89.7 22.9 %copy-start.8 = (f32[192,1536]{1,0:T(8,128)}, f32[192,1536]{1,0:T(8,128)S(1)}, u32[]{:S(2)}) copy-start(f32[192,1536]{1,0:T(8,128)S(1)} %collective-permute-done.14.refs_3_) | copy-start | bytes 3538948
  92.6 20.1 %collective-permute-start.17 = (f32[96,1536]{1,0:T(8,128)}, f32[96,1536]{1,0:T(8,128)}, u32[]{:S(2)}, u32[]{:S(2)}) collective-permute-start(f32[96,1536]{1,0:T(8,128)} %get-tuple-element.210), channel_id=1, source_target_pairs={{0,8},{2,10},{4,12},{6,14},{8,0},{10,2},{12,4},{14,6},{16,24},{18,... | collective-permute-start | bytes 1769480 | tf_op jit(solution)/shard_map/ppermute | solution.py:414
  101.7 5.0 %copy-start.11 = (f32[258,768]{1,0:T(8,128)S(1)}, f32[258,768]{1,0:T(8,128)}, u32[]{:S(2)}) copy-start(f32[258,768]{1,0:T(8,128)} %copy-done.10) | copy-start | bytes 2377732
  101.7 5.0 %collective-permute-start.4 = (f32[392,1536]{1,0:T(8,128)}, f32[392,1536]{1,0:T(8,128)}, u32[]{:S(2)}, u32[]{:S(2)}) collective-permute-start(f32[392,1536]{1,0:T(8,128)} %get-tuple-element.26), channel_id=1, source_target_pairs={{0,2},{2,0},{4,6},{6,4},{8,10},{10,8},{12,14},{14,12},{16,18},{18,... | collective-permute-start | bytes 7225352 | tf_op jit(solution)/shard_map/cond/branch_1_fun/ppermute | solution.py:478
  101.8 4.7 %collective-permute-start.5 = (f32[8,1536]{1,0:T(8,128)S(1)}, f32[8,1536]{1,0:T(8,128)}, u32[]{:S(2)}, u32[]{:S(2)}) collective-permute-start(f32[8,1536]{1,0:T(8,128)S(1)} %get-tuple-element.27), channel_id=1, source_target_pairs={{0,1},{1,0},{2,3},{3,2},{4,5},{5,4},{6,7},{7,6},{8,9},{9,8},{10,11... | collective-permute-start | bytes 147464 | tf_op jit(solution)/shard_map/cond/branch_1_fun/ppermute | solution.py:482
  102.3 4.3 %collective-permute-start.6 = (f32[8,1536]{1,0:T(8,128)S(1)}, f32[8,1536]{1,0:T(8,128)}, u32[]{:S(2)}, u32[]{:S(2)}) collective-permute-start(f32[8,1536]{1,0:T(8,128)S(1)} %get-tuple-element.27), channel_id=1, source_target_pairs={{0,3},{1,2},{2,1},{3,0},{4,7},{5,6},{6,5},{7,4},{8,11},{9,10},{10,... | collective-permute-start | bytes 147464 | tf_op jit(solution)/shard_map/cond/branch_1_fun/ppermute | solution.py:482
  106.7 21.3 %collective-permute-start.13 = (f32[258,768]{1,0:T(8,128)S(1)}, f32[258,768]{1,0:T(8,128)S(1)}, u32[]{:S(2)}, u32[]{:S(2)}) collective-permute-start(f32[258,768]{1,0:T(8,128)S(1)} %copy-done.11), channel_id=1, source_target_pairs={{0,1},{1,0},{2,3},{3,2},{4,5},{5,4},{6,7},{7,6},{8,9},{9,8},{10,11... | collective-permute-start | bytes 2377736 | tf_op jit(solution)/shard_map/ppermute | solution.py:534
  109.5 16.8 %collective-permute-start.16 = (f32[200,768]{1,0:T(8,128)S(1)}, f32[200,768]{1,0:T(8,128)S(1)}, u32[]{:S(2)}, u32[]{:S(2)}) collective-permute-start(f32[200,768]{1,0:T(8,128)S(1)} %get-tuple-element.207), channel_id=1, source_target_pairs={{0,4},{2,6},{4,0},{6,2},{8,12},{10,14},{12,8},{14,10},{16,20},{18,... | collective-permute-start | bytes 1843208 | tf_op jit(solution)/shard_map/ppermute | solution.py:414
  112.2 24.0 %collective-permute-start.22 = (f32[96,1536]{1,0:T(8,128)S(1)}, f32[96,1536]{1,0:T(8,128)S(1)}, u32[]{:S(2)}, u32[]{:S(2)}) collective-permute-start(f32[96,1536]{1,0:T(8,128)S(1)} %get-tuple-element.222), channel_id=1, source_target_pairs={{0,8},{2,10},{4,12},{6,14},{8,0},{10,2},{12,4},{14,6},{16,24},{18,... | collective-permute-start | bytes 1769480 | tf_op jit(solution)/shard_map/ppermute | solution.py:414
  114.5 19.2 %collective-permute-start.23 = (f32[48,1536]{1,0:T(8,128)S(1)}, f32[48,1536]{1,0:T(8,128)S(1)}, u32[]{:S(2)}, u32[]{:S(2)}) collective-permute-start(f32[48,1536]{1,0:T(8,128)S(1)} %get-tuple-element.223), channel_id=1, source_target_pairs={{0,16},{2,18},{4,20},{6,22},{8,24},{10,26},{12,28},{14,30},{16,0},... | collective-permute-start | bytes 884744 | tf_op jit(solution)/shard_map/ppermute | solution.py:414
  119.0 21.6 %collective-permute-start.21 = (f32[192,768]{1,0:T(8,128)S(1)}, f32[192,768]{1,0:T(8,128)S(1)}, u32[]{:S(2)}, u32[]{:S(2)}) collective-permute-start(f32[192,768]{1,0:T(8,128)S(1)} %get-tuple-element.221), channel_id=1, source_target_pairs={{0,4},{2,6},{4,0},{6,2},{8,12},{10,14},{12,8},{14,10},{16,20},{18,... | collective-permute-start | bytes 1769480 | tf_op jit(solution)/shard_map/ppermute | solution.py:414
  129.9 14.3 %collective-permute-start.20 = (f32[104,768]{1,0:T(8,128)S(1)}, f32[104,768]{1,0:T(8,128)S(1)}, u32[]{:S(2)}, u32[]{:S(2)}) collective-permute-start(f32[104,768]{1,0:T(8,128)S(1)} %get-tuple-element.220), channel_id=1, source_target_pairs={{0,8},{2,10},{4,12},{6,14},{8,0},{10,2},{12,4},{14,6},{16,24},{18,... | collective-permute-start | bytes 958472 | tf_op jit(solution)/shard_map/ppermute | solution.py:414
  130.4 36.2 %collective-permute-start.19 = (f32[528,768]{1,0:T(8,128)}, f32[528,768]{1,0:T(8,128)S(1)}, u32[]{:S(2)}, u32[]{:S(2)}) collective-permute-start(f32[528,768]{1,0:T(8,128)} %get-tuple-element.219.refs_0_), channel_id=1, source_target_pairs={{0,1},{1,0},{2,3},{3,2},{4,5},{5,4},{6,7},{7,6},{8,9},{9,8},{10,11... | collective-permute-start | bytes 4866056 | tf_op jit(solution)/shard_map/ppermute | solution.py:534
  137.9 18.4 %collective-permute-start.26 = (f32[48,1536]{1,0:T(8,128)S(1)}, f32[48,1536]{1,0:T(8,128)S(1)}, u32[]{:S(2)}, u32[]{:S(2)}) collective-permute-start(f32[48,1536]{1,0:T(8,128)S(1)} %get-tuple-element.230), channel_id=1, source_target_pairs={{0,16},{2,18},{4,20},{6,22},{8,24},{10,26},{12,28},{14,30},{16,0},... | collective-permute-start | bytes 884744 | tf_op jit(solution)/shard_map/ppermute | solution.py:414
  140.6 18.2 %copy-start.12 = (f32[192,768]{1,0:T(8,128)}, f32[192,768]{1,0:T(8,128)S(1)}, u32[]{:S(2)}) copy-start(f32[192,768]{1,0:T(8,128)S(1)} %collective-permute-done.21.refs_3_) | copy-start | bytes 1769476
  142.2 16.6 %collective-permute-start.25 = (f32[96,768]{1,0:T(8,128)S(1)}, f32[96,768]{1,0:T(8,128)S(1)}, u32[]{:S(2)}, u32[]{:S(2)}) collective-permute-start(f32[96,768]{1,0:T(8,128)S(1)} %get-tuple-element.229), channel_id=1, source_target_pairs={{0,8},{2,10},{4,12},{6,14},{8,0},{10,2},{12,4},{14,6},{16,24},{18,... | collective-permute-start | bytes 884744 | tf_op jit(solution)/shard_map/ppermute | solution.py:414
  145.8 15.5 %collective-permute-start.24 = (f32[56,768]{1,0:T(8,128)S(1)}, f32[56,768]{1,0:T(8,128)S(1)}, u32[]{:S(2)}, u32[]{:S(2)}) collective-permute-start(f32[56,768]{1,0:T(8,128)S(1)} %get-tuple-element.228), channel_id=1, source_target_pairs={{0,16},{2,18},{4,20},{6,22},{8,24},{10,26},{12,28},{14,30},{16,0},... | collective-permute-start | bytes 516104 | tf_op jit(solution)/shard_map/ppermute | solution.py:414
  160.4 8.5 %collective-permute-start.27 = (f32[48,768]{1,0:T(8,128)S(1)}, f32[48,768]{1,0:T(8,128)S(1)}, u32[]{:S(2)}, u32[]{:S(2)}) collective-permute-start(f32[48,768]{1,0:T(8,128)S(1)} %get-tuple-element.239), channel_id=1, source_target_pairs={{0,16},{2,18},{4,20},{6,22},{8,24},{10,26},{12,28},{14,30},{16,0},... | collective-permute-start | bytes 442376 | tf_op jit(solution)/shard_map/ppermute | solution.py:414
  166.6 2.3 %copy-start.13 = (f32[192,768]{1,0:T(8,128)S(1)}, f32[192,768]{1,0:T(8,128)}, u32[]{:S(2)}) copy-start(f32[192,768]{1,0:T(8,128)} %copy-done.12) | copy-start | bytes 1769476
  (2 other events, 4.0 us)

commit v5 on v4

--- a/solution.py
+++ b/solution.py
@@ -573,7 +573,7 @@
             [scalars(), whole(seqs[b]), one_of(cotangent, b)] + [whole(a) for a in args[3:]],
             [far((rows, width)), far((rows, width), BF16), far((rows, hidden_width), BF16),
              far((rows, hidden_width), BF16), shape((rows, width)), far((8, width))],
-            44, f"forward{b}", deep=(1, 3, 4, 5, 6),
+            44, f"forward{b}", cost=32, deep=(1, 3, 4, 5, 6),
         )
         for kept, one in zip((middles, seconds, hiddens, uppers, norms, smalls), got):
             kept.append(one)

time: 174 us -> 173 us (level)
    unnamed x47 -> x45, local copies, waits for them, and re-layouts: 4.83 us -> 4.83 us
  transfers between devices with their start and end apart: 28 -> 28, of which waited for: 13 -> 13; matrix products, arithmetic and copies ran while one was open for 2% -> 2% of each run, Pallas kernels for 60% -> 59%
where the time goes in v5:
time: 173 us; the launch traced here: 172 us
  Pallas kernels  104 us (60%)
  starting transfers between devices  30.9 us (18%)
  waiting for transfers between devices  27.6 us (16%)
  local copies, waits for them, and re-layouts  6.83 us (4%)
  other arithmetic  1.83 us (1%)
    pallas_call x30, Pallas kernels, kernel(): pl.pallas_call(body, out_shape=tuple(outs), grid_spec=pltpu.PrefetchScala...  104 us
    ppermute x12, starting transfers between devices, step(): lax.ppermute(send, 'dp', flips(self.dp, bit))  15.8 us
    ppermute x12, waiting for transfers between devices, step(): lax.ppermute(send, 'dp', flips(self.dp, bit))  12.9 us
    ppermute x8, starting transfers between devices, per_device(): across = lambda v: lax.ppermute(v, 'mp', SWAP)  10.9 us
    ppermute x3, waiting for transfers between devices, weight_sum(): swap = lambda v: lax.ppermute(v, 'dp', flips(dp, 0))  7.16 us
    unnamed x45, local copies, waits for them, and re-layouts  4.83 us
  transfers between devices with their start and end apart: 28, of which 13 were waited for; matrix products, arithmetic and copies ran while one was open for 2% of the time, Pallas kernels for 59%

profile of v5, /device:TPU:0, one launch (start us, length us, event | category | flops | bytes accessed | tf_op | source)
XLA Modules:
  0.0 171.9 jit_solution(12824647913585553966)
XLA Ops:
  1.6 3.0 %collective-permute-start.8 = (f32[96,768]{1,0:T(8,128)S(1)}, f32[96,768]{1,0:T(8,128)S(1)}, u32[]{:S(2)}, u32[]{:S(2)}) collective-permute-start(f32[96,768]{1,0:T(8,128)S(1)} %dynamic-slice_convert_fusion), channel_id=1, source_target_pairs={{0,1},{1,0},{2,3},{3,2},{4,5},{5,4},{6,7},{7,6},{8,9},{9,8},{10,11... | collective-permute-start | bytes 884744 | tf_op jit(solution)/shard_map/ppermute | solution.py:534
  4.6 6.1 %attend0.1 = (f32[258,768]{1,0:T(8,128)}, bf16[258,768]{1,0:T(8,128)(2,1)}, bf16[258,1152]{1,0:T(8,128)(2,1)}, f32[258,128]{1,0:T(8,128)}, f32[258,384]{1,0:T(8,128)S(1)}, /*index=5*/f32[8,128]{1,0:T(8,128)S(1)}) custom-call(s32[2,256]{1,0:T(2,128)} %refs_0_.5, bf16[2,1024,768]{2,1,0:T(8,128)(2,1)} %refs_1_.5, bf16[2,2,768]{2,1,0:T(2,128)(2,1)} %refs_2_.7, ...), custom_call_target="tpu_custom_call" | custom-call | flops 2147483648 | bytes 1 | tf_op jit(solution)/shard_map/attend0/pallas_call | solution.py:70
  11.6 1.7 collective-permute-start.9
  15.1 6.4 %attend1.1 = (f32[258,768]{1,0:T(8,128)}, bf16[258,768]{1,0:T(8,128)(2,1)}, bf16[258,1152]{1,0:T(8,128)(2,1)}, f32[258,128]{1,0:T(8,128)}, f32[258,384]{1,0:T(8,128)S(1)}, /*index=5*/f32[8,128]{1,0:T(8,128)S(1)}) custom-call(s32[2,256]{1,0:T(2,128)} %refs_0_.5, bf16[2,1024,768]{2,1,0:T(8,128)(2,1)} %refs_1_.5, bf16[2,2,768]{2,1,0:T(2,128)(2,1)} %refs_2_.7, ...), custom_call_target="tpu_custom_call" | custom-call | flops 2147483648 | bytes 1 | tf_op jit(solution)/shard_map/attend1/pallas_call | solution.py:70
  22.0 2.3 %conditional.4 = (f32[96,768]{1,0:T(8,128)}, f32[96,768]{1,0:T(8,128)}) conditional(s32[]{:T(128)} %bitcast.5, () %tuple.43, (f32[96,768]{1,0:T(8,128)S(1)}, f32[96,768]{1,0:T(8,128)}) %tuple.44), branch_computations={%region_0.1_spmd, %region_1.2_spmd} | conditional | bytes 2359392 | solution.py:110
  22.5 1.6 collective-permute-done
  27.0 5.6 %forward0.1 = (f32[258,768]{1,0:T(8,128)}, bf16[258,768]{1,0:T(8,128)(2,1)}, bf16[258,1536]{1,0:T(8,128)(2,1)}, bf16[258,1536]{1,0:T(8,128)(2,1)}, f32[258,768]{...) custom-call(s32[5]{0:T(128)S(1)} %stack.44.refs_0_, f32[258,768]{1,0:T(8,128)} %get-tuple-element.143.refs_1_.refs_5_, ...), custom_call_target="tpu_custom_call" | custom-call | flops 4294967296 | bytes 1 | tf_op jit(solution)/shard_map/forward0/pallas_call | solution.py:70
  34.1 5.6 %forward1.1 = (f32[258,768]{1,0:T(8,128)}, bf16[258,768]{1,0:T(8,128)(2,1)}, bf16[258,1536]{1,0:T(8,128)(2,1)}, bf16[258,1536]{1,0:T(8,128)(2,1)}, f32[258,768]{...) custom-call(s32[5]{0:T(128)S(1)} %stack.44.refs_0_, f32[258,768]{1,0:T(8,128)} %get-tuple-element.154.refs_1_.refs_5_, ...), custom_call_target="tpu_custom_call" | custom-call | flops 4294967296 | bytes 1 | tf_op jit(solution)/shard_map/forward1/pallas_call | solution.py:70
  39.8 5.6 %down_grads.1 = (f32[384,1536]{1,0:T(8,128)}, f32[384,1536]{1,0:T(8,128)}, f32[8,128]{1,0:T(8,128)S(1)}) custom-call(s32[5]{0:T(128)S(1)} %stack.44.refs_0_, bf16[2,258,768]{2,1,0:T(8,128)(2,1)} %copy-done, bf16[2,258,768]{2,1,0:T(8,128)(2,1)} %copy-done, bf16[258,1536]{1,0:T(8,128)(2,1)} %get-tuple-element.153.refs_3_, ...), custom_call_target="tpu_custom_call" | custom-call | flops 2147483648 | bytes 1 | tf_op jit(solution)/shard_map/down_grads/pallas_call | solution.py:70
  46.0 4.9 %conditional.5 = (f32[384,1536]{1,0:T(8,128)}, f32[528,768]{1,0:T(8,128)}) conditional(s32[]{:T(128)} %bitcast.5, () %tuple.41, (f32[384,1536]{1,0:T(8,128)}, bf16[258,1536]{1,0:T(8,128)(2,1)S(1)}, bf16[258,1536]{1,0:T(8,128)(2,1)S(1)}, bf16[1536,768]{1,0:T(8,128)(2,1)S(1)}) %tuple.70), branch_computations={%region_2.3_spmd, %region_3.4_spmd} | conditional | flops 2147483648 | bytes 9437241 | solution.py:110
  46.0 2.7 %branch.1 = f32[528,768]{1,0:T(8,128)} custom-call(bf16[258,1536]{1,0:T(8,128)(2,1)S(1)} %get-tuple-element.23.refs_0_, bf16[258,1536]{1,0:T(8,128)(2,1)S(1)} %get-tuple-element.24.refs_1_, bf16[1536,768]{1,0:T(8,128)(2,1)S(1)} %get-tuple-element.25.refs_2_), custom_call_target="tpu_custom_call" | custom-call | flops 2147483648 | bytes 1 | tf_op jit(solution)/shard_map/cond/branch_1_fun/branch/pallas_call | solution.py:70
  48.6 2.2 %collective-permute-done.2 = f32[384,1536]{1,0:T(8,128)} collective-permute-done((f32[384,1536]{1,0:T(8,128)}, f32[384,1536]{1,0:T(8,128)}, u32[]{:S(2)}, u32[]{:S(2)}) %collective-permute-start.2) | collective-permute-done | bytes 2359328 | tf_op jit(solution)/shard_map/cond/branch_1_fun/ppermute | solution.py:478
  50.9 3.5 %down0_step1.1 = (f32[192,1536]{1,0:T(8,128)}, f32[8,128]{1,0:T(8,128)S(1)}) custom-call(s32[5]{0:T(128)S(1)} %stack.44.refs_0_, f32[384,1536]{1,0:T(8,128)} %get-tuple-element.169.refs_1_, f32[384,1536]{1,0:T(8,128)} %get-tuple-element.170.refs_2_, f32[8,128]{1,0:T(8,128)S(1)} %get-tuple-element.171.refs_3_), custom_call_target="tpu_custom_call" | custom-call | flops 2147483648 | bytes 1 | tf_op jit(solution)/shard_map/down0_step1/pallas_call | solution.py:70
  54.7 9.1 %backward0.1 = (f32[258,768]{1,0:T(8,128)}, bf16[258,768]{1,0:T(8,128)(2,1)}, bf16[258,1152]{1,0:T(8,128)(2,1)}, f32[258,768]{1,0:T(8,128)}, f32[8,768]{1,0:T(8,...) custom-call(f32[258,768]{1,0:T(8,128)} %get-tuple-element.165.refs_0_, f32[258,768]{1,0:T(8,128)} %collective-permute-done.12.refs_1_, ...), custom_call_target="tpu_custom_call" | custom-call | flops 8589934592 | bytes 1 | tf_op jit(solution)/shard_map/backward0/pallas_call | solution.py:70
  63.8 1.7 %collective-permute-start.15 = (f32[258,768]{1,0:T(8,128)}, f32[258,768]{1,0:T(8,128)}, u32[]{:S(2)}, u32[]{:S(2)}) collective-permute-start(f32[258,768]{1,0:T(8,128)} %get-tuple-element.197.refs_2_), channel_id=1, source_target_pairs={{0,1},{1,0},{2,3},{3,2},{4,5},{5,4},{6,7},{7,6},{8,9},{9,8},{10,11... | collective-permute-start | bytes 2377736 | tf_op jit(solution)/shard_map/ppermute | solution.py:534
  65.5 5.5 %up_grads.1 = (f32[384,1536]{1,0:T(8,128)}, f32[384,1536]{1,0:T(8,128)}, f32[8,128]{1,0:T(8,128)S(1)}) custom-call(s32[5]{0:T(128)S(1)} %stack.44.refs_0_, bf16[258,768]{1,0:T(8,128)(2,1)} %get-tuple-element.174.refs_1_, bf16[258,768]{1,0:T(8,128)(2,1)} %get-tuple-element.175.refs_2_, bf16[258,1536]{1,0:T(8,128)(2,1)} %get-tuple-element.176.refs_3_, ...), custom_call_target="tpu_custom_call" | custom-call | flops 2147483648 | bytes 1 | tf_op jit(solution)/shard_map/up_grads/pallas_call | solution.py:70
  71.0 4.9 %conditional.6 = (f32[384,1536]{1,0:T(8,128)}) conditional(s32[]{:T(128)} %bitcast.5, () %tuple.46, f32[384,1536]{1,0:T(8,128)} %get-tuple-element.180), branch_computations={%region_4.5_spmd, %region_5.6_spmd} | conditional | bytes 9437232 | solution.py:110
  71.0 4.9 %collective-permute-done.3 = f32[384,1536]{1,0:T(8,128)} collective-permute-done((f32[384,1536]{1,0:T(8,128)}, f32[384,1536]{1,0:T(8,128)}, u32[]{:S(2)}, u32[]{:S(2)}) %collective-permute-start.3) | collective-permute-done | bytes 2359328 | tf_op jit(solution)/shard_map/cond/branch_1_fun/ppermute | solution.py:478
  75.9 3.3 %up0_step1.1 = (f32[192,1536]{1,0:T(8,128)}, f32[8,128]{1,0:T(8,128)S(1)}) custom-call(s32[5]{0:T(128)S(1)} %stack.44.refs_0_, f32[384,1536]{1,0:T(8,128)} %get-tuple-element.179.refs_1_, f32[384,1536]{1,0:T(8,128)} %get-tuple-element.282.refs_2_, f32[8,128]{1,0:T(8,128)S(1)} %get-tuple-element.181.refs_3_), custom_call_target="tpu_custom_call" | custom-call | flops 2147483648 | bytes 1 | tf_op jit(solution)/shard_map/up0_step1/pallas_call | solution.py:70
  80.7 8.7 %backward1.1 = (f32[258,768]{1,0:T(8,128)}, bf16[258,768]{1,0:T(8,128)(2,1)}, bf16[258,1152]{1,0:T(8,128)(2,1)}, f32[258,768]{1,0:T(8,128)S(1)}, f32[8,768]{1,0:...) custom-call(f32[258,768]{1,0:T(8,128)} %get-tuple-element.161.refs_0_, ...), custom_call_target="tpu_custom_call" | custom-call | flops 8589934592 | bytes 1 | tf_op jit(solution)/shard_map/backward1/pallas_call | solution.py:70
  89.5 2.1 %down0_step2.1 = (f32[96,1536]{1,0:T(8,128)S(1)}, f32[8,128]{1,0:T(8,128)S(1)}) custom-call(s32[5]{0:T(128)S(1)} %stack.44.refs_0_, f32[384,1536]{1,0:T(8,128)} %get-tuple-element.169.refs_1_, f32[384,1536]{1,0:T(8,128)} %get-tuple-element.170.refs_2_, f32[192,1536]{1,0:T(8,128)} %collective-permute-done.14.refs_3_, f32[8,128]{1,0:T(8,128)S(1)} %get-tuple-element.199.refs_4_), custom_call_target="tpu_custom_call" | custom-call | flops 2147483648 | bytes 1 | tf_op jit(solution)/shard_map/down0_step2/pallas_call | solution.py:70
  91.5 1.6 collective-permute-start.17
  93.2 7.6 %last_grads.1 = (f32[392,1536]{1,0:T(8,128)}, f32[392,1536]{1,0:T(8,128)}, f32[8,128]{1,0:T(8,128)S(1)}) custom-call(s32[5]{0:T(128)S(1)} %stack.44.refs_0_, bf16[258,768]{1,0:T(8,128)(2,1)} %get-tuple-element.185.refs_1_, bf16[258,768]{1,0:T(8,128)(2,1)} %get-tuple-element.186.refs_2_, f32[258,384]{1,0:T(8,128)} %copy-done.11, f32[258,384]{1,0:T(8,128)} %copy-done.12, ...), custom_call_target="tpu_custom_call" | custom-call | flops 2147483648 | bytes 1 | tf_op jit(solution)/shard_map/last_grads/pallas_call | solution.py:70
  100.7 5.0 %conditional.7 = (f32[392,1536]{1,0:T(8,128)}, f32[8,1536]{1,0:T(8,128)}, f32[8,1536]{1,0:T(8,128)}) conditional(s32[]{:T(128)} %bitcast.5, () %tuple.48, (f32[392,1536]{1,0:T(8,128)}, f32[8,1536]{1,0:T(8,128)S(1)}) %tuple.49), branch_computations={%region_6.7_spmd, %region_7.8_spmd} | conditional | bytes 10027152 | solution.py:110
  102.7 2.9 %collective-permute-done.5 = f32[8,1536]{1,0:T(8,128)} collective-permute-done((f32[8,1536]{1,0:T(8,128)S(1)}, f32[8,1536]{1,0:T(8,128)}, u32[]{:S(2)}, u32[]{:S(2)}) %collective-permute-start.5) | collective-permute-done | bytes 49184 | tf_op jit(solution)/shard_map/cond/branch_1_fun/ppermute | solution.py:482
  106.7 1.9 %last0_step1.1 = (f32[200,768]{1,0:T(8,128)S(1)}, f32[8,128]{1,0:T(8,128)S(1)}) custom-call(s32[5]{0:T(128)S(1)} %stack.44.refs_0_, f32[392,1536]{1,0:T(8,128)} %get-tuple-element.201.refs_1_.refs_3_.refs_4_.refs_5_.refs_6_, f32[392,1536]{1,0:T(8,128)} %get-tuple-element.203.refs_2_.refs_4_.refs_5_.refs_6_.refs_7_, ...), custom_call_target="tpu_custom_call" | custom-call | flops 2147483648 | bytes 1 | tf_op jit(solution)/shard_map/last0_step1/pallas_call | solution.py:70
  109.2 2.1 %up0_step2.1 = (f32[96,1536]{1,0:T(8,128)S(1)}, f32[8,128]{1,0:T(8,128)S(1)}) custom-call(s32[5]{0:T(128)S(1)} %stack.44.refs_0_, f32[384,1536]{1,0:T(8,128)} %get-tuple-element.179.refs_1_, f32[384,1536]{1,0:T(8,128)} %get-tuple-element.282.refs_2_, f32[192,1536]{1,0:T(8,128)} %collective-permute-done.18.refs_3_, f32[8,128]{1,0:T(8,128)S(1)} %get-tuple-element.212.refs_4_), custom_call_target="tpu_custom_call" | custom-call | flops 2147483648 | bytes 1 | tf_op jit(solution)/shard_map/up0_step2/pallas_call | solution.py:70
  111.8 1.7 %down0_step3.1 = (f32[48,1536]{1,0:T(8,128)S(1)}, f32[8,128]{1,0:T(8,128)S(1)}) custom-call(s32[5]{0:T(128)S(1)} %stack.44.refs_0_, f32[384,1536]{1,0:T(8,128)} %get-tuple-element.169.refs_1_, f32[384,1536]{1,0:T(8,128)} %get-tuple-element.170.refs_2_, f32[192,1536]{1,0:T(8,128)} %collective-permute-done.14.refs_3_, ...), custom_call_target="tpu_custom_call" | custom-call | flops 2147483648 | bytes 1 | tf_op jit(solution)/shard_map/down0_step3/pallas_call | solution.py:70
  113.5 2.7 %collective-permute-start.23 = (f32[48,1536]{1,0:T(8,128)S(1)}, f32[48,1536]{1,0:T(8,128)S(1)}, u32[]{:S(2)}, u32[]{:S(2)}) collective-permute-start(f32[48,1536]{1,0:T(8,128)S(1)} %get-tuple-element.223), channel_id=1, source_target_pairs={{0,16},{2,18},{4,20},{6,22},{8,24},{10,26},{12,28},{14,30},{16,0},... | collective-permute-start | bytes 884744 | tf_op jit(solution)/shard_map/ppermute | solution.py:414
  116.2 1.9 %last1_step1.1 = (f32[192,768]{1,0:T(8,128)S(1)}, f32[8,128]{1,0:T(8,128)S(1)}) custom-call(s32[5]{0:T(128)S(1)} %stack.44.refs_0_, f32[392,1536]{1,0:T(8,128)} %get-tuple-element.201.refs_1_.refs_3_.refs_4_.refs_5_.refs_6_, f32[392,1536]{1,0:T(8,128)} %get-tuple-element.203.refs_2_.refs_4_.refs_5_.refs_6_.refs_7_, f32[8,128]{1,0:T(8,128)S(1)} %get-tuple-element.214.refs_3_), custom_call_target="tpu_custom_call" | custom-call | flops 2147483648 | bytes 1 | tf_op jit(solution)/shard_map/last1_step1/pallas_call | solution.py:70
  119.6 2.4 %input0.1 = (f32[258,768]{1,0:T(8,128)S(1)}, f32[8,128]{1,0:T(8,128)S(1)}) custom-call(f32[768]{0:T(1024)} %refs_0_.7, f32[258,768]{1,0:T(8,128)} %get-tuple-element.143.refs_1_.refs_5_, f32[258,768]{1,0:T(8,128)} %get-tuple-element.197.refs_2_, f32[258,768]{1,0:T(8,128)} %collective-permute-done.15.refs_3_, f32[258,768]{1,0:T(8,128)} %get-tuple-element.209.refs_4_, ...), custom_call_target="tpu_custom_call" | custom-call | flops 2147483648 | bytes 1 | tf_op jit(solution)/shard_map/input0/pallas_call | solution.py:70
  122.0 3.4 %collective-permute-done.16.refs_3_.refs_8_.refs_9_.refs_10_ = f32[200,768]{1,0:T(8,128)S(1)} collective-permute-done((f32[200,768]{1,0:T(8,128)S(1)}, f32[200,768]{1,0:T(8,128)S(1)}, u32[]{:S(2)}, u32[]{:S(2)}) %collective-permute-start.16) | collective-permute-done | bytes 614432 | tf_op jit(solution)/shard_map/ppermute | solution.py:414
  125.4 1.7 last0_step2.1
  127.0 1.9 %input1.1 = (f32[258,768]{1,0:T(8,128)S(1)}, f32[8,128]{1,0:T(8,128)S(1)}) custom-call(f32[768]{0:T(1024)} %refs_0_.7, f32[258,768]{1,0:T(8,128)} %get-tuple-element.154.refs_1_.refs_5_, f32[258,768]{1,0:T(8,128)S(1)} %copy-done.6, f32[258,768]{1,0:T(8,128)S(1)} %collective-permute-done.13.refs_3_, f32[258,768]{1,0:T(8,128)} %get-tuple-element.184.refs_4_, ...), custom_call_target="tpu_custom_call" | custom-call | flops 2147483648 | bytes 1 | tf_op jit(solution)/shard_map/input1/pallas_call | solution.py:70
  130.7 2.0 %copy.35 = f32[2,258,768]{2,0,1:T(2,128)} copy(f32[2,258,768]{2,1,0:T(8,128)S(1)} %pad_maximum_fusion) | data formatting | bytes 3170304
  132.7 2.5 %down0_last.1 = (f32[48,1536]{1,0:T(8,128)}, f32[8,128]{1,0:T(8,128)S(1)}) custom-call(s32[5]{0:T(128)S(1)} %stack.44.refs_0_, f32[384,1536]{1,0:T(8,128)} %get-tuple-element.169.refs_1_, f32[384,1536]{1,0:T(8,128)} %get-tuple-element.170.refs_2_, f32[192,1536]{1,0:T(8,128)} %collective-permute-done.14.refs_3_, f32[96,1536]{1,0:T(8,128)S(1)} %copy-done.10, ...), custom_call_target="tpu_custom_call" | custom-call | flops 2147483648 | bytes 1 | tf_op jit(solution)/shard_map/down0_last/pallas_call | solution.py:70
  135.2 1.8 %up0_step3.1 = (f32[48,1536]{1,0:T(8,128)S(1)}, f32[8,128]{1,0:T(8,128)S(1)}) custom-call(s32[5]{0:T(128)S(1)} %stack.44.refs_0_, f32[384,1536]{1,0:T(8,128)} %get-tuple-element.179.refs_1_, f32[384,1536]{1,0:T(8,128)} %get-tuple-element.282.refs_2_, f32[192,1536]{1,0:T(8,128)} %collective-permute-done.18.refs_3_, ...), custom_call_target="tpu_custom_call" | custom-call | flops 2147483648 | bytes 1 | tf_op jit(solution)/shard_map/up0_step3/pallas_call | solution.py:70
  137.0 2.6 %collective-permute-start.26 = (f32[48,1536]{1,0:T(8,128)S(1)}, f32[48,1536]{1,0:T(8,128)S(1)}, u32[]{:S(2)}, u32[]{:S(2)}) collective-permute-start(f32[48,1536]{1,0:T(8,128)S(1)} %get-tuple-element.230), channel_id=1, source_target_pairs={{0,16},{2,18},{4,20},{6,22},{8,24},{10,26},{12,28},{14,30},{16,0},... | collective-permute-start | bytes 884744 | tf_op jit(solution)/shard_map/ppermute | solution.py:414
  139.6 1.7 last1_step2.1
  141.3 1.6 collective-permute-start.25
  143.3 1.6 last0_step3.1
  144.9 2.2 %collective-permute-start.24 = (f32[56,768]{1,0:T(8,128)S(1)}, f32[56,768]{1,0:T(8,128)S(1)}, u32[]{:S(2)}, u32[]{:S(2)}) collective-permute-start(f32[56,768]{1,0:T(8,128)S(1)} %get-tuple-element.228), channel_id=1, source_target_pairs={{0,16},{2,18},{4,20},{6,22},{8,24},{10,26},{12,28},{14,30},{16,0},... | collective-permute-start | bytes 516104 | tf_op jit(solution)/shard_map/ppermute | solution.py:414
  147.1 8.3 %collective-permute-done.26.refs_5_ = f32[48,1536]{1,0:T(8,128)S(1)} collective-permute-done((f32[48,1536]{1,0:T(8,128)S(1)}, f32[48,1536]{1,0:T(8,128)S(1)}, u32[]{:S(2)}, u32[]{:S(2)}) %collective-permute-start.26) | collective-permute-done | bytes 294944 | tf_op jit(solution)/shard_map/ppermute | solution.py:414
  155.4 2.5 %up0_last.1 = (f32[48,1536]{1,0:T(8,128)}, f32[8,128]{1,0:T(8,128)S(1)}) custom-call(s32[5]{0:T(128)S(1)} %stack.44.refs_0_, f32[384,1536]{1,0:T(8,128)} %get-tuple-element.179.refs_1_, f32[384,1536]{1,0:T(8,128)} %get-tuple-element.282.refs_2_, f32[192,1536]{1,0:T(8,128)} %collective-permute-done.18.refs_3_, ...), custom_call_target="tpu_custom_call" | custom-call | flops 2147483648 | bytes 1 | tf_op jit(solution)/shard_map/up0_last/pallas_call | solution.py:70
  160.4 1.6 last0_last.1
  163.9 1.8 %collective-permute-done.19.refs_1_ = f32[528,768]{1,0:T(8,128)S(1)} collective-permute-done((f32[528,768]{1,0:T(8,128)}, f32[528,768]{1,0:T(8,128)S(1)}, u32[]{:S(2)}, u32[]{:S(2)}) %collective-permute-start.19) | collective-permute-done | bytes 1622048 | tf_op jit(solution)/shard_map/ppermute | solution.py:534
  165.7 2.3 %output.1 = (bf16[2,258,768]{2,1,0:T(8,128)(2,1)S(1)}, f32[8,128]{1,0:T(8,128)S(1)}) custom-call(f32[528,768]{1,0:T(8,128)} %get-tuple-element.219.refs_0_, f32[528,768]{1,0:T(8,128)S(1)} %collective-permute-done.19.refs_1_, f32[768]{0:T(1024)} %refs_2_.8, f32[258,768]{1,0:T(8,128)} %get-tuple-element.166.refs_2_.refs_3_, ...), custom_call_target="tpu_custom_call" | custom-call | flops 2147483648 | bytes 1 | tf_op jit(solution)/shard_map/output/pallas_call | solution.py:70
  168.0 1.6 last1_last.1
  (98 shorter events, 25.9 us)
Async XLA Ops:
  1.6 10.0 %collective-permute-start.8 = (f32[96,768]{1,0:T(8,128)S(1)}, f32[96,768]{1,0:T(8,128)S(1)}, u32[]{:S(2)}, u32[]{:S(2)}) collective-permute-start(f32[96,768]{1,0:T(8,128)S(1)} %dynamic-slice_convert_fusion), channel_id=1, source_target_pairs={{0,1},{1,0},{2,3},{3,2},{4,5},{5,4},{6,7},{7,6},{8,9},{9,8},{10,11... | collective-permute-start | bytes 884744 | tf_op jit(solution)/shard_map/ppermute | solution.py:534
  4.6 10.4 %copy-start.17 = (bf16[2,258,768]{2,0,1:T(2,128)(2,1)S(1)}, bf16[2,258,768]{2,0,1:T(2,128)(2,1)}, u32[]{:S(2)}) copy-start(bf16[2,258,768]{2,0,1:T(2,128)(2,1)} %param.37) | copy-start | bytes 2377732
  10.8 15.0 %copy-start.11 = (f32[258,384]{1,0:T(8,128)}, f32[258,384]{1,0:T(8,128)S(1)}, u32[]{:S(2)}) copy-start(f32[258,384]{1,0:T(8,128)S(1)} %get-tuple-element.144.refs_7_.refs_3_) | copy-start | bytes 1188868
  11.6 10.4 %collective-permute-start.9 = (f32[96,768]{1,0:T(8,128)S(1)}, f32[96,768]{1,0:T(8,128)}, u32[]{:S(2)}, u32[]{:S(2)}) collective-permute-start(f32[96,768]{1,0:T(8,128)S(1)} %collective-permute-done.8.refs_2_), channel_id=1, source_target_pairs={{0,4},{2,6},{4,0},{6,2},{8,12},{10,14},{12,8},{14,10},{16,20},{18,... | collective-permute-start | bytes 884744 | tf_op jit(solution)/shard_map/ppermute | solution.py:558
  13.4 12.4 %collective-permute-start.7 = (f32[258,384]{1,0:T(8,128)S(1)}, f32[258,384]{1,0:T(8,128)S(1)}, u32[]{:S(2)}, u32[]{:S(2)}) collective-permute-start(f32[258,384]{1,0:T(8,128)S(1)} %get-tuple-element.144.refs_7_.refs_3_), channel_id=1, source_target_pairs={{0,1},{1,0},{2,3},{3,2},{4,5},{5,4},{6,7},{7,6},{8,9},{9,8},{10,11... | collective-permute-start | bytes 1188872 | tf_op jit(solution)/shard_map/ppermute | solution.py:534
  15.1 19.0 %copy-start = (bf16[2,258,768]{2,1,0:T(8,128)(2,1)}, bf16[2,258,768]{2,1,0:T(8,128)(2,1)S(1)}, u32[]{:S(2)}) copy-start(bf16[2,258,768]{2,1,0:T(8,128)(2,1)S(1)} %copy.30.refs_2_.refs_1_.refs_6_) | copy-start | bytes 2377732
  15.1 9.2 %copy-start.2 = (bf16[384,768]{1,0:T(8,128)(2,1)S(1)}, bf16[384,768]{1,0:T(8,128)(2,1)}, u32[]{:S(2)}) copy-start(bf16[384,768]{1,0:T(8,128)(2,1)} %refs_8_.3) | copy-start | bytes 1769476
  21.5 12.6 %copy-start.12 = (f32[258,384]{1,0:T(8,128)}, f32[258,384]{1,0:T(8,128)S(1)}, u32[]{:S(2)}) copy-start(f32[258,384]{1,0:T(8,128)S(1)} %get-tuple-element.155.refs_7_.refs_4_) | copy-start | bytes 1188868
  21.5 12.6 %collective-permute-start.10 = (f32[258,384]{1,0:T(8,128)S(1)}, f32[258,384]{1,0:T(8,128)S(1)}, u32[]{:S(2)}, u32[]{:S(2)}) collective-permute-start(f32[258,384]{1,0:T(8,128)S(1)} %get-tuple-element.155.refs_7_.refs_4_), channel_id=1, source_target_pairs={{0,1},{1,0},{2,3},{3,2},{4,5},{5,4},{6,7},{7,6},{8,9},{9,8},{10,11... | collective-permute-start | bytes 1188872 | tf_op jit(solution)/shard_map/ppermute | solution.py:534
  22.0 2.1 %collective-permute-start = (f32[96,768]{1,0:T(8,128)S(1)}, f32[96,768]{1,0:T(8,128)}, u32[]{:S(2)}, u32[]{:S(2)}) collective-permute-start(f32[96,768]{1,0:T(8,128)S(1)} %get-tuple-element.20), channel_id=1, source_target_pairs={{0,2},{2,0},{4,6},{6,4},{8,10},{10,8},{12,14},{14,12},{16,18},{18,... | collective-permute-start | bytes 884744 | tf_op jit(solution)/shard_map/cond/branch_1_fun/ppermute | solution.py:559
  22.0 2.3 %collective-permute-start.1 = (f32[96,768]{1,0:T(8,128)}, f32[96,768]{1,0:T(8,128)}, u32[]{:S(2)}, u32[]{:S(2)}) collective-permute-start(f32[96,768]{1,0:T(8,128)} %get-tuple-element.21), channel_id=1, source_target_pairs={{0,2},{2,0},{4,6},{6,4},{8,10},{10,8},{12,14},{14,12},{16,18},{18,... | collective-permute-start | bytes 884744 | tf_op jit(solution)/shard_map/cond/branch_1_fun/ppermute | solution.py:559
  24.4 1.9 %copy-start.3 = (bf16[768,1536]{1,0:T(8,128)(2,1)S(1)}, bf16[768,1536]{1,0:T(8,128)(2,1)}, u32[]{:S(2)}) copy-start(bf16[768,1536]{1,0:T(8,128)(2,1)} %refs_10_.3) | copy-start | bytes 7077892
  24.4 2.6 %copy-start.18 = (bf16[1536,768]{1,0:T(8,128)(2,1)S(1)}, bf16[1536,768]{1,0:T(8,128)(2,1)}, u32[]{:S(2)}) copy-start(bf16[1536,768]{1,0:T(8,128)(2,1)} %refs_11_.3) | copy-start | bytes 7077892
  32.6 22.1 %collective-permute-start.12 = (f32[258,768]{1,0:T(8,128)}, f32[258,768]{1,0:T(8,128)}, u32[]{:S(2)}, u32[]{:S(2)}) collective-permute-start(f32[258,768]{1,0:T(8,128)} %get-tuple-element.165.refs_0_), channel_id=1, source_target_pairs={{0,1},{1,0},{2,3},{3,2},{4,5},{5,4},{6,7},{7,6},{8,9},{9,8},{10,11... | collective-permute-start | bytes 2377736 | tf_op jit(solution)/shard_map/ppermute | solution.py:534
  39.8 5.6 %copy-start.19 = (bf16[258,1536]{1,0:T(8,128)(2,1)S(1)}, bf16[258,1536]{1,0:T(8,128)(2,1)}, u32[]{:S(2)}) copy-start(bf16[258,1536]{1,0:T(8,128)(2,1)} %get-tuple-element.153.refs_3_) | copy-start | bytes 2377732
  39.8 5.6 %copy-start.20 = (bf16[258,1536]{1,0:T(8,128)(2,1)S(1)}, bf16[258,1536]{1,0:T(8,128)(2,1)}, u32[]{:S(2)}) copy-start(bf16[258,1536]{1,0:T(8,128)(2,1)} %get-tuple-element.157.refs_4_) | copy-start | bytes 2377732
  45.4 35.3 %collective-permute-start.11 = (f32[258,768]{1,0:T(8,128)}, f32[258,768]{1,0:T(8,128)}, u32[]{:S(2)}, u32[]{:S(2)}) collective-permute-start(f32[258,768]{1,0:T(8,128)} %get-tuple-element.161.refs_0_), channel_id=1, source_target_pairs={{0,1},{1,0},{2,3},{3,2},{4,5},{5,4},{6,7},{7,6},{8,9},{9,8},{10,11... | collective-permute-start | bytes 2377736 | tf_op jit(solution)/shard_map/ppermute | solution.py:534
  46.0 4.9 %collective-permute-start.2 = (f32[384,1536]{1,0:T(8,128)}, f32[384,1536]{1,0:T(8,128)}, u32[]{:S(2)}, u32[]{:S(2)}) collective-permute-start(f32[384,1536]{1,0:T(8,128)} %get-tuple-element.22), channel_id=1, source_target_pairs={{0,2},{2,0},{4,6},{6,4},{8,10},{10,8},{12,14},{14,12},{16,18},{18,... | collective-permute-start | bytes 7077896 | tf_op jit(solution)/shard_map/cond/branch_1_fun/ppermute | solution.py:478
  50.8 3.9 %copy-start.1 = (bf16[2,258,768]{2,1,0:T(8,128)(2,1)S(1)}, bf16[2,258,768]{2,1,0:T(8,128)(2,1)}, u32[]{:S(2)}) copy-start(bf16[2,258,768]{2,1,0:T(8,128)(2,1)} %copy-done) | copy-start | bytes 2377732
  50.9 3.9 %copy-start.4 = (bf16[3,768,384]{2,1,0:T(8,128)(2,1)S(1)}, bf16[3,768,384]{2,1,0:T(8,128)(2,1)}, u32[]{:S(2)}) copy-start(bf16[3,768,384]{2,1,0:T(8,128)(2,1)} %refs_9_.3) | copy-start | bytes 5308420
  54.4 35.1 %collective-permute-start.14 = (f32[192,1536]{1,0:T(8,128)}, f32[192,1536]{1,0:T(8,128)}, u32[]{:S(2)}, u32[]{:S(2)}) collective-permute-start(f32[192,1536]{1,0:T(8,128)} %get-tuple-element.196), channel_id=1, source_target_pairs={{0,4},{2,6},{4,0},{6,2},{8,12},{10,14},{12,8},{14,10},{16,20},{18,... | collective-permute-start | bytes 3538952 | tf_op jit(solution)/shard_map/ppermute | solution.py:414
  63.8 25.6 %collective-permute-start.15 = (f32[258,768]{1,0:T(8,128)}, f32[258,768]{1,0:T(8,128)}, u32[]{:S(2)}, u32[]{:S(2)}) collective-permute-start(f32[258,768]{1,0:T(8,128)} %get-tuple-element.197.refs_2_), channel_id=1, source_target_pairs={{0,1},{1,0},{2,3},{3,2},{4,5},{5,4},{6,7},{7,6},{8,9},{9,8},{10,11... | collective-permute-start | bytes 2377736 | tf_op jit(solution)/shard_map/ppermute | solution.py:534
  71.0 4.9 %collective-permute-start.3 = (f32[384,1536]{1,0:T(8,128)}, f32[384,1536]{1,0:T(8,128)}, u32[]{:S(2)}, u32[]{:S(2)}) collective-permute-start(f32[384,1536]{1,0:T(8,128)} %param.5), channel_id=1, source_target_pairs={{0,2},{2,0},{4,6},{6,4},{8,10},{10,8},{12,14},{14,12},{16,18},{18,... | collective-permute-start | bytes 7077896 | tf_op jit(solution)/shard_map/cond/branch_1_fun/ppermute | solution.py:478
  79.2 30.0 %collective-permute-start.18 = (f32[192,1536]{1,0:T(8,128)}, f32[192,1536]{1,0:T(8,128)}, u32[]{:S(2)}, u32[]{:S(2)}) collective-permute-start(f32[192,1536]{1,0:T(8,128)} %get-tuple-element.211), channel_id=1, source_target_pairs={{0,4},{2,6},{4,0},{6,2},{8,12},{10,14},{12,8},{14,10},{16,20},{18,... | collective-permute-start | bytes 3538952 | tf_op jit(solution)/shard_map/ppermute | solution.py:414
  89.4 2.1 %copy-start.5 = (f32[258,768]{1,0:T(8,128)}, f32[258,768]{1,0:T(8,128)S(1)}, u32[]{:S(2)}) copy-start(f32[258,768]{1,0:T(8,128)S(1)} %get-tuple-element.183.refs_2_) | copy-start | bytes 2377732
  89.4 3.8 %copy-start.13 = (f32[8,768]{1,0:T(8,128)S(1)}, f32[8,768]{1,0:T(8,128)}, u32[]{:S(2)}) copy-start(f32[8,768]{1,0:T(8,128)} %get-tuple-element.191.refs_9_) | copy-start | bytes 73732
  89.4 3.8 %copy-start.14 = (f32[8,768]{1,0:T(8,128)S(1)}, f32[8,768]{1,0:T(8,128)}, u32[]{:S(2)}) copy-start(f32[8,768]{1,0:T(8,128)} %get-tuple-element.192.refs_10_) | copy-start | bytes 73732
  89.4 3.7 %copy-start.15 = (f32[8,768]{1,0:T(8,128)S(1)}, f32[8,768]{1,0:T(8,128)}, u32[]{:S(2)}) copy-start(f32[8,768]{1,0:T(8,128)} %get-tuple-element.193.refs_11_) | copy-start | bytes 73732
  89.4 3.7 %copy-start.16 = (f32[8,768]{1,0:T(8,128)S(1)}, f32[8,768]{1,0:T(8,128)}, u32[]{:S(2)}) copy-start(f32[8,768]{1,0:T(8,128)} %get-tuple-element.194.refs_12_) | copy-start | bytes 73732
  91.5 20.2 %collective-permute-start.17 = (f32[96,1536]{1,0:T(8,128)S(1)}, f32[96,1536]{1,0:T(8,128)S(1)}, u32[]{:S(2)}, u32[]{:S(2)}) collective-permute-start(f32[96,1536]{1,0:T(8,128)S(1)} %get-tuple-element.210), channel_id=1, source_target_pairs={{0,8},{2,10},{4,12},{6,14},{8,0},{10,2},{12,4},{14,6},{16,24},{18,... | collective-permute-start | bytes 1769480 | tf_op jit(solution)/shard_map/ppermute | solution.py:414
  100.7 5.0 %copy-start.6 = (f32[258,768]{1,0:T(8,128)S(1)}, f32[258,768]{1,0:T(8,128)}, u32[]{:S(2)}) copy-start(f32[258,768]{1,0:T(8,128)} %copy-done.5) | copy-start | bytes 2377732
  100.8 5.0 %collective-permute-start.4 = (f32[392,1536]{1,0:T(8,128)}, f32[392,1536]{1,0:T(8,128)}, u32[]{:S(2)}, u32[]{:S(2)}) collective-permute-start(f32[392,1536]{1,0:T(8,128)} %get-tuple-element.26), channel_id=1, source_target_pairs={{0,2},{2,0},{4,6},{6,4},{8,10},{10,8},{12,14},{14,12},{16,18},{18,... | collective-permute-start | bytes 7225352 | tf_op jit(solution)/shard_map/cond/branch_1_fun/ppermute | solution.py:478
  100.8 4.7 %collective-permute-start.5 = (f32[8,1536]{1,0:T(8,128)S(1)}, f32[8,1536]{1,0:T(8,128)}, u32[]{:S(2)}, u32[]{:S(2)}) collective-permute-start(f32[8,1536]{1,0:T(8,128)S(1)} %get-tuple-element.27), channel_id=1, source_target_pairs={{0,1},{1,0},{2,3},{3,2},{4,5},{5,4},{6,7},{7,6},{8,9},{9,8},{10,11... | collective-permute-start | bytes 147464 | tf_op jit(solution)/shard_map/cond/branch_1_fun/ppermute | solution.py:482
  101.4 4.3 %collective-permute-start.6 = (f32[8,1536]{1,0:T(8,128)S(1)}, f32[8,1536]{1,0:T(8,128)}, u32[]{:S(2)}, u32[]{:S(2)}) collective-permute-start(f32[8,1536]{1,0:T(8,128)S(1)} %get-tuple-element.27), channel_id=1, source_target_pairs={{0,3},{1,2},{2,1},{3,0},{4,7},{5,6},{6,5},{7,4},{8,11},{9,10},{10,... | collective-permute-start | bytes 147464 | tf_op jit(solution)/shard_map/cond/branch_1_fun/ppermute | solution.py:482
  105.8 21.3 %collective-permute-start.13 = (f32[258,768]{1,0:T(8,128)S(1)}, f32[258,768]{1,0:T(8,128)S(1)}, u32[]{:S(2)}, u32[]{:S(2)}) collective-permute-start(f32[258,768]{1,0:T(8,128)S(1)} %copy-done.6), channel_id=1, source_target_pairs={{0,1},{1,0},{2,3},{3,2},{4,5},{5,4},{6,7},{7,6},{8,9},{9,8},{10,11... | collective-permute-start | bytes 2377736 | tf_op jit(solution)/shard_map/ppermute | solution.py:534
  108.6 16.8 %collective-permute-start.16 = (f32[200,768]{1,0:T(8,128)S(1)}, f32[200,768]{1,0:T(8,128)S(1)}, u32[]{:S(2)}, u32[]{:S(2)}) collective-permute-start(f32[200,768]{1,0:T(8,128)S(1)} %get-tuple-element.207), channel_id=1, source_target_pairs={{0,4},{2,6},{4,0},{6,2},{8,12},{10,14},{12,8},{14,10},{16,20},{18,... | collective-permute-start | bytes 1843208 | tf_op jit(solution)/shard_map/ppermute | solution.py:414
  111.3 24.0 %collective-permute-start.22 = (f32[96,1536]{1,0:T(8,128)S(1)}, f32[96,1536]{1,0:T(8,128)S(1)}, u32[]{:S(2)}, u32[]{:S(2)}) collective-permute-start(f32[96,1536]{1,0:T(8,128)S(1)} %get-tuple-element.222), channel_id=1, source_target_pairs={{0,8},{2,10},{4,12},{6,14},{8,0},{10,2},{12,4},{14,6},{16,24},{18,... | collective-permute-start | bytes 1769480 | tf_op jit(solution)/shard_map/ppermute | solution.py:414
  113.5 19.2 %collective-permute-start.23 = (f32[48,1536]{1,0:T(8,128)S(1)}, f32[48,1536]{1,0:T(8,128)S(1)}, u32[]{:S(2)}, u32[]{:S(2)}) collective-permute-start(f32[48,1536]{1,0:T(8,128)S(1)} %get-tuple-element.223), channel_id=1, source_target_pairs={{0,16},{2,18},{4,20},{6,22},{8,24},{10,26},{12,28},{14,30},{16,0},... | collective-permute-start | bytes 884744 | tf_op jit(solution)/shard_map/ppermute | solution.py:414
  118.0 21.6 %collective-permute-start.21 = (f32[192,768]{1,0:T(8,128)S(1)}, f32[192,768]{1,0:T(8,128)S(1)}, u32[]{:S(2)}, u32[]{:S(2)}) collective-permute-start(f32[192,768]{1,0:T(8,128)S(1)} %get-tuple-element.221), channel_id=1, source_target_pairs={{0,4},{2,6},{4,0},{6,2},{8,12},{10,14},{12,8},{14,10},{16,20},{18,... | collective-permute-start | bytes 1769480 | tf_op jit(solution)/shard_map/ppermute | solution.py:414
  129.0 14.3 %collective-permute-start.20 = (f32[104,768]{1,0:T(8,128)S(1)}, f32[104,768]{1,0:T(8,128)S(1)}, u32[]{:S(2)}, u32[]{:S(2)}) collective-permute-start(f32[104,768]{1,0:T(8,128)S(1)} %get-tuple-element.220), channel_id=1, source_target_pairs={{0,8},{2,10},{4,12},{6,14},{8,0},{10,2},{12,4},{14,6},{16,24},{18,... | collective-permute-start | bytes 958472 | tf_op jit(solution)/shard_map/ppermute | solution.py:414
  129.5 36.2 %collective-permute-start.19 = (f32[528,768]{1,0:T(8,128)}, f32[528,768]{1,0:T(8,128)S(1)}, u32[]{:S(2)}, u32[]{:S(2)}) collective-permute-start(f32[528,768]{1,0:T(8,128)} %get-tuple-element.219.refs_0_), channel_id=1, source_target_pairs={{0,1},{1,0},{2,3},{3,2},{4,5},{5,4},{6,7},{7,6},{8,9},{9,8},{10,11... | collective-permute-start | bytes 4866056 | tf_op jit(solution)/shard_map/ppermute | solution.py:534
  130.7 2.0 %copy-start.10 = (f32[96,1536]{1,0:T(8,128)S(1)}, f32[96,1536]{1,0:T(8,128)}, u32[]{:S(2)}) copy-start(f32[96,1536]{1,0:T(8,128)} %copy-done.9) | copy-start | bytes 1769476
  137.0 18.4 %collective-permute-start.26 = (f32[48,1536]{1,0:T(8,128)S(1)}, f32[48,1536]{1,0:T(8,128)S(1)}, u32[]{:S(2)}, u32[]{:S(2)}) collective-permute-start(f32[48,1536]{1,0:T(8,128)S(1)} %get-tuple-element.230), channel_id=1, source_target_pairs={{0,16},{2,18},{4,20},{6,22},{8,24},{10,26},{12,28},{14,30},{16,0},... | collective-permute-start | bytes 884744 | tf_op jit(solution)/shard_map/ppermute | solution.py:414
  139.6 18.3 %copy-start.7 = (f32[192,768]{1,0:T(8,128)}, f32[192,768]{1,0:T(8,128)S(1)}, u32[]{:S(2)}) copy-start(f32[192,768]{1,0:T(8,128)S(1)} %collective-permute-done.21.refs_3_) | copy-start | bytes 1769476
  141.3 16.6 %collective-permute-start.25 = (f32[96,768]{1,0:T(8,128)S(1)}, f32[96,768]{1,0:T(8,128)S(1)}, u32[]{:S(2)}, u32[]{:S(2)}) collective-permute-start(f32[96,768]{1,0:T(8,128)S(1)} %get-tuple-element.229), channel_id=1, source_target_pairs={{0,8},{2,10},{4,12},{6,14},{8,0},{10,2},{12,4},{14,6},{16,24},{18,... | collective-permute-start | bytes 884744 | tf_op jit(solution)/shard_map/ppermute | solution.py:414
  144.9 15.5 %collective-permute-start.24 = (f32[56,768]{1,0:T(8,128)S(1)}, f32[56,768]{1,0:T(8,128)S(1)}, u32[]{:S(2)}, u32[]{:S(2)}) collective-permute-start(f32[56,768]{1,0:T(8,128)S(1)} %get-tuple-element.228), channel_id=1, source_target_pairs={{0,16},{2,18},{4,20},{6,22},{8,24},{10,26},{12,28},{14,30},{16,0},... | collective-permute-start | bytes 516104 | tf_op jit(solution)/shard_map/ppermute | solution.py:414
  159.5 8.5 %collective-permute-start.27 = (f32[48,768]{1,0:T(8,128)S(1)}, f32[48,768]{1,0:T(8,128)S(1)}, u32[]{:S(2)}, u32[]{:S(2)}) collective-permute-start(f32[48,768]{1,0:T(8,128)S(1)} %get-tuple-element.239), channel_id=1, source_target_pairs={{0,16},{2,18},{4,20},{6,22},{8,24},{10,26},{12,28},{14,30},{16,0},... | collective-permute-start | bytes 442376 | tf_op jit(solution)/shard_map/ppermute | solution.py:414
  165.7 2.3 %copy-start.8 = (f32[192,768]{1,0:T(8,128)S(1)}, f32[192,768]{1,0:T(8,128)}, u32[]{:S(2)}) copy-start(f32[192,768]{1,0:T(8,128)} %copy-done.7) | copy-start | bytes 1769476
  (1 other events, 1.7 us)

commit v6 on v5

--- a/solution.py
+++ b/solution.py
@@ -467,7 +467,7 @@
     keep, send = chain.call(
         partial(grads_body, layout, order, chunk, len(smalls)), [ids, *args, *smalls],
         [scalars(), *specs] + [whole(v) for v in smalls], [far(dims), far(dims)], 32,
-        f"{name}_grads", grid=begin, out_specs=[block, block],
+        f"{name}_grads", cost=32, grid=begin, out_specs=[block, block],
         scratch=[
             pltpu.VMEM((width, depth), BF16),
             pltpu.VMEM((depth, chunk), BF16),

time: 173 us -> 173 us (level)
  no operation moved by 1% of the time
where the time goes in v6:
time: 173 us; the launch traced here: 172 us
  Pallas kernels  104 us (60%)
  starting transfers between devices  30.9 us (18%)
  waiting for transfers between devices  27.6 us (16%)
  local copies, waits for them, and re-layouts  6.83 us (4%)
  other arithmetic  1.83 us (1%)
    pallas_call x30, Pallas kernels, kernel(): pl.pallas_call(body, out_shape=tuple(outs), grid_spec=pltpu.PrefetchScala...  104 us
    ppermute x12, starting transfers between devices, step(): lax.ppermute(send, 'dp', flips(self.dp, bit))  15.8 us
    ppermute x12, waiting for transfers between devices, step(): lax.ppermute(send, 'dp', flips(self.dp, bit))  12.9 us
    ppermute x8, starting transfers between devices, per_device(): across = lambda v: lax.ppermute(v, 'mp', SWAP)  10.9 us
    ppermute x3, waiting for transfers between devices, weight_sum(): swap = lambda v: lax.ppermute(v, 'dp', flips(dp, 0))  7.16 us
    unnamed x45, local copies, waits for them, and re-layouts  4.83 us
  transfers between devices with their start and end apart: 28, of which 13 were waited for; matrix products, arithmetic and copies ran while one was open for 2% of the time, Pallas kernels for 59%

profile of v6, /device:TPU:0, one launch (start us, length us, event | category | flops | bytes accessed | tf_op | source)
XLA Modules:
  0.0 171.9 jit_solution(12824647913585553966)
XLA Ops:
  1.6 3.0 %collective-permute-start.8 = (f32[96,768]{1,0:T(8,128)S(1)}, f32[96,768]{1,0:T(8,128)S(1)}, u32[]{:S(2)}, u32[]{:S(2)}) collective-permute-start(f32[96,768]{1,0:T(8,128)S(1)} %dynamic-slice_convert_fusion), channel_id=1, source_target_pairs={{0,1},{1,0},{2,3},{3,2},{4,5},{5,4},{6,7},{7,6},{8,9},{9,8},{10,11... | collective-permute-start | bytes 884744 | tf_op jit(solution)/shard_map/ppermute | solution.py:534
  4.6 6.1 %attend0.1 = (f32[258,768]{1,0:T(8,128)}, bf16[258,768]{1,0:T(8,128)(2,1)}, bf16[258,1152]{1,0:T(8,128)(2,1)}, f32[258,128]{1,0:T(8,128)}, f32[258,384]{1,0:T(8,128)S(1)}, /*index=5*/f32[8,128]{1,0:T(8,128)S(1)}) custom-call(s32[2,256]{1,0:T(2,128)} %refs_0_.5, bf16[2,1024,768]{2,1,0:T(8,128)(2,1)} %refs_1_.5, bf16[2,2,768]{2,1,0:T(2,128)(2,1)} %refs_2_.7, ...), custom_call_target="tpu_custom_call" | custom-call | flops 2147483648 | bytes 1 | tf_op jit(solution)/shard_map/attend0/pallas_call | solution.py:70
  11.6 1.7 collective-permute-start.9
  15.1 6.4 %attend1.1 = (f32[258,768]{1,0:T(8,128)}, bf16[258,768]{1,0:T(8,128)(2,1)}, bf16[258,1152]{1,0:T(8,128)(2,1)}, f32[258,128]{1,0:T(8,128)}, f32[258,384]{1,0:T(8,128)S(1)}, /*index=5*/f32[8,128]{1,0:T(8,128)S(1)}) custom-call(s32[2,256]{1,0:T(2,128)} %refs_0_.5, bf16[2,1024,768]{2,1,0:T(8,128)(2,1)} %refs_1_.5, bf16[2,2,768]{2,1,0:T(2,128)(2,1)} %refs_2_.7, ...), custom_call_target="tpu_custom_call" | custom-call | flops 2147483648 | bytes 1 | tf_op jit(solution)/shard_map/attend1/pallas_call | solution.py:70
  22.0 2.3 %conditional.4 = (f32[96,768]{1,0:T(8,128)}, f32[96,768]{1,0:T(8,128)}) conditional(s32[]{:T(128)} %bitcast.5, () %tuple.43, (f32[96,768]{1,0:T(8,128)S(1)}, f32[96,768]{1,0:T(8,128)}) %tuple.44), branch_computations={%region_0.1_spmd, %region_1.2_spmd} | conditional | bytes 2359392 | solution.py:110
  22.5 1.6 collective-permute-done
  27.0 5.6 %forward0.1 = (f32[258,768]{1,0:T(8,128)}, bf16[258,768]{1,0:T(8,128)(2,1)}, bf16[258,1536]{1,0:T(8,128)(2,1)}, bf16[258,1536]{1,0:T(8,128)(2,1)}, f32[258,768]{...) custom-call(s32[5]{0:T(128)S(1)} %stack.44.refs_0_, f32[258,768]{1,0:T(8,128)} %get-tuple-element.143.refs_1_.refs_5_, ...), custom_call_target="tpu_custom_call" | custom-call | flops 4294967296 | bytes 1 | tf_op jit(solution)/shard_map/forward0/pallas_call | solution.py:70
  34.1 5.6 %forward1.1 = (f32[258,768]{1,0:T(8,128)}, bf16[258,768]{1,0:T(8,128)(2,1)}, bf16[258,1536]{1,0:T(8,128)(2,1)}, bf16[258,1536]{1,0:T(8,128)(2,1)}, f32[258,768]{...) custom-call(s32[5]{0:T(128)S(1)} %stack.44.refs_0_, f32[258,768]{1,0:T(8,128)} %get-tuple-element.154.refs_1_.refs_5_, ...), custom_call_target="tpu_custom_call" | custom-call | flops 4294967296 | bytes 1 | tf_op jit(solution)/shard_map/forward1/pallas_call | solution.py:70
  39.8 5.6 %down_grads.1 = (f32[384,1536]{1,0:T(8,128)}, f32[384,1536]{1,0:T(8,128)}, f32[8,128]{1,0:T(8,128)S(1)}) custom-call(s32[5]{0:T(128)S(1)} %stack.44.refs_0_, bf16[2,258,768]{2,1,0:T(8,128)(2,1)} %copy-done, bf16[2,258,768]{2,1,0:T(8,128)(2,1)} %copy-done, bf16[258,1536]{1,0:T(8,128)(2,1)} %get-tuple-element.153.refs_3_, ...), custom_call_target="tpu_custom_call" | custom-call | flops 4294967296 | bytes 1 | tf_op jit(solution)/shard_map/down_grads/pallas_call | solution.py:70
  46.0 4.9 %conditional.5 = (f32[384,1536]{1,0:T(8,128)}, f32[528,768]{1,0:T(8,128)}) conditional(s32[]{:T(128)} %bitcast.5, () %tuple.41, (f32[384,1536]{1,0:T(8,128)}, bf16[258,1536]{1,0:T(8,128)(2,1)S(1)}, bf16[258,1536]{1,0:T(8,128)(2,1)S(1)}, bf16[1536,768]{1,0:T(8,128)(2,1)S(1)}) %tuple.70), branch_computations={%region_2.3_spmd, %region_3.4_spmd} | conditional | flops 2147483648 | bytes 9437241 | solution.py:110
  46.0 2.7 %branch.1 = f32[528,768]{1,0:T(8,128)} custom-call(bf16[258,1536]{1,0:T(8,128)(2,1)S(1)} %get-tuple-element.23.refs_0_, bf16[258,1536]{1,0:T(8,128)(2,1)S(1)} %get-tuple-element.24.refs_1_, bf16[1536,768]{1,0:T(8,128)(2,1)S(1)} %get-tuple-element.25.refs_2_), custom_call_target="tpu_custom_call" | custom-call | flops 2147483648 | bytes 1 | tf_op jit(solution)/shard_map/cond/branch_1_fun/branch/pallas_call | solution.py:70
  48.6 2.2 %collective-permute-done.2 = f32[384,1536]{1,0:T(8,128)} collective-permute-done((f32[384,1536]{1,0:T(8,128)}, f32[384,1536]{1,0:T(8,128)}, u32[]{:S(2)}, u32[]{:S(2)}) %collective-permute-start.2) | collective-permute-done | bytes 2359328 | tf_op jit(solution)/shard_map/cond/branch_1_fun/ppermute | solution.py:478
  50.9 3.5 %down0_step1.1 = (f32[192,1536]{1,0:T(8,128)}, f32[8,128]{1,0:T(8,128)S(1)}) custom-call(s32[5]{0:T(128)S(1)} %stack.44.refs_0_, f32[384,1536]{1,0:T(8,128)} %get-tuple-element.169.refs_1_, f32[384,1536]{1,0:T(8,128)} %get-tuple-element.170.refs_2_, f32[8,128]{1,0:T(8,128)S(1)} %get-tuple-element.171.refs_3_), custom_call_target="tpu_custom_call" | custom-call | flops 2147483648 | bytes 1 | tf_op jit(solution)/shard_map/down0_step1/pallas_call | solution.py:70
  54.7 9.1 %backward0.1 = (f32[258,768]{1,0:T(8,128)}, bf16[258,768]{1,0:T(8,128)(2,1)}, bf16[258,1152]{1,0:T(8,128)(2,1)}, f32[258,768]{1,0:T(8,128)}, f32[8,768]{1,0:T(8,...) custom-call(f32[258,768]{1,0:T(8,128)} %get-tuple-element.165.refs_0_, f32[258,768]{1,0:T(8,128)} %collective-permute-done.12.refs_1_, ...), custom_call_target="tpu_custom_call" | custom-call | flops 8589934592 | bytes 1 | tf_op jit(solution)/shard_map/backward0/pallas_call | solution.py:70
  63.8 1.7 %collective-permute-start.15 = (f32[258,768]{1,0:T(8,128)}, f32[258,768]{1,0:T(8,128)}, u32[]{:S(2)}, u32[]{:S(2)}) collective-permute-start(f32[258,768]{1,0:T(8,128)} %get-tuple-element.197.refs_2_), channel_id=1, source_target_pairs={{0,1},{1,0},{2,3},{3,2},{4,5},{5,4},{6,7},{7,6},{8,9},{9,8},{10,11... | collective-permute-start | bytes 2377736 | tf_op jit(solution)/shard_map/ppermute | solution.py:534
  65.5 5.5 %up_grads.1 = (f32[384,1536]{1,0:T(8,128)}, f32[384,1536]{1,0:T(8,128)}, f32[8,128]{1,0:T(8,128)S(1)}) custom-call(s32[5]{0:T(128)S(1)} %stack.44.refs_0_, bf16[258,768]{1,0:T(8,128)(2,1)} %get-tuple-element.174.refs_1_, bf16[258,768]{1,0:T(8,128)(2,1)} %get-tuple-element.175.refs_2_, bf16[258,1536]{1,0:T(8,128)(2,1)} %get-tuple-element.176.refs_3_, ...), custom_call_target="tpu_custom_call" | custom-call | flops 4294967296 | bytes 1 | tf_op jit(solution)/shard_map/up_grads/pallas_call | solution.py:70
  71.0 4.9 %conditional.6 = (f32[384,1536]{1,0:T(8,128)}) conditional(s32[]{:T(128)} %bitcast.5, () %tuple.46, f32[384,1536]{1,0:T(8,128)} %get-tuple-element.180), branch_computations={%region_4.5_spmd, %region_5.6_spmd} | conditional | bytes 9437232 | solution.py:110
  71.0 4.9 %collective-permute-done.3 = f32[384,1536]{1,0:T(8,128)} collective-permute-done((f32[384,1536]{1,0:T(8,128)}, f32[384,1536]{1,0:T(8,128)}, u32[]{:S(2)}, u32[]{:S(2)}) %collective-permute-start.3) | collective-permute-done | bytes 2359328 | tf_op jit(solution)/shard_map/cond/branch_1_fun/ppermute | solution.py:478
  75.9 3.3 %up0_step1.1 = (f32[192,1536]{1,0:T(8,128)}, f32[8,128]{1,0:T(8,128)S(1)}) custom-call(s32[5]{0:T(128)S(1)} %stack.44.refs_0_, f32[384,1536]{1,0:T(8,128)} %get-tuple-element.179.refs_1_, f32[384,1536]{1,0:T(8,128)} %get-tuple-element.282.refs_2_, f32[8,128]{1,0:T(8,128)S(1)} %get-tuple-element.181.refs_3_), custom_call_target="tpu_custom_call" | custom-call | flops 2147483648 | bytes 1 | tf_op jit(solution)/shard_map/up0_step1/pallas_call | solution.py:70
  80.7 8.7 %backward1.1 = (f32[258,768]{1,0:T(8,128)}, bf16[258,768]{1,0:T(8,128)(2,1)}, bf16[258,1152]{1,0:T(8,128)(2,1)}, f32[258,768]{1,0:T(8,128)S(1)}, f32[8,768]{1,0:...) custom-call(f32[258,768]{1,0:T(8,128)} %get-tuple-element.161.refs_0_, ...), custom_call_target="tpu_custom_call" | custom-call | flops 8589934592 | bytes 1 | tf_op jit(solution)/shard_map/backward1/pallas_call | solution.py:70
  89.5 2.1 %down0_step2.1 = (f32[96,1536]{1,0:T(8,128)S(1)}, f32[8,128]{1,0:T(8,128)S(1)}) custom-call(s32[5]{0:T(128)S(1)} %stack.44.refs_0_, f32[384,1536]{1,0:T(8,128)} %get-tuple-element.169.refs_1_, f32[384,1536]{1,0:T(8,128)} %get-tuple-element.170.refs_2_, f32[192,1536]{1,0:T(8,128)} %collective-permute-done.14.refs_3_, f32[8,128]{1,0:T(8,128)S(1)} %get-tuple-element.199.refs_4_), custom_call_target="tpu_custom_call" | custom-call | flops 2147483648 | bytes 1 | tf_op jit(solution)/shard_map/down0_step2/pallas_call | solution.py:70
  91.5 1.6 collective-permute-start.17
  93.2 7.6 %last_grads.1 = (f32[392,1536]{1,0:T(8,128)}, f32[392,1536]{1,0:T(8,128)}, f32[8,128]{1,0:T(8,128)S(1)}) custom-call(s32[5]{0:T(128)S(1)} %stack.44.refs_0_, bf16[258,768]{1,0:T(8,128)(2,1)} %get-tuple-element.185.refs_1_, bf16[258,768]{1,0:T(8,128)(2,1)} %get-tuple-element.186.refs_2_, f32[258,384]{1,0:T(8,128)} %copy-done.11, f32[258,384]{1,0:T(8,128)} %copy-done.12, ...), custom_call_target="tpu_custom_call" | custom-call | flops 4294967296 | bytes 1 | tf_op jit(solution)/shard_map/last_grads/pallas_call | solution.py:70
  100.7 5.0 %conditional.7 = (f32[392,1536]{1,0:T(8,128)}, f32[8,1536]{1,0:T(8,128)}, f32[8,1536]{1,0:T(8,128)}) conditional(s32[]{:T(128)} %bitcast.5, () %tuple.48, (f32[392,1536]{1,0:T(8,128)}, f32[8,1536]{1,0:T(8,128)S(1)}) %tuple.49), branch_computations={%region_6.7_spmd, %region_7.8_spmd} | conditional | bytes 10027152 | solution.py:110
  102.7 2.9 %collective-permute-done.5 = f32[8,1536]{1,0:T(8,128)} collective-permute-done((f32[8,1536]{1,0:T(8,128)S(1)}, f32[8,1536]{1,0:T(8,128)}, u32[]{:S(2)}, u32[]{:S(2)}) %collective-permute-start.5) | collective-permute-done | bytes 49184 | tf_op jit(solution)/shard_map/cond/branch_1_fun/ppermute | solution.py:482
  106.7 1.9 %last0_step1.1 = (f32[200,768]{1,0:T(8,128)S(1)}, f32[8,128]{1,0:T(8,128)S(1)}) custom-call(s32[5]{0:T(128)S(1)} %stack.44.refs_0_, f32[392,1536]{1,0:T(8,128)} %get-tuple-element.201.refs_1_.refs_3_.refs_4_.refs_5_.refs_6_, f32[392,1536]{1,0:T(8,128)} %get-tuple-element.203.refs_2_.refs_4_.refs_5_.refs_6_.refs_7_, ...), custom_call_target="tpu_custom_call" | custom-call | flops 2147483648 | bytes 1 | tf_op jit(solution)/shard_map/last0_step1/pallas_call | solution.py:70
  109.2 2.1 %up0_step2.1 = (f32[96,1536]{1,0:T(8,128)S(1)}, f32[8,128]{1,0:T(8,128)S(1)}) custom-call(s32[5]{0:T(128)S(1)} %stack.44.refs_0_, f32[384,1536]{1,0:T(8,128)} %get-tuple-element.179.refs_1_, f32[384,1536]{1,0:T(8,128)} %get-tuple-element.282.refs_2_, f32[192,1536]{1,0:T(8,128)} %collective-permute-done.18.refs_3_, f32[8,128]{1,0:T(8,128)S(1)} %get-tuple-element.212.refs_4_), custom_call_target="tpu_custom_call" | custom-call | flops 2147483648 | bytes 1 | tf_op jit(solution)/shard_map/up0_step2/pallas_call | solution.py:70
  111.8 1.7 %down0_step3.1 = (f32[48,1536]{1,0:T(8,128)S(1)}, f32[8,128]{1,0:T(8,128)S(1)}) custom-call(s32[5]{0:T(128)S(1)} %stack.44.refs_0_, f32[384,1536]{1,0:T(8,128)} %get-tuple-element.169.refs_1_, f32[384,1536]{1,0:T(8,128)} %get-tuple-element.170.refs_2_, f32[192,1536]{1,0:T(8,128)} %collective-permute-done.14.refs_3_, ...), custom_call_target="tpu_custom_call" | custom-call | flops 2147483648 | bytes 1 | tf_op jit(solution)/shard_map/down0_step3/pallas_call | solution.py:70
  113.5 2.7 %collective-permute-start.23 = (f32[48,1536]{1,0:T(8,128)S(1)}, f32[48,1536]{1,0:T(8,128)S(1)}, u32[]{:S(2)}, u32[]{:S(2)}) collective-permute-start(f32[48,1536]{1,0:T(8,128)S(1)} %get-tuple-element.223), channel_id=1, source_target_pairs={{0,16},{2,18},{4,20},{6,22},{8,24},{10,26},{12,28},{14,30},{16,0},... | collective-permute-start | bytes 884744 | tf_op jit(solution)/shard_map/ppermute | solution.py:414
  116.2 1.9 %last1_step1.1 = (f32[192,768]{1,0:T(8,128)S(1)}, f32[8,128]{1,0:T(8,128)S(1)}) custom-call(s32[5]{0:T(128)S(1)} %stack.44.refs_0_, f32[392,1536]{1,0:T(8,128)} %get-tuple-element.201.refs_1_.refs_3_.refs_4_.refs_5_.refs_6_, f32[392,1536]{1,0:T(8,128)} %get-tuple-element.203.refs_2_.refs_4_.refs_5_.refs_6_.refs_7_, f32[8,128]{1,0:T(8,128)S(1)} %get-tuple-element.214.refs_3_), custom_call_target="tpu_custom_call" | custom-call | flops 2147483648 | bytes 1 | tf_op jit(solution)/shard_map/last1_step1/pallas_call | solution.py:70
  119.6 2.4 %input0.1 = (f32[258,768]{1,0:T(8,128)S(1)}, f32[8,128]{1,0:T(8,128)S(1)}) custom-call(f32[768]{0:T(1024)} %refs_0_.7, f32[258,768]{1,0:T(8,128)} %get-tuple-element.143.refs_1_.refs_5_, f32[258,768]{1,0:T(8,128)} %get-tuple-element.197.refs_2_, f32[258,768]{1,0:T(8,128)} %collective-permute-done.15.refs_3_, f32[258,768]{1,0:T(8,128)} %get-tuple-element.209.refs_4_, ...), custom_call_target="tpu_custom_call" | custom-call | flops 2147483648 | bytes 1 | tf_op jit(solution)/shard_map/input0/pallas_call | solution.py:70
  122.0 3.4 %collective-permute-done.16.refs_3_.refs_8_.refs_9_.refs_10_ = f32[200,768]{1,0:T(8,128)S(1)} collective-permute-done((f32[200,768]{1,0:T(8,128)S(1)}, f32[200,768]{1,0:T(8,128)S(1)}, u32[]{:S(2)}, u32[]{:S(2)}) %collective-permute-start.16) | collective-permute-done | bytes 614432 | tf_op jit(solution)/shard_map/ppermute | solution.py:414
  125.4 1.7 last0_step2.1
  127.0 1.9 %input1.1 = (f32[258,768]{1,0:T(8,128)S(1)}, f32[8,128]{1,0:T(8,128)S(1)}) custom-call(f32[768]{0:T(1024)} %refs_0_.7, f32[258,768]{1,0:T(8,128)} %get-tuple-element.154.refs_1_.refs_5_, f32[258,768]{1,0:T(8,128)S(1)} %copy-done.6, f32[258,768]{1,0:T(8,128)S(1)} %collective-permute-done.13.refs_3_, f32[258,768]{1,0:T(8,128)} %get-tuple-element.184.refs_4_, ...), custom_call_target="tpu_custom_call" | custom-call | flops 2147483648 | bytes 1 | tf_op jit(solution)/shard_map/input1/pallas_call | solution.py:70
  130.7 2.0 %copy.35 = f32[2,258,768]{2,0,1:T(2,128)} copy(f32[2,258,768]{2,1,0:T(8,128)S(1)} %pad_maximum_fusion) | data formatting | bytes 3170304
  132.7 2.5 %down0_last.1 = (f32[48,1536]{1,0:T(8,128)}, f32[8,128]{1,0:T(8,128)S(1)}) custom-call(s32[5]{0:T(128)S(1)} %stack.44.refs_0_, f32[384,1536]{1,0:T(8,128)} %get-tuple-element.169.refs_1_, f32[384,1536]{1,0:T(8,128)} %get-tuple-element.170.refs_2_, f32[192,1536]{1,0:T(8,128)} %collective-permute-done.14.refs_3_, f32[96,1536]{1,0:T(8,128)S(1)} %copy-done.10, ...), custom_call_target="tpu_custom_call" | custom-call | flops 2147483648 | bytes 1 | tf_op jit(solution)/shard_map/down0_last/pallas_call | solution.py:70
  135.2 1.8 %up0_step3.1 = (f32[48,1536]{1,0:T(8,128)S(1)}, f32[8,128]{1,0:T(8,128)S(1)}) custom-call(s32[5]{0:T(128)S(1)} %stack.44.refs_0_, f32[384,1536]{1,0:T(8,128)} %get-tuple-element.179.refs_1_, f32[384,1536]{1,0:T(8,128)} %get-tuple-element.282.refs_2_, f32[192,1536]{1,0:T(8,128)} %collective-permute-done.18.refs_3_, ...), custom_call_target="tpu_custom_call" | custom-call | flops 2147483648 | bytes 1 | tf_op jit(solution)/shard_map/up0_step3/pallas_call | solution.py:70
  137.0 2.6 %collective-permute-start.26 = (f32[48,1536]{1,0:T(8,128)S(1)}, f32[48,1536]{1,0:T(8,128)S(1)}, u32[]{:S(2)}, u32[]{:S(2)}) collective-permute-start(f32[48,1536]{1,0:T(8,128)S(1)} %get-tuple-element.230), channel_id=1, source_target_pairs={{0,16},{2,18},{4,20},{6,22},{8,24},{10,26},{12,28},{14,30},{16,0},... | collective-permute-start | bytes 884744 | tf_op jit(solution)/shard_map/ppermute | solution.py:414
  139.6 1.7 last1_step2.1
  141.3 1.6 collective-permute-start.25
  143.3 1.6 last0_step3.1
  144.9 2.2 %collective-permute-start.24 = (f32[56,768]{1,0:T(8,128)S(1)}, f32[56,768]{1,0:T(8,128)S(1)}, u32[]{:S(2)}, u32[]{:S(2)}) collective-permute-start(f32[56,768]{1,0:T(8,128)S(1)} %get-tuple-element.228), channel_id=1, source_target_pairs={{0,16},{2,18},{4,20},{6,22},{8,24},{10,26},{12,28},{14,30},{16,0},... | collective-permute-start | bytes 516104 | tf_op jit(solution)/shard_map/ppermute | solution.py:414
  147.1 8.3 %collective-permute-done.26.refs_5_ = f32[48,1536]{1,0:T(8,128)S(1)} collective-permute-done((f32[48,1536]{1,0:T(8,128)S(1)}, f32[48,1536]{1,0:T(8,128)S(1)}, u32[]{:S(2)}, u32[]{:S(2)}) %collective-permute-start.26) | collective-permute-done | bytes 294944 | tf_op jit(solution)/shard_map/ppermute | solution.py:414
  155.4 2.5 %up0_last.1 = (f32[48,1536]{1,0:T(8,128)}, f32[8,128]{1,0:T(8,128)S(1)}) custom-call(s32[5]{0:T(128)S(1)} %stack.44.refs_0_, f32[384,1536]{1,0:T(8,128)} %get-tuple-element.179.refs_1_, f32[384,1536]{1,0:T(8,128)} %get-tuple-element.282.refs_2_, f32[192,1536]{1,0:T(8,128)} %collective-permute-done.18.refs_3_, ...), custom_call_target="tpu_custom_call" | custom-call | flops 2147483648 | bytes 1 | tf_op jit(solution)/shard_map/up0_last/pallas_call | solution.py:70
  160.4 1.6 last0_last.1
  163.9 1.8 %collective-permute-done.19.refs_1_ = f32[528,768]{1,0:T(8,128)S(1)} collective-permute-done((f32[528,768]{1,0:T(8,128)}, f32[528,768]{1,0:T(8,128)S(1)}, u32[]{:S(2)}, u32[]{:S(2)}) %collective-permute-start.19) | collective-permute-done | bytes 1622048 | tf_op jit(solution)/shard_map/ppermute | solution.py:534
  165.7 2.3 %output.1 = (bf16[2,258,768]{2,1,0:T(8,128)(2,1)S(1)}, f32[8,128]{1,0:T(8,128)S(1)}) custom-call(f32[528,768]{1,0:T(8,128)} %get-tuple-element.219.refs_0_, f32[528,768]{1,0:T(8,128)S(1)} %collective-permute-done.19.refs_1_, f32[768]{0:T(1024)} %refs_2_.8, f32[258,768]{1,0:T(8,128)} %get-tuple-element.166.refs_2_.refs_3_, ...), custom_call_target="tpu_custom_call" | custom-call | flops 2147483648 | bytes 1 | tf_op jit(solution)/shard_map/output/pallas_call | solution.py:70
  168.0 1.6 last1_last.1
  (98 shorter events, 25.9 us)
Async XLA Ops:
  1.6 10.0 %collective-permute-start.8 = (f32[96,768]{1,0:T(8,128)S(1)}, f32[96,768]{1,0:T(8,128)S(1)}, u32[]{:S(2)}, u32[]{:S(2)}) collective-permute-start(f32[96,768]{1,0:T(8,128)S(1)} %dynamic-slice_convert_fusion), channel_id=1, source_target_pairs={{0,1},{1,0},{2,3},{3,2},{4,5},{5,4},{6,7},{7,6},{8,9},{9,8},{10,11... | collective-permute-start | bytes 884744 | tf_op jit(solution)/shard_map/ppermute | solution.py:534
  4.6 10.4 %copy-start.17 = (bf16[2,258,768]{2,0,1:T(2,128)(2,1)S(1)}, bf16[2,258,768]{2,0,1:T(2,128)(2,1)}, u32[]{:S(2)}) copy-start(bf16[2,258,768]{2,0,1:T(2,128)(2,1)} %param.37) | copy-start | bytes 2377732
  10.8 15.0 %copy-start.11 = (f32[258,384]{1,0:T(8,128)}, f32[258,384]{1,0:T(8,128)S(1)}, u32[]{:S(2)}) copy-start(f32[258,384]{1,0:T(8,128)S(1)} %get-tuple-element.144.refs_7_.refs_3_) | copy-start | bytes 1188868
  11.6 10.4 %collective-permute-start.9 = (f32[96,768]{1,0:T(8,128)S(1)}, f32[96,768]{1,0:T(8,128)}, u32[]{:S(2)}, u32[]{:S(2)}) collective-permute-start(f32[96,768]{1,0:T(8,128)S(1)} %collective-permute-done.8.refs_2_), channel_id=1, source_target_pairs={{0,4},{2,6},{4,0},{6,2},{8,12},{10,14},{12,8},{14,10},{16,20},{18,... | collective-permute-start | bytes 884744 | tf_op jit(solution)/shard_map/ppermute | solution.py:558
  13.4 12.4 %collective-permute-start.7 = (f32[258,384]{1,0:T(8,128)S(1)}, f32[258,384]{1,0:T(8,128)S(1)}, u32[]{:S(2)}, u32[]{:S(2)}) collective-permute-start(f32[258,384]{1,0:T(8,128)S(1)} %get-tuple-element.144.refs_7_.refs_3_), channel_id=1, source_target_pairs={{0,1},{1,0},{2,3},{3,2},{4,5},{5,4},{6,7},{7,6},{8,9},{9,8},{10,11... | collective-permute-start | bytes 1188872 | tf_op jit(solution)/shard_map/ppermute | solution.py:534
  15.1 19.0 %copy-start = (bf16[2,258,768]{2,1,0:T(8,128)(2,1)}, bf16[2,258,768]{2,1,0:T(8,128)(2,1)S(1)}, u32[]{:S(2)}) copy-start(bf16[2,258,768]{2,1,0:T(8,128)(2,1)S(1)} %copy.30.refs_2_.refs_1_.refs_6_) | copy-start | bytes 2377732
  15.1 9.2 %copy-start.2 = (bf16[384,768]{1,0:T(8,128)(2,1)S(1)}, bf16[384,768]{1,0:T(8,128)(2,1)}, u32[]{:S(2)}) copy-start(bf16[384,768]{1,0:T(8,128)(2,1)} %refs_8_.3) | copy-start | bytes 1769476
  21.5 12.6 %copy-start.12 = (f32[258,384]{1,0:T(8,128)}, f32[258,384]{1,0:T(8,128)S(1)}, u32[]{:S(2)}) copy-start(f32[258,384]{1,0:T(8,128)S(1)} %get-tuple-element.155.refs_7_.refs_4_) | copy-start | bytes 1188868
  21.5 12.6 %collective-permute-start.10 = (f32[258,384]{1,0:T(8,128)S(1)}, f32[258,384]{1,0:T(8,128)S(1)}, u32[]{:S(2)}, u32[]{:S(2)}) collective-permute-start(f32[258,384]{1,0:T(8,128)S(1)} %get-tuple-element.155.refs_7_.refs_4_), channel_id=1, source_target_pairs={{0,1},{1,0},{2,3},{3,2},{4,5},{5,4},{6,7},{7,6},{8,9},{9,8},{10,11... | collective-permute-start | bytes 1188872 | tf_op jit(solution)/shard_map/ppermute | solution.py:534
  22.0 2.1 %collective-permute-start = (f32[96,768]{1,0:T(8,128)S(1)}, f32[96,768]{1,0:T(8,128)}, u32[]{:S(2)}, u32[]{:S(2)}) collective-permute-start(f32[96,768]{1,0:T(8,128)S(1)} %get-tuple-element.20), channel_id=1, source_target_pairs={{0,2},{2,0},{4,6},{6,4},{8,10},{10,8},{12,14},{14,12},{16,18},{18,... | collective-permute-start | bytes 884744 | tf_op jit(solution)/shard_map/cond/branch_1_fun/ppermute | solution.py:559
  22.0 2.3 %collective-permute-start.1 = (f32[96,768]{1,0:T(8,128)}, f32[96,768]{1,0:T(8,128)}, u32[]{:S(2)}, u32[]{:S(2)}) collective-permute-start(f32[96,768]{1,0:T(8,128)} %get-tuple-element.21), channel_id=1, source_target_pairs={{0,2},{2,0},{4,6},{6,4},{8,10},{10,8},{12,14},{14,12},{16,18},{18,... | collective-permute-start | bytes 884744 | tf_op jit(solution)/shard_map/cond/branch_1_fun/ppermute | solution.py:559
  24.4 1.9 %copy-start.3 = (bf16[768,1536]{1,0:T(8,128)(2,1)S(1)}, bf16[768,1536]{1,0:T(8,128)(2,1)}, u32[]{:S(2)}) copy-start(bf16[768,1536]{1,0:T(8,128)(2,1)} %refs_10_.3) | copy-start | bytes 7077892
  24.4 2.6 %copy-start.18 = (bf16[1536,768]{1,0:T(8,128)(2,1)S(1)}, bf16[1536,768]{1,0:T(8,128)(2,1)}, u32[]{:S(2)}) copy-start(bf16[1536,768]{1,0:T(8,128)(2,1)} %refs_11_.3) | copy-start | bytes 7077892
  32.6 22.1 %collective-permute-start.12 = (f32[258,768]{1,0:T(8,128)}, f32[258,768]{1,0:T(8,128)}, u32[]{:S(2)}, u32[]{:S(2)}) collective-permute-start(f32[258,768]{1,0:T(8,128)} %get-tuple-element.165.refs_0_), channel_id=1, source_target_pairs={{0,1},{1,0},{2,3},{3,2},{4,5},{5,4},{6,7},{7,6},{8,9},{9,8},{10,11... | collective-permute-start | bytes 2377736 | tf_op jit(solution)/shard_map/ppermute | solution.py:534
  39.8 5.6 %copy-start.19 = (bf16[258,1536]{1,0:T(8,128)(2,1)S(1)}, bf16[258,1536]{1,0:T(8,128)(2,1)}, u32[]{:S(2)}) copy-start(bf16[258,1536]{1,0:T(8,128)(2,1)} %get-tuple-element.153.refs_3_) | copy-start | bytes 2377732
  39.8 5.6 %copy-start.20 = (bf16[258,1536]{1,0:T(8,128)(2,1)S(1)}, bf16[258,1536]{1,0:T(8,128)(2,1)}, u32[]{:S(2)}) copy-start(bf16[258,1536]{1,0:T(8,128)(2,1)} %get-tuple-element.157.refs_4_) | copy-start | bytes 2377732
  45.4 35.3 %collective-permute-start.11 = (f32[258,768]{1,0:T(8,128)}, f32[258,768]{1,0:T(8,128)}, u32[]{:S(2)}, u32[]{:S(2)}) collective-permute-start(f32[258,768]{1,0:T(8,128)} %get-tuple-element.161.refs_0_), channel_id=1, source_target_pairs={{0,1},{1,0},{2,3},{3,2},{4,5},{5,4},{6,7},{7,6},{8,9},{9,8},{10,11... | collective-permute-start | bytes 2377736 | tf_op jit(solution)/shard_map/ppermute | solution.py:534
  46.0 4.9 %collective-permute-start.2 = (f32[384,1536]{1,0:T(8,128)}, f32[384,1536]{1,0:T(8,128)}, u32[]{:S(2)}, u32[]{:S(2)}) collective-permute-start(f32[384,1536]{1,0:T(8,128)} %get-tuple-element.22), channel_id=1, source_target_pairs={{0,2},{2,0},{4,6},{6,4},{8,10},{10,8},{12,14},{14,12},{16,18},{18,... | collective-permute-start | bytes 7077896 | tf_op jit(solution)/shard_map/cond/branch_1_fun/ppermute | solution.py:478
  50.8 3.9 %copy-start.1 = (bf16[2,258,768]{2,1,0:T(8,128)(2,1)S(1)}, bf16[2,258,768]{2,1,0:T(8,128)(2,1)}, u32[]{:S(2)}) copy-start(bf16[2,258,768]{2,1,0:T(8,128)(2,1)} %copy-done) | copy-start | bytes 2377732
  50.9 3.9 %copy-start.4 = (bf16[3,768,384]{2,1,0:T(8,128)(2,1)S(1)}, bf16[3,768,384]{2,1,0:T(8,128)(2,1)}, u32[]{:S(2)}) copy-start(bf16[3,768,384]{2,1,0:T(8,128)(2,1)} %refs_9_.3) | copy-start | bytes 5308420
  54.4 35.1 %collective-permute-start.14 = (f32[192,1536]{1,0:T(8,128)}, f32[192,1536]{1,0:T(8,128)}, u32[]{:S(2)}, u32[]{:S(2)}) collective-permute-start(f32[192,1536]{1,0:T(8,128)} %get-tuple-element.196), channel_id=1, source_target_pairs={{0,4},{2,6},{4,0},{6,2},{8,12},{10,14},{12,8},{14,10},{16,20},{18,... | collective-permute-start | bytes 3538952 | tf_op jit(solution)/shard_map/ppermute | solution.py:414
  63.8 25.6 %collective-permute-start.15 = (f32[258,768]{1,0:T(8,128)}, f32[258,768]{1,0:T(8,128)}, u32[]{:S(2)}, u32[]{:S(2)}) collective-permute-start(f32[258,768]{1,0:T(8,128)} %get-tuple-element.197.refs_2_), channel_id=1, source_target_pairs={{0,1},{1,0},{2,3},{3,2},{4,5},{5,4},{6,7},{7,6},{8,9},{9,8},{10,11... | collective-permute-start | bytes 2377736 | tf_op jit(solution)/shard_map/ppermute | solution.py:534
  71.0 4.9 %collective-permute-start.3 = (f32[384,1536]{1,0:T(8,128)}, f32[384,1536]{1,0:T(8,128)}, u32[]{:S(2)}, u32[]{:S(2)}) collective-permute-start(f32[384,1536]{1,0:T(8,128)} %param.5), channel_id=1, source_target_pairs={{0,2},{2,0},{4,6},{6,4},{8,10},{10,8},{12,14},{14,12},{16,18},{18,... | collective-permute-start | bytes 7077896 | tf_op jit(solution)/shard_map/cond/branch_1_fun/ppermute | solution.py:478
  79.2 30.0 %collective-permute-start.18 = (f32[192,1536]{1,0:T(8,128)}, f32[192,1536]{1,0:T(8,128)}, u32[]{:S(2)}, u32[]{:S(2)}) collective-permute-start(f32[192,1536]{1,0:T(8,128)} %get-tuple-element.211), channel_id=1, source_target_pairs={{0,4},{2,6},{4,0},{6,2},{8,12},{10,14},{12,8},{14,10},{16,20},{18,... | collective-permute-start | bytes 3538952 | tf_op jit(solution)/shard_map/ppermute | solution.py:414
  89.4 2.1 %copy-start.5 = (f32[258,768]{1,0:T(8,128)}, f32[258,768]{1,0:T(8,128)S(1)}, u32[]{:S(2)}) copy-start(f32[258,768]{1,0:T(8,128)S(1)} %get-tuple-element.183.refs_2_) | copy-start | bytes 2377732
  89.4 3.8 %copy-start.13 = (f32[8,768]{1,0:T(8,128)S(1)}, f32[8,768]{1,0:T(8,128)}, u32[]{:S(2)}) copy-start(f32[8,768]{1,0:T(8,128)} %get-tuple-element.191.refs_9_) | copy-start | bytes 73732
  89.4 3.8 %copy-start.14 = (f32[8,768]{1,0:T(8,128)S(1)}, f32[8,768]{1,0:T(8,128)}, u32[]{:S(2)}) copy-start(f32[8,768]{1,0:T(8,128)} %get-tuple-element.192.refs_10_) | copy-start | bytes 73732
  89.4 3.7 %copy-start.15 = (f32[8,768]{1,0:T(8,128)S(1)}, f32[8,768]{1,0:T(8,128)}, u32[]{:S(2)}) copy-start(f32[8,768]{1,0:T(8,128)} %get-tuple-element.193.refs_11_) | copy-start | bytes 73732
  89.4 3.7 %copy-start.16 = (f32[8,768]{1,0:T(8,128)S(1)}, f32[8,768]{1,0:T(8,128)}, u32[]{:S(2)}) copy-start(f32[8,768]{1,0:T(8,128)} %get-tuple-element.194.refs_12_) | copy-start | bytes 73732
  91.5 20.2 %collective-permute-start.17 = (f32[96,1536]{1,0:T(8,128)S(1)}, f32[96,1536]{1,0:T(8,128)S(1)}, u32[]{:S(2)}, u32[]{:S(2)}) collective-permute-start(f32[96,1536]{1,0:T(8,128)S(1)} %get-tuple-element.210), channel_id=1, source_target_pairs={{0,8},{2,10},{4,12},{6,14},{8,0},{10,2},{12,4},{14,6},{16,24},{18,... | collective-permute-start | bytes 1769480 | tf_op jit(solution)/shard_map/ppermute | solution.py:414
  100.7 5.0 %copy-start.6 = (f32[258,768]{1,0:T(8,128)S(1)}, f32[258,768]{1,0:T(8,128)}, u32[]{:S(2)}) copy-start(f32[258,768]{1,0:T(8,128)} %copy-done.5) | copy-start | bytes 2377732
  100.8 5.0 %collective-permute-start.4 = (f32[392,1536]{1,0:T(8,128)}, f32[392,1536]{1,0:T(8,128)}, u32[]{:S(2)}, u32[]{:S(2)}) collective-permute-start(f32[392,1536]{1,0:T(8,128)} %get-tuple-element.26), channel_id=1, source_target_pairs={{0,2},{2,0},{4,6},{6,4},{8,10},{10,8},{12,14},{14,12},{16,18},{18,... | collective-permute-start | bytes 7225352 | tf_op jit(solution)/shard_map/cond/branch_1_fun/ppermute | solution.py:478
  100.8 4.7 %collective-permute-start.5 = (f32[8,1536]{1,0:T(8,128)S(1)}, f32[8,1536]{1,0:T(8,128)}, u32[]{:S(2)}, u32[]{:S(2)}) collective-permute-start(f32[8,1536]{1,0:T(8,128)S(1)} %get-tuple-element.27), channel_id=1, source_target_pairs={{0,1},{1,0},{2,3},{3,2},{4,5},{5,4},{6,7},{7,6},{8,9},{9,8},{10,11... | collective-permute-start | bytes 147464 | tf_op jit(solution)/shard_map/cond/branch_1_fun/ppermute | solution.py:482
  101.4 4.3 %collective-permute-start.6 = (f32[8,1536]{1,0:T(8,128)S(1)}, f32[8,1536]{1,0:T(8,128)}, u32[]{:S(2)}, u32[]{:S(2)}) collective-permute-start(f32[8,1536]{1,0:T(8,128)S(1)} %get-tuple-element.27), channel_id=1, source_target_pairs={{0,3},{1,2},{2,1},{3,0},{4,7},{5,6},{6,5},{7,4},{8,11},{9,10},{10,... | collective-permute-start | bytes 147464 | tf_op jit(solution)/shard_map/cond/branch_1_fun/ppermute | solution.py:482
  105.8 21.3 %collective-permute-start.13 = (f32[258,768]{1,0:T(8,128)S(1)}, f32[258,768]{1,0:T(8,128)S(1)}, u32[]{:S(2)}, u32[]{:S(2)}) collective-permute-start(f32[258,768]{1,0:T(8,128)S(1)} %copy-done.6), channel_id=1, source_target_pairs={{0,1},{1,0},{2,3},{3,2},{4,5},{5,4},{6,7},{7,6},{8,9},{9,8},{10,11... | collective-permute-start | bytes 2377736 | tf_op jit(solution)/shard_map/ppermute | solution.py:534
  108.6 16.8 %collective-permute-start.16 = (f32[200,768]{1,0:T(8,128)S(1)}, f32[200,768]{1,0:T(8,128)S(1)}, u32[]{:S(2)}, u32[]{:S(2)}) collective-permute-start(f32[200,768]{1,0:T(8,128)S(1)} %get-tuple-element.207), channel_id=1, source_target_pairs={{0,4},{2,6},{4,0},{6,2},{8,12},{10,14},{12,8},{14,10},{16,20},{18,... | collective-permute-start | bytes 1843208 | tf_op jit(solution)/shard_map/ppermute | solution.py:414
  111.3 24.0 %collective-permute-start.22 = (f32[96,1536]{1,0:T(8,128)S(1)}, f32[96,1536]{1,0:T(8,128)S(1)}, u32[]{:S(2)}, u32[]{:S(2)}) collective-permute-start(f32[96,1536]{1,0:T(8,128)S(1)} %get-tuple-element.222), channel_id=1, source_target_pairs={{0,8},{2,10},{4,12},{6,14},{8,0},{10,2},{12,4},{14,6},{16,24},{18,... | collective-permute-start | bytes 1769480 | tf_op jit(solution)/shard_map/ppermute | solution.py:414
  113.5 19.2 %collective-permute-start.23 = (f32[48,1536]{1,0:T(8,128)S(1)}, f32[48,1536]{1,0:T(8,128)S(1)}, u32[]{:S(2)}, u32[]{:S(2)}) collective-permute-start(f32[48,1536]{1,0:T(8,128)S(1)} %get-tuple-element.223), channel_id=1, source_target_pairs={{0,16},{2,18},{4,20},{6,22},{8,24},{10,26},{12,28},{14,30},{16,0},... | collective-permute-start | bytes 884744 | tf_op jit(solution)/shard_map/ppermute | solution.py:414
  118.0 21.6 %collective-permute-start.21 = (f32[192,768]{1,0:T(8,128)S(1)}, f32[192,768]{1,0:T(8,128)S(1)}, u32[]{:S(2)}, u32[]{:S(2)}) collective-permute-start(f32[192,768]{1,0:T(8,128)S(1)} %get-tuple-element.221), channel_id=1, source_target_pairs={{0,4},{2,6},{4,0},{6,2},{8,12},{10,14},{12,8},{14,10},{16,20},{18,... | collective-permute-start | bytes 1769480 | tf_op jit(solution)/shard_map/ppermute | solution.py:414
  129.0 14.3 %collective-permute-start.20 = (f32[104,768]{1,0:T(8,128)S(1)}, f32[104,768]{1,0:T(8,128)S(1)}, u32[]{:S(2)}, u32[]{:S(2)}) collective-permute-start(f32[104,768]{1,0:T(8,128)S(1)} %get-tuple-element.220), channel_id=1, source_target_pairs={{0,8},{2,10},{4,12},{6,14},{8,0},{10,2},{12,4},{14,6},{16,24},{18,... | collective-permute-start | bytes 958472 | tf_op jit(solution)/shard_map/ppermute | solution.py:414
  129.5 36.2 %collective-permute-start.19 = (f32[528,768]{1,0:T(8,128)}, f32[528,768]{1,0:T(8,128)S(1)}, u32[]{:S(2)}, u32[]{:S(2)}) collective-permute-start(f32[528,768]{1,0:T(8,128)} %get-tuple-element.219.refs_0_), channel_id=1, source_target_pairs={{0,1},{1,0},{2,3},{3,2},{4,5},{5,4},{6,7},{7,6},{8,9},{9,8},{10,11... | collective-permute-start | bytes 4866056 | tf_op jit(solution)/shard_map/ppermute | solution.py:534
  130.7 2.0 %copy-start.10 = (f32[96,1536]{1,0:T(8,128)S(1)}, f32[96,1536]{1,0:T(8,128)}, u32[]{:S(2)}) copy-start(f32[96,1536]{1,0:T(8,128)} %copy-done.9) | copy-start | bytes 1769476
  137.0 18.4 %collective-permute-start.26 = (f32[48,1536]{1,0:T(8,128)S(1)}, f32[48,1536]{1,0:T(8,128)S(1)}, u32[]{:S(2)}, u32[]{:S(2)}) collective-permute-start(f32[48,1536]{1,0:T(8,128)S(1)} %get-tuple-element.230), channel_id=1, source_target_pairs={{0,16},{2,18},{4,20},{6,22},{8,24},{10,26},{12,28},{14,30},{16,0},... | collective-permute-start | bytes 884744 | tf_op jit(solution)/shard_map/ppermute | solution.py:414
  139.6 18.3 %copy-start.7 = (f32[192,768]{1,0:T(8,128)}, f32[192,768]{1,0:T(8,128)S(1)}, u32[]{:S(2)}) copy-start(f32[192,768]{1,0:T(8,128)S(1)} %collective-permute-done.21.refs_3_) | copy-start | bytes 1769476
  141.3 16.6 %collective-permute-start.25 = (f32[96,768]{1,0:T(8,128)S(1)}, f32[96,768]{1,0:T(8,128)S(1)}, u32[]{:S(2)}, u32[]{:S(2)}) collective-permute-start(f32[96,768]{1,0:T(8,128)S(1)} %get-tuple-element.229), channel_id=1, source_target_pairs={{0,8},{2,10},{4,12},{6,14},{8,0},{10,2},{12,4},{14,6},{16,24},{18,... | collective-permute-start | bytes 884744 | tf_op jit(solution)/shard_map/ppermute | solution.py:414
  144.9 15.5 %collective-permute-start.24 = (f32[56,768]{1,0:T(8,128)S(1)}, f32[56,768]{1,0:T(8,128)S(1)}, u32[]{:S(2)}, u32[]{:S(2)}) collective-permute-start(f32[56,768]{1,0:T(8,128)S(1)} %get-tuple-element.228), channel_id=1, source_target_pairs={{0,16},{2,18},{4,20},{6,22},{8,24},{10,26},{12,28},{14,30},{16,0},... | collective-permute-start | bytes 516104 | tf_op jit(solution)/shard_map/ppermute | solution.py:414
  159.5 8.5 %collective-permute-start.27 = (f32[48,768]{1,0:T(8,128)S(1)}, f32[48,768]{1,0:T(8,128)S(1)}, u32[]{:S(2)}, u32[]{:S(2)}) collective-permute-start(f32[48,768]{1,0:T(8,128)S(1)} %get-tuple-element.239), channel_id=1, source_target_pairs={{0,16},{2,18},{4,20},{6,22},{8,24},{10,26},{12,28},{14,30},{16,0},... | collective-permute-start | bytes 442376 | tf_op jit(solution)/shard_map/ppermute | solution.py:414
  165.7 2.3 %copy-start.8 = (f32[192,768]{1,0:T(8,128)S(1)}, f32[192,768]{1,0:T(8,128)}, u32[]{:S(2)}) copy-start(f32[192,768]{1,0:T(8,128)} %copy-done.7) | copy-start | bytes 1769476
  (1 other events, 1.7 us)
